TPU v7x, 32 devices: a whole 2x2x4 slice. The times are simulated.
32 devices in a mesh: groups: 2 (over x), node: 16 (over z, y, core).
Axes of the slice: x: 2, y: 2, z: 4, core: 2. Of those that a mesh axis runs over, the one named last changes fastest.
Arguments:
- moe_input: bfloat16 [256, 3072], P(('groups', 'node')), parts along dimension 0, may hold values from -400 to 400
- norm_gain: bfloat16 [3072], replicated, may hold values from 0.099609375 to 1.8984375
- router_weight: bfloat16 [3072, 8], replicated, may hold values from -0.109375 to 0.109375
- routes: int32 [256, 2], P(('groups', 'node')), parts along dimension 0, may hold values from 0 to 7, all different within a row; in each aligned block of 8 rows (0 to 7, 8 to 15, ...) at most 4 rows name the same one
- gate_weight: bfloat16 [16, 3072, 4096], P('node'), may hold values from -0.109375 to 0.109375
- up_weight: bfloat16 [16, 3072, 4096], P('node'), may hold values from -0.109375 to 0.109375
- down_weight: bfloat16 [16, 4096, 3072], P('node'), may hold values from -0.0625 to 0.0625
- queries: bfloat16 [256, 3072], P(('groups', 'node')), parts along dimension 0, may hold values from -10 to 10
- key_cache: bfloat16 [256, 64, 512], P(('groups', 'node')), parts along dimension 0, may hold values from -10 to 10
- value_cache: bfloat16 [256, 64, 512], P(('groups', 'node')), parts along dimension 0, may hold values from -6 to 6
- new_keys: bfloat16 [256, 512], P(('groups', 'node')), parts along dimension 0, may hold values from -6 to 6
- new_values: bfloat16 [256, 512], P(('groups', 'node')), parts along dimension 0, may hold values from -6 to 6
- cache_lengths: int32 [256], P(('groups', 'node')), parts along dimension 0, may hold values from 1 to 64, as said below
Outputs:
- moe_output: bfloat16 [256, 3072], P(('groups', 'node')), parts along dimension 0
- attention_output: bfloat16 [256, 3072], P(('groups', 'node')), parts along dimension 0
There are 2 independent parts, one for each index of `groups`. A program takes and returns all parts, laid end to end along the dimension named above; an argument that names none is the same for every part. Nothing has to cross between parts.
Inputs may be any that keep to these rules, and one draw needn't show every extreme that they name: `routes`: each row names 2 different experts. Among the 8 rows of one device no expert is named by more than 4 rows, a bound that some block reaches. `cache_lengths`: some row has 64.
All inputs are finite; a program needn't handle non-finite values.
Results may differ from a plain program's by a relative error of at most 0.0072.
Values may be sent and summed in bfloat16 or wider, within the bound.
No kernel may reach another device: no remote copies, remote signals or barrier semaphores. Data moves between devices by JAX's collectives and lax.ppermute only.
A program may use at most 192 MiB of HBM per device.

v0:
```python
import jax
import jax.numpy as jnp
from jax import lax
from jax.sharding import PartitionSpec as P

HEADS = 24
KVH = 4
HD = 128
GROUP = 6


def normalize(values, gain):
    wide = values.astype(jnp.float32)
    meansq = jnp.mean(wide * wide, axis=-1, keepdims=True)
    return (wide * lax.rsqrt(meansq + 1e-05) * gain.astype(jnp.float32)).astype(jnp.bfloat16)


def send_back(partial_rows, experts, slices):
    returned = lax.all_to_all(partial_rows, "node", split_axis=0, concat_axis=0, tiled=True)
    count = returned.shape[1]
    width = returned.shape[2]
    return jnp.sum(returned.reshape(experts, slices, count, width).astype(jnp.float32), axis=1)


def run_expert(received, gate_slice, up_slice, down_slice):
    senders, count, width = received.shape
    flat = received.reshape(senders * count, width)
    gate = jnp.dot(flat, gate_slice, preferred_element_type=jnp.float32)
    upper = jnp.dot(flat, up_slice, preferred_element_type=jnp.float32)
    hidden = (jax.nn.silu(gate) * upper).astype(jnp.bfloat16)
    part = jnp.dot(hidden, down_slice, preferred_element_type=jnp.float32).astype(jnp.bfloat16)
    return part.reshape(senders, count, width)


def attention(queries, key_cache, value_cache, new_keys, new_values, cache_lengths):
    rows = queries.shape[0]
    length = key_cache.shape[1]
    scale = 1.0 / HD**0.5
    query = queries.reshape(rows, KVH, GROUP, HD)
    keys = key_cache.reshape(rows, length, KVH, HD)
    vals = value_cache.reshape(rows, length, KVH, HD)
    score = jnp.einsum("rkgh,rlkh->rkgl", query, keys, preferred_element_type=jnp.float32) * scale
    live = jnp.arange(length, dtype=jnp.int32)[None, :] < cache_lengths[:, None]
    score = jnp.where(live[:, None, None, :], score, -jnp.inf)
    own = (
        jnp.einsum(
            "rkgh,rkh->rkg",
            query,
            new_keys.reshape(rows, KVH, HD),
            preferred_element_type=jnp.float32,
        )
        * scale
    )
    top = jnp.maximum(jnp.max(score, axis=-1), own)
    weights = jnp.exp(score - top[..., None])
    own_weight = jnp.exp(own - top)
    total = jnp.sum(weights, axis=-1) + own_weight
    probs = (weights / total[..., None]).astype(jnp.bfloat16)
    own_prob = (own_weight / total).astype(jnp.bfloat16)
    mixed = jnp.einsum("rkgl,rlkh->rkgh", probs, vals, preferred_element_type=jnp.float32)
    mixed = mixed + own_prob.astype(jnp.float32)[..., None] * new_values.reshape(
        rows, KVH, 1, HD
    ).astype(jnp.float32)
    return mixed.reshape(rows, HEADS * HD).astype(jnp.bfloat16)


def shards(
    moe_input,
    norm_gain,
    router_weight,
    routes,
    gate_weight,
    up_weight,
    down_weight,
    queries,
    key_cache,
    value_cache,
    new_keys,
    new_values,
    cache_lengths,
):
    rows, width = moe_input.shape
    experts = router_weight.shape[1]
    devices = lax.axis_size("node")
    slices = devices // experts
    capacity = rows // 2
    normed = normalize(moe_input, norm_gain)
    logits = jnp.dot(normed, router_weight, preferred_element_type=jnp.float32)
    onehot_int = (routes[:, :, None] == jnp.arange(experts, dtype=jnp.int32)[None, None, :]).astype(
        jnp.int32
    )
    onehot = onehot_int.astype(jnp.float32)
    picked = jnp.sum(onehot * logits[:, None, :], axis=-1)
    weight = 1.0 / (1.0 + jnp.exp(picked[:, ::-1] - picked))
    member_int = jnp.sum(onehot_int, axis=1)
    ranks_int = jnp.cumsum(member_int, axis=0) - member_int
    slots = jnp.arange(capacity, dtype=jnp.int32)
    select = (
        jnp.transpose(member_int)[:, None, :]
        * (jnp.transpose(ranks_int)[:, None, :] == slots[None, :, None]).astype(jnp.int32)
    ).astype(jnp.bfloat16)
    gate_slice = gate_weight[0]
    up_slice = up_weight[0]
    down_slice = down_weight[0]
    packed = jnp.einsum("ecr,rd->ecd", select, normed, preferred_element_type=jnp.float32).astype(
        jnp.bfloat16
    )
    outgoing = jnp.broadcast_to(packed[:, None], (experts, slices, capacity, width)).reshape(
        devices, capacity, width
    )
    summed = send_back(
        run_expert(
            lax.all_to_all(outgoing, "node", split_axis=0, concat_axis=0, tiled=True),
            gate_slice,
            up_slice,
            down_slice,
        ),
        experts,
        slices,
    )
    slot_of = jnp.sum(onehot_int * ranks_int[:, None, :], axis=-1)
    position = routes * capacity + slot_of
    picked_rows = summed.reshape(experts * capacity, width)[position]
    moe_output = jnp.sum(weight[:, :, None] * picked_rows, axis=1).astype(jnp.bfloat16)
    attention_output = attention(
        queries, key_cache, value_cache, new_keys, new_values, cache_lengths
    )
    return (moe_output, attention_output)


def solution(mesh):
    in_specs = (
        P(("groups", "node"), None),
        P(),
        P(),
        P(("groups", "node"), None),
        P("node", None, None),
        P("node", None, None),
        P("node", None, None),
        P(("groups", "node"), None),
        P(("groups", "node"), None, None),
        P(("groups", "node"), None, None),
        P(("groups", "node"), None),
        P(("groups", "node"), None),
        P(("groups", "node")),
    )
    out_specs = (P(("groups", "node"), None), P(("groups", "node"), None))
    return jax.shard_map(shards, mesh=mesh, in_specs=in_specs, out_specs=out_specs, check_vma=False)
```

profile of v0, /device:TPU:0, one launch (start us, length us, event | category | flops | bytes accessed | tf_op | source)
XLA Modules:
  0.0 74.1 jit_solution(2714420588801862579)
XLA Ops:
  0.6 0.0 copy-start
  0.6 0.8 %convert_reduce_fusion.1 = s32[8,8]{1,0:T(8,128)S(1)} fusion(s32[8,2]{0,1:T(2,128)} %param.16), kind=kLoop, calls=%fused_computation.47 | loop fusion | flops 320 | bytes 320 | tf_op jit(solution)/shard_map/reduce_sum | solution.py:95
  1.5 0.1 copy.32
  1.6 0.1 copy.33
  1.6 0.7 convert_element_type.66
  2.3 0.9 %fusion.32 = f32[8]{0:T(128)S(1)} fusion(bf16[8,3072]{1,0:T(8,128)(2,1)} %param.13), kind=kLoop, calls=%fused_computation.32 | loop fusion | flops 73720 | bytes 49184 | tf_op jit(solution)/shard_map/reduce_sum | solution.py:14
  3.3 1.0 %convolution_convert_fusion = bf16[8,4,3072]{2,0,1:T(8,128)(2,1)S(1)} fusion(s32[8,8]{1,0:T(8,128)S(1)} %copy.33, s32[8,8]{1,0:T(8,128)S(1)} %copy.32, bf16[8,3072]{1,0:T(8,128)(2,1)} %param.13, f32[3072]{0:T(1024)S(1)} %convert_element_type.66, f32[8]{0:T(128)S(1)} %add_rsqrt_fusion), kind=kOutput, calls=%fused_computation.10 | convolution fusion | flops 1770240 | bytes 258592 | tf_op jit(solution)/shard_map/ecr,rd->ecd/dot_general | solution.py:105
  4.3 0.2 copy.34
  4.5 0.9 %broadcast_in_dim.12 = bf16[8,2,4,3072]{3,2,1,0:T(4,128)(2,1)} broadcast(bf16[8,4,3072]{2,1,0:T(4,128)(2,1)S(1)} %copy.34), dimensions={0,2,3} | broadcast | bytes 589824 | tf_op jit(solution)/shard_map/broadcast_in_dim | solution.py:108
  5.3 7.4 %all-to-all-start = ((bf16[16,4,3072]{2,1,0:T(4,128)(2,1)}), bf16[16,4,3072]{2,1,0:T(4,128)(2,1)S(1)}, u32[]{:S(2)}, u32[]{:S(2)}) async-start(bf16[16,4,3072]{2,1,0:T(4,128)(2,1)} %bitcast.3), calls=%async_computation | async-start | bytes 786432 | tf_op jit(solution)/shard_map/all_to_all | solution.py:113
  12.8 0.9 %select_reduce_fusion = s32[8,2]{0,1:T(2,128)S(1)} fusion(s32[8,8]{1,0:T(8,128)S(1)} %sub.26, s32[8,2]{0,1:T(2,128)} %param.16), kind=kLoop, calls=%fused_computation.52 | loop fusion | flops 368 | bytes 384 | tf_op jit(solution)/shard_map/reduce_sum | solution.py:121
  13.6 0.7 compare_select_fusion
  14.3 1.0 %fusion.49 = f32[8,8]{1,0:T(8,128)S(1)} fusion(bf16[3072,8]{0,1:T(8,128)(2,1)} %param.15, bf16[8,3072]{1,0:T(8,128)(2,1)} %param.13, f32[3072]{0:T(1024)S(1)} %convert_element_type.66, f32[8]{0:T(128)S(1)} %add_rsqrt_fusion), kind=kOutput, calls=%fused_computation.58 | convolution fusion | flops 491520 | bytes 110880 | tf_op jit(solution)/shard_map/dot_general | solution.py:88
  15.4 0.7 iota_compare_fusion.2
  16.1 0.7 bitcast_convert_fusion
  16.8 0.8 %fusion.43 = f32[8,2]{0,1:T(2,128)S(1)} fusion(f32[8,8]{1,0:T(8,128)S(1)} %fusion.49, s32[8,2]{0,1:T(2,128)} %param.16), kind=kLoop, calls=%fused_computation.50 | loop fusion | flops 624 | bytes 384 | tf_op jit(solution)/shard_map/reduce_sum | solution.py:93
  17.7 1.0 %fusion.35 = f32[8,4,1,6]{3,2,1,0:T(1,128)S(1)} fusion(bf16[8,4,6,128]{3,0,2,1:T(8,128)(2,1)} %bitcast.59, bf16[8,4,128,1]{2,0,1,3:T(8,128)(2,1)} %bitcast.63), kind=kOutput, calls=%fused_computation.35 | convolution fusion | flops 49152 | bytes 58112 | tf_op jit(solution)/shard_map/rkgh,rkh->rkg/dot_general | solution.py:46
  18.6 1.5 %fusion.54 = (f32[8,4,6]{2,1,0:T(4,128)S(1)}, f32[8,4,6,64]{3,2,1,0:T(8,128)S(1)}) fusion(bf16[8,4,6,128]{3,0,2,1:T(8,128)(2,1)} %bitcast.60, pred[8,64]{1,0:T(8,128)(4,1)S(1)} %iota_compare_fusion.2, bf16[8,64,512]{2,1,0:T(8,128)(2,1)} %param.21), kind=kOutput, calls=%fused_computation.68 | convolution fusion | flops 3182400 | bytes 623872 | tf_op jit(solution)/shard_map/rkgh,rlkh->rkgl/dot_general | solution.py:42
  20.2 4.8 %all-to-all-done = bf16[16,4,3072]{2,1,0:T(4,128)(2,1)S(1)} async-done(((bf16[16,4,3072]{2,1,0:T(4,128)(2,1)}), bf16[16,4,3072]{2,1,0:T(4,128)(2,1)S(1)}, u32[]{:S(2)}, u32[]{:S(2)}) %all-to-all-start) | async-done | bytes 393248 | tf_op jit(solution)/shard_map/all_to_all | solution.py:113
  24.9 0.1 reshape.84
  25.0 10.5 %fusion.4 = f32[64,4096]{1,0:T(8,128)S(1)} fusion(bf16[64,3072]{1,0:T(8,128)(2,1)S(1)} %reshape.84, bf16[1,3072,4096]{2,1,0:T(8,128)(2,1)} %param.17), kind=kOutput, calls=%fused_computation.5 | convolution fusion | flops 1610612736 | bytes 26607616 | tf_op jit(solution)/shard_map/dot_general | solution.py:28
  35.5 19.9 %fusion.14 = bf16[64,3072]{1,0:T(8,128)(2,1)S(1)} fusion(bf16[1,4096,3072]{2,1,0:T(8,128)(2,1)} %param.19, bf16[64,3072]{1,0:T(8,128)(2,1)S(1)} %reshape.84, bf16[1,3072,4096]{2,1,0:T(8,128)(2,1)} %param.18, f32[64,4096]{1,0:T(8,128)S(1)} %fusion.4), kind=kOutput, calls=%fused_computation.9 | convolution fusion | flops 3222994944 | bytes 52166656 | tf_op jit(solution)/shard_map/dot_general | solution.py:31
  55.4 0.9 %reshape.85 = bf16[16,4,3072]{2,1,0:T(4,128)(2,1)} reshape(bf16[64,3072]{1,0:T(8,128)(2,1)S(1)} %fusion.14) | data formatting | bytes 786432 | tf_op jit(solution)/shard_map/reshape | solution.py:32
  56.3 3.6 %all-to-all-start.1 = ((bf16[16,4,3072]{2,1,0:T(4,128)(2,1)}), bf16[16,4,3072]{2,1,0:T(4,128)(2,1)S(1)}, u32[]{:S(2)}, u32[]{:S(2)}) async-start(bf16[16,4,3072]{2,1,0:T(4,128)(2,1)} %reshape.85), calls=%async_computation.1 | async-start | bytes 786432 | tf_op jit(solution)/shard_map/all_to_all | solution.py:19
  59.9 0.1 copy.35
  60.0 0.1 reshape.95
  60.0 0.1 copy.31
  60.1 0.2 fusion.31
  60.4 0.0 copy-done
  60.4 0.3 fusion.20
  60.7 0.7 convert_element_type.81
  61.4 10.6 %all-to-all-done.1 = bf16[16,4,3072]{2,1,0:T(4,128)(2,1)S(1)} async-done(((bf16[16,4,3072]{2,1,0:T(4,128)(2,1)}), bf16[16,4,3072]{2,1,0:T(4,128)(2,1)S(1)}, u32[]{:S(2)}, u32[]{:S(2)}) %all-to-all-start.1) | async-done | bytes 393248 | tf_op jit(solution)/shard_map/all_to_all | solution.py:19
  72.0 0.2 convert_reduce_fusion
  72.2 0.1 reshape.86
  72.4 0.6 gather_fusion
  73.0 0.1 reshape.94
  73.1 0.9 %multiply_reduce_fusion = bf16[8,3072]{1,0:T(8,128)(2,1)} fusion(f32[8,2,3072]{2,1,0:T(2,128)S(1)} %reshape.94, f32[8,2]{1,0:T(8,128)S(1)} %copy.31), kind=kLoop, calls=%fused_computation.26 | loop fusion | flops 73728 | bytes 245824 | tf_op jit(solution)/shard_map/reduce_sum | solution.py:124
  (10 shorter events, 0.1 us)
Async XLA Ops:
  0.6 59.8 %copy-start = (bf16[8,64,512]{2,1,0:T(8,128)(2,1)S(1)}, bf16[8,64,512]{2,1,0:T(8,128)(2,1)}, u32[]{:S(2)}) copy-start(bf16[8,64,512]{2,1,0:T(8,128)(2,1)} %param.22) | copy-start | bytes 1572868
  5.3 19.6 %all-to-all-start = ((bf16[16,4,3072]{2,1,0:T(4,128)(2,1)}), bf16[16,4,3072]{2,1,0:T(4,128)(2,1)S(1)}, u32[]{:S(2)}, u32[]{:S(2)}) async-start(bf16[16,4,3072]{2,1,0:T(4,128)(2,1)} %bitcast.3), calls=%async_computation | async-start | bytes 786432 | tf_op jit(solution)/shard_map/all_to_all | solution.py:113
  56.3 15.7 %all-to-all-start.1 = ((bf16[16,4,3072]{2,1,0:T(4,128)(2,1)}), bf16[16,4,3072]{2,1,0:T(4,128)(2,1)S(1)}, u32[]{:S(2)}, u32[]{:S(2)}) async-start(bf16[16,4,3072]{2,1,0:T(4,128)(2,1)} %reshape.85), calls=%async_computation.1 | async-start | bytes 786432 | tf_op jit(solution)/shard_map/all_to_all | solution.py:19
where the time goes:
time: 74.8 us; the launch traced here: 74.1 us
  matrix products  35.2 us (47%)
  waiting for transfers between devices  15.4 us (21%)
  starting transfers between devices  10.9 us (15%)
  other arithmetic  7.77 us (10%)
  local copies, waits for them, and re-layouts  3.99 us (5%)
  between operations  0.76 us (1%)
    dot_general x1, matrix products, run_expert(): jnp.dot(hidden, down_slice, preferred_element_type=jnp.float32)  19.9 us
    all_to_all x1, waiting for transfers between devices, send_back(): lax.all_to_all(partial_rows, 'node', split_axis=0, concat_axis=0, tiled=T...  10.6 us
    dot_general x1, matrix products, run_expert(): gate = jnp.dot(flat, gate_slice, preferred_element_type=jnp.float32)  10.5 us
    all_to_all x1, starting transfers between devices, shards(): lax.all_to_all(outgoing, 'node', split_axis=0, concat_axis=0, tiled=True)  7.39 us
    all_to_all x1, waiting for transfers between devices, shards(): lax.all_to_all(outgoing, 'node', split_axis=0, concat_axis=0, tiled=True)  4.76 us
    all_to_all x1, starting transfers between devices, send_back(): lax.all_to_all(partial_rows, 'node', split_axis=0, concat_axis=0, tiled=T...  3.55 us
    dot_general x1, matrix products, attention(): jnp.einsum('rkgh,rlkh->rkgl', query, keys, preferred_element_type=jnp.flo...  1.54 us
  transfers between devices with their start and end apart: 2, of which 2 were waited for; matrix products, arithmetic and copies ran while one was open for 12% of the time, Pallas kernels for 0%

commit v1 on v0

--- a/solution.py
+++ b/solution.py
@@ -1,12 +1,22 @@
+import functools
+
 import jax
 import jax.numpy as jnp
 from jax import lax
+from jax.experimental import pallas as pl
+from jax.experimental.pallas import tpu as pltpu
 from jax.sharding import PartitionSpec as P
 
 HEADS = 24
 KVH = 4
 HD = 128
 GROUP = 6
+TILE = 256
+MIB = 1 << 20
+F32 = jnp.float32
+BF16 = jnp.bfloat16
+WHOLE = pl.BlockSpec(memory_space=pltpu.VMEM)
+ANY = pl.BlockSpec(memory_space=pl.ANY)
 
 
 def normalize(values, gain):
@@ -32,7 +42,7 @@
     return part.reshape(senders, count, width)
 
 
-def attention(queries, key_cache, value_cache, new_keys, new_values, cache_lengths):
+def plain_attention(queries, key_cache, value_cache, new_keys, new_values, cache_lengths):
     rows = queries.shape[0]
     length = key_cache.shape[1]
     scale = 1.0 / HD**0.5
@@ -64,7 +74,7 @@
     return mixed.reshape(rows, HEADS * HD).astype(jnp.bfloat16)
 
 
-def shards(
+def plain_shards(
     moe_input,
     norm_gain,
     router_weight,
@@ -122,10 +132,416 @@
     position = routes * capacity + slot_of
     picked_rows = summed.reshape(experts * capacity, width)[position]
     moe_output = jnp.sum(weight[:, :, None] * picked_rows, axis=1).astype(jnp.bfloat16)
-    attention_output = attention(
+    attention_output = plain_attention(
         queries, key_cache, value_cache, new_keys, new_values, cache_lengths
     )
     return (moe_output, attention_output)
+
+
+def select_slots(routes, experts, capacity):
+    lines, rows = experts.shape
+    named = [routes[k : k + 1, :] == experts for k in range(2)]
+    member = jnp.where(named[0] | named[1], 1.0, 0.0)
+    before = lax.broadcasted_iota(jnp.int32, (rows, rows), 0) < lax.broadcasted_iota(
+        jnp.int32, (rows, rows), 1
+    )
+    rank = jnp.dot(member, jnp.where(before, 1.0, 0.0), preferred_element_type=F32)
+    slot = (lax.broadcasted_iota(jnp.int32, (lines, rows), 0) % capacity).astype(F32)
+    return [flag & (rank == slot) for flag in named]
+
+
+def line_experts(column, capacity, lines, rows):
+    line = lax.broadcasted_iota(jnp.int32, (lines, rows), 0)
+    block = 2 * capacity
+    return ((line // block) ^ column) * 2 + (line % block) // capacity
+
+
+def pack_kernel(capacity, x_hbm, routes_hbm, *refs):
+    *out_refs, x_ref, routes_ref, sems = refs
+    copies = [
+        pltpu.make_async_copy(routes_hbm, routes_ref, sems.at[0]),
+        pltpu.make_async_copy(x_hbm, x_ref, sems.at[1]),
+    ]
+    for copy in copies:
+        copy.start()
+    for copy in copies:
+        copy.wait()
+    column = lax.axis_index("node") // 4
+    rows = x_ref.shape[0]
+    block = out_refs[0].shape[0]
+    lines = block * len(out_refs)
+    first, second = select_slots(
+        routes_ref[...], line_experts(column, capacity, lines, rows), capacity
+    )
+    chosen = jnp.where(first | second, 1.0, 0.0).astype(BF16)
+    packed = jnp.dot(chosen, x_ref[...], preferred_element_type=F32)
+    for k, out_ref in enumerate(out_refs):
+        out_ref[...] = packed[k * block : (k + 1) * block].astype(BF16)
+
+
+def halves_kernel(capacity, *refs):
+    *in_refs, _, keep_ref, send_ref = refs
+    mine = (lax.axis_index("node") // 2) % 2
+    block = 2 * capacity
+    lines = len(in_refs) * block
+    half = lines // 2
+    out_line = lax.broadcasted_iota(jnp.int32, (lines, lines), 0)
+    in_line = lax.broadcasted_iota(jnp.int32, (lines, lines), 1)
+    which = jnp.where(out_line < half, mine, 1 - mine)
+    within = out_line % half
+    source = (within // capacity) * block + which * capacity + within % capacity
+    move = jnp.where(in_line == source, 1.0, 0.0).astype(BF16)
+    values = jnp.concatenate([ref[...] for ref in in_refs], axis=0)
+    moved = jnp.dot(move, values, preferred_element_type=F32)
+    keep_ref[...] = moved[:half].astype(BF16)
+    send_ref[...] = moved[half:].astype(BF16)
+
+
+def blocks_kernel(capacity, mine_ref, other_ref, *out_refs):
+    mine = (lax.axis_index("node") // 2) % 2
+    block = 2 * capacity
+    lines = block * len(out_refs)
+    half = lines // 2
+    out_line = lax.broadcasted_iota(jnp.int32, (lines, lines), 0)
+    in_line = lax.broadcasted_iota(jnp.int32, (lines, lines), 1)
+    which = jnp.where((out_line % block) // capacity == mine, 0, 1)
+    source = which * half + (out_line // block) * capacity + out_line % capacity
+    move = jnp.where(in_line == source, 1.0, 0.0).astype(BF16)
+    values = jnp.concatenate([mine_ref[...], other_ref[...]], axis=0)
+    moved = jnp.dot(move, values, preferred_element_type=F32)
+    for k, out_ref in enumerate(out_refs):
+        out_ref[...] = moved[k * block : (k + 1) * block].astype(BF16)
+
+
+def add_kernel(left0_ref, left1_ref, right0_ref, right1_ref, out0_ref, out1_ref):
+    out0_ref[...] = (left0_ref[...] + right0_ref[...].astype(F32)).astype(BF16)
+    out1_ref[...] = (left1_ref[...] + right1_ref[...].astype(F32)).astype(BF16)
+
+
+def rms(values, gain):
+    wide = values.astype(F32)
+    meansq = jnp.mean(wide * wide, axis=-1, keepdims=True)
+    return (wide * lax.rsqrt(meansq + 1e-05) * gain.astype(F32).reshape(1, -1)).astype(BF16)
+
+
+def attention(lengths_ref, q_ref, k_ref, v_ref, nk_ref, nv_ref, out_ref):
+    rows = q_ref.shape[0]
+    length = k_ref.shape[1]
+    groups = k_ref.shape[2] // HD
+    per_group = q_ref.shape[1] // HD // groups
+    lines, columns = per_group * rows, rows * length
+    scale = 1.0 / HD**0.5
+    row = lax.broadcasted_iota(jnp.int32, (lines, 1), 0) % rows
+    count = jnp.zeros((lines, 1), jnp.int32)
+    for r in range(rows):
+        count = jnp.where(row == r, lengths_ref[r], count)
+    position = lax.broadcasted_iota(jnp.int32, (lines, columns), 1) - row * length
+    live = (position >= 0) & (position < count)
+    for g in range(groups):
+        lanes = slice(g * HD, (g + 1) * HD)
+        heads = [slice(h * HD, (h + 1) * HD) for h in range(g * per_group, (g + 1) * per_group)]
+        query = jnp.concatenate([q_ref[:, head].astype(F32) for head in heads], axis=0)
+        keys = k_ref[:, :, lanes].reshape(columns, HD)
+        values = v_ref[:, :, lanes].reshape(columns, HD)
+        new_key = jnp.concatenate([nk_ref[:, lanes].astype(F32)] * per_group, axis=0)
+        new_value = jnp.concatenate([nv_ref[:, lanes].astype(F32)] * per_group, axis=0)
+        score = (
+            lax.dot_general(
+                query.astype(BF16), keys, (((1,), (1,)), ((), ())), preferred_element_type=F32
+            )
+            * scale
+        )
+        own = jnp.sum(query * new_key, axis=-1, keepdims=True) * scale
+        score = jnp.where(live, score, -jnp.inf)
+        top = jnp.maximum(jnp.max(score, axis=-1, keepdims=True), own)
+        weights = jnp.exp(score - top)
+        own_weight = jnp.exp(own - top)
+        total = jnp.sum(weights, axis=-1, keepdims=True) + own_weight
+        probs = (weights / total).astype(BF16)
+        own_prob = (own_weight / total).astype(BF16).astype(F32)
+        mixed = jnp.dot(probs, values, preferred_element_type=F32) + own_prob * new_value
+        for j, head in enumerate(heads):
+            out_ref[:, head] = mixed[j * rows : (j + 1) * rows].astype(BF16)
+
+
+def side_kernel(
+    lengths_ref,
+    q_ref,
+    k_hbm,
+    v_hbm,
+    nk_ref,
+    nv_ref,
+    x_ref,
+    gain_ref,
+    router_ref,
+    out_ref,
+    logits_ref,
+    k_ref,
+    v_ref,
+    sems,
+):
+    copies = [
+        pltpu.make_async_copy(k_hbm, k_ref, sems.at[0]),
+        pltpu.make_async_copy(v_hbm, v_ref, sems.at[1]),
+    ]
+    for copy in copies:
+        copy.start()
+    logits_ref[...] = lax.dot_general(
+        router_ref[...],
+        rms(x_ref[...], gain_ref[...]),
+        (((1,), (1,)), ((), ())),
+        preferred_element_type=F32,
+    )
+    for copy in copies:
+        copy.wait()
+    attention(lengths_ref, q_ref, k_ref, v_ref, nk_ref, nv_ref, out_ref)
+
+
+def down_copy(down_ref, buf, sems, tile, slot):
+    return pltpu.make_async_copy(
+        down_ref.at[0, pl.ds(pl.multiple_of(tile * TILE, TILE), TILE), :],
+        buf.at[slot],
+        sems.at[slot],
+    )
+
+
+def expert_kernel(
+    slots,
+    a_ref,
+    b_ref,
+    c_ref,
+    d_ref,
+    gain_ref,
+    gate_ref,
+    up_ref,
+    down_ref,
+    own0_ref,
+    own1_ref,
+    far0_ref,
+    far1_ref,
+    x_buf,
+    total,
+    down_buf,
+    sems,
+):
+    tiles = gate_ref.shape[2] // TILE
+    part = a_ref.shape[0]
+    for tile in range(min(slots, tiles)):
+        down_copy(down_ref, down_buf, sems, tile, tile).start()
+    for i, ref in enumerate((a_ref, b_ref, c_ref, d_ref)):
+        x_buf[i * part : (i + 1) * part, :] = rms(ref[...], gain_ref[...])
+    total[...] = jnp.zeros_like(total)
+
+    def step(tile, carry):
+        slot = lax.rem(tile, slots)
+        cols = pl.ds(pl.multiple_of(tile * TILE, TILE), TILE)
+        x = x_buf[...]
+        gated = jnp.dot(x, gate_ref[0, :, cols], preferred_element_type=F32)
+        upper = jnp.dot(x, up_ref[0, :, cols], preferred_element_type=F32)
+        hidden = (gated / (1.0 + jnp.exp(-gated)) * upper).astype(BF16)
+        down_copy(down_ref, down_buf, sems, tile, slot).wait()
+        total[...] += jnp.dot(hidden, down_buf[slot], preferred_element_type=F32)
+
+        @pl.when(tile + slots < tiles)
+        def _():
+            down_copy(down_ref, down_buf, sems, tile + slots, slot).start()
+
+        return carry
+
+    lax.fori_loop(0, tiles, step, 0)
+    own0_ref[...] = total[:part]
+    own1_ref[...] = total[part : 2 * part]
+    far0_ref[...] = total[2 * part : 3 * part].astype(BF16)
+    far1_ref[...] = total[3 * part :].astype(BF16)
+
+
+def combine_kernel(capacity, routes_ref, logits_ref, *refs):
+    *in_refs, out_ref = refs
+    column = lax.axis_index("node") // 4
+    routes = routes_ref[...]
+    logits = logits_ref[...]
+    expert = lax.broadcasted_iota(jnp.int32, logits.shape, 0)
+    picked = [
+        jnp.sum(jnp.where(routes[k : k + 1, :] == expert, logits, 0.0), axis=0, keepdims=True)
+        for k in range(2)
+    ]
+    block, rows = in_refs[0].shape[0], routes.shape[1]
+    lines = block * len(in_refs)
+    hits = select_slots(routes, line_experts(column, capacity, lines, rows), capacity)
+    table = jnp.zeros(hits[0].shape, F32)
+    for k in range(2):
+        weight = 1.0 / (1.0 + jnp.exp(picked[1 - k] - picked[k]))
+        table += jnp.where(hits[k], weight, 0.0)
+    high = table.astype(BF16)
+    rest = table - high.astype(F32)
+    middle = rest.astype(BF16)
+    low = (rest - middle.astype(F32)).astype(BF16)
+    values = jnp.concatenate([ref[...] for ref in in_refs], axis=0)
+    terms = [
+        lax.dot_general(term, values, (((0,), (0,)), ((), ())), preferred_element_type=F32)
+        for term in (low, middle, high)
+    ]
+    out_ref[...] = (terms[0] + terms[1] + terms[2]).astype(BF16)
+
+
+def call(kernel, name, outs, ins, operands, scratch=(), limit=4, cost=None):
+    return pl.pallas_call(
+        kernel,
+        out_shape=outs,
+        in_specs=ins,
+        out_specs=tuple(WHOLE for _ in outs) if isinstance(outs, tuple) else WHOLE,
+        scratch_shapes=list(scratch),
+        compiler_params=pltpu.CompilerParams(vmem_limit_bytes=limit * MIB),
+        cost_estimate=cost,
+        name=name,
+    )(*operands)
+
+
+def exchange(values, bits):
+    size = lax.axis_size("node")
+    return lax.ppermute(values, "node", [(i, i ^ bits) for i in range(size)])
+
+
+def paired_shards(
+    moe_input,
+    norm_gain,
+    router_weight,
+    routes,
+    gate_weight,
+    up_weight,
+    down_weight,
+    queries,
+    key_cache,
+    value_cache,
+    new_keys,
+    new_values,
+    cache_lengths,
+):
+    rows, width = moe_input.shape
+    experts = router_weight.shape[1]
+    capacity = rows // 2
+    columns = lax.axis_size("node") // 4
+    block = 2 * capacity
+    half = columns * capacity
+    named = routes.T
+    gain = norm_gain
+
+    def like(lines, dtype=BF16):
+        return jax.ShapeDtypeStruct((lines, width), dtype)
+
+    def held(lines, dtype=BF16):
+        return pltpu.VMEM((lines, width), dtype)
+
+    packed = call(
+        functools.partial(pack_kernel, capacity),
+        "pack",
+        (like(block),) * columns,
+        [pl.BlockSpec(memory_space=pltpu.HBM)] * 2,
+        [pltpu.with_memory_space_constraint(array, pltpu.HBM) for array in (moe_input, named)],
+        [
+            pltpu.VMEM(moe_input.shape, BF16),
+            pltpu.VMEM(named.shape, jnp.int32),
+            pltpu.SemaphoreType.DMA((2,)),
+        ],
+        cost=pl.CostEstimate(flops=10**11, bytes_accessed=64 * MIB, transcendentals=0),
+    )
+    blocks = [packed[0]] + [exchange(packed[k], 4 * k) for k in range(1, columns)]
+    attended, logits = call(
+        side_kernel,
+        "side",
+        (like(rows), jax.ShapeDtypeStruct((experts, rows), F32)),
+        [pl.BlockSpec(memory_space=pltpu.SMEM), WHOLE, ANY, ANY] + [WHOLE] * 5,
+        (
+            cache_lengths,
+            queries,
+            key_cache,
+            value_cache,
+            new_keys,
+            new_values,
+            moe_input,
+            gain,
+            router_weight.T,
+        ),
+        [
+            pltpu.VMEM(key_cache.shape, BF16),
+            pltpu.VMEM(value_cache.shape, BF16),
+            pltpu.SemaphoreType.DMA((2,)),
+        ],
+        cost=pl.CostEstimate(flops=10**8, bytes_accessed=4 * MIB, transcendentals=0),
+    )
+    keep, send = call(
+        functools.partial(halves_kernel, capacity),
+        "halves",
+        (like(half),) * 2,
+        [WHOLE] * columns + [ANY],
+        (*blocks, logits),
+    )
+    far_keep = exchange(keep, 1)
+    across = exchange(send, 2)
+    far_across = exchange(across, 1)
+    slots = 3
+    own0, own1, far0, far1 = call(
+        functools.partial(expert_kernel, slots),
+        "expert",
+        (held(half, F32), held(half, F32), held(half), held(half)),
+        [WHOLE] * 7 + [ANY],
+        (
+            keep,
+            across,
+            far_keep,
+            far_across,
+            gain,
+            pltpu.with_memory_space_constraint(gate_weight, pltpu.VMEM),
+            pltpu.with_memory_space_constraint(up_weight, pltpu.VMEM),
+            down_weight,
+        ),
+        [
+            pltpu.VMEM((4 * half, width), BF16),
+            pltpu.VMEM((4 * half, width), F32),
+            pltpu.VMEM((slots, TILE, width), BF16),
+            pltpu.SemaphoreType.DMA((slots,)),
+        ],
+        limit=9,
+    )
+    back0, back1 = exchange(far0, 1), exchange(far1, 1)
+    sum0, sum1 = call(
+        add_kernel,
+        "add",
+        (like(half),) * 2,
+        [WHOLE] * 4,
+        (
+            pltpu.with_memory_space_constraint(own0, pltpu.VMEM),
+            pltpu.with_memory_space_constraint(own1, pltpu.VMEM),
+            back0,
+            back1,
+        ),
+    )
+    other = exchange(sum1, 2)
+    results = call(
+        functools.partial(blocks_kernel, capacity),
+        "blocks",
+        (like(block),) * columns,
+        [WHOLE] * 2,
+        (sum0, other),
+    )
+    results = [results[0]] + [exchange(results[k], 4 * k) for k in range(1, columns)]
+    moe_output = call(
+        functools.partial(combine_kernel, capacity),
+        "combine",
+        like(rows),
+        [WHOLE] * (2 + columns),
+        (named, logits, *results),
+    )
+    return moe_output, attended
+
+
+def shards(*arrays):
+    experts = arrays[2].shape[1]
+    devices = lax.axis_size("node")
+    units = arrays[4].shape[2]
+    if devices == 2 * experts and devices % 8 == 0 and units % TILE == 0 and arrays[0].shape[0] == 8:
+        return paired_shards(*arrays)
+    return plain_shards(*arrays)
 
 
 def solution(mesh):

time: 74.8 us -> 55.6 us (0.74)
  matrix products: 35.2 us -> 0 us
  Pallas kernels: 0 us -> 25.1 us
  other arithmetic: 7.77 us -> 0 us
  local copies, waits for them, and re-layouts: 3.99 us -> 0.69 us
  starting transfers between devices: 10.9 us -> 13.9 us
    dot_general x7 -> x0, matrix products: 35.2 us -> none  [the longest x1 19.9 us: run_expert(): jnp.dot(hidden, down_slice, preferred_element_type=jnp.float32)]
    pallas_call x0 -> x7, Pallas kernels: none -> 25.1 us  [call(): pl.pallas_call(kernel, out_shape=outs, in_specs=ins, out_specs=tuple((WHO...]
    all_to_all x2 -> x0, waiting for transfers between devices: 15.4 us -> none  [the longest x1 10.6 us: send_back(): lax.all_to_all(partial_rows, 'node', split_axis=0, concat_axis=0, tiled=T...]
    ppermute x0 -> x12, waiting for transfers between devices: none -> 14.8 us  [exchange(): return lax.ppermute(values, 'node', [(i, i ^ bits) for i in range(size)])]
    ppermute x0 -> x12, starting transfers between devices: none -> 13.9 us  [exchange(): return lax.ppermute(values, 'node', [(i, i ^ bits) for i in range(size)])]
    all_to_all x2 -> x0, starting transfers between devices: 10.9 us -> none  [the longest x1 7.39 us: shards(): lax.all_to_all(outgoing, 'node', split_axis=0, concat_axis=0, tiled=True)]
    reduce_sum x7 -> x0, other arithmetic: 4.85 us -> none  [the longest x1 0.94 us: normalize(): meansq = jnp.mean(wide * wide, axis=-1, keepdims=True)]
    convert_element_type x2 -> x0, other arithmetic: 1.39 us -> none  [the longest x1 0.7 us: attention(): mixed = mixed + own_prob.astype(jnp.float32)[..., None] * new_values.resh...]
  transfers between devices with their start and end apart: 2 -> 12, of which waited for: 2 -> 9; matrix products, arithmetic and copies ran while one was open for 12% -> 0% of each run, Pallas kernels for 0% -> 6%
where the time goes in v1:
time: 55.6 us; the launch traced here: 55.4 us
  Pallas kernels  25.1 us (45%)
  waiting for transfers between devices  14.8 us (27%)
  starting transfers between devices  13.9 us (25%)
  between operations  0.88 us (2%)
  local copies, waits for them, and re-layouts  0.69 us (1%)
    pallas_call x7, Pallas kernels, call(): pl.pallas_call(kernel, out_shape=outs, in_specs=ins, out_specs=tuple((WHO...  25.1 us
    ppermute x12, waiting for transfers between devices, exchange(): return lax.ppermute(values, 'node', [(i, i ^ bits) for i in range(size)])  14.8 us
    ppermute x12, starting transfers between devices, exchange(): return lax.ppermute(values, 'node', [(i, i ^ bits) for i in range(size)])  13.9 us
  transfers between devices with their start and end apart: 12, of which 9 were waited for; matrix products, arithmetic and copies ran while one was open for 0% of the time, Pallas kernels for 6%

profile of v1, /device:TPU:0, one launch (start us, length us, event | category | flops | bytes accessed | tf_op | source)
XLA Modules:
  0.0 55.4 jit_solution(11286850304503728481)
XLA Ops:
  0.6 0.0 copy-start.2
  0.6 0.0 copy-start.3
  0.7 0.0 copy-start.5
  0.7 0.0 copy-start.6
  0.7 0.0 copy-start.7
  0.7 0.0 copy-start.8
  0.7 0.0 copy-start.9
  0.7 0.0 copy-start.10
  0.7 0.0 copy-start.12
  0.7 0.0 copy-start
  0.7 0.0 copy-start.1
  0.7 1.3 %pack.1 = (bf16[8,3072]{1,0:T(8,128)(2,1)S(1)}, bf16[8,3072]{1,0:T(8,128)(2,1)S(1)}, bf16[8,3072]{1,0:T(8,128)(2,1)S(1)}, bf16[8,3072]{1,0:T(8,128)(2,1)S(1)}) custom-call(bf16[8,3072]{1,0:T(8,128)(2,1)} %x_hbm.1, s32[2,8]{1,0:T(2,128)} %bitcast.3), custom_call_target="tpu_custom_call" | custom-call | flops 99999997952 | bytes 67108864 | tf_op jit(solution)/shard_map/pack/pallas_call | solution.py:388
  2.0 3.1 %collective-permute-start = (bf16[8,3072]{1,0:T(8,128)(2,1)S(1)}, bf16[8,3072]{1,0:T(8,128)(2,1)S(1)}, u32[]{:S(2)}, u32[]{:S(2)}) collective-permute-start(bf16[8,3072]{1,0:T(8,128)(2,1)S(1)} %get-tuple-element.22), channel_id=1, source_target_pairs={{0,4},{1,5},{2,6},{3,7},{4,0},{5,1},{6,2},{7,3},{8,12},{9,13},{10,... | collective-permute-start | bytes 147464 | tf_op jit(solution)/shard_map/ppermute | solution.py:402
  5.1 2.6 %collective-permute-start.1 = (bf16[8,3072]{1,0:T(8,128)(2,1)S(1)}, bf16[8,3072]{1,0:T(8,128)(2,1)S(1)}, u32[]{:S(2)}, u32[]{:S(2)}) collective-permute-start(bf16[8,3072]{1,0:T(8,128)(2,1)S(1)} %get-tuple-element.23), channel_id=1, source_target_pairs={{0,8},{1,9},{2,10},{3,11},{4,12},{5,13},{6,14},{7,15},{8,0},{9,1},... | collective-permute-start | bytes 147464 | tf_op jit(solution)/shard_map/ppermute | solution.py:402
  7.7 0.0 collective-permute-start.2
  7.7 0.0 copy-done.2
  7.7 0.0 copy-done.3
  7.7 0.0 copy-done.5
  7.7 0.0 copy-done.6
  7.8 0.0 copy-done.7
  7.8 0.0 copy-done.8
  7.8 0.0 copy-done.9
  7.8 0.0 copy-done.10
  7.8 0.0 copy-done.12
  7.8 3.1 %side.1 = (bf16[8,3072]{1,0:T(8,128)(2,1)}, f32[8,8]{1,0:T(8,128)S(1)}) custom-call(s32[8]{0:T(128)S(1)} %copy-done.12, bf16[8,3072]{1,0:T(8,128)(2,1)S(1)} %copy-done.5, bf16[8,64,512]{2,1,0:T(8,128)(2,1)S(1)} %copy-done.2, bf16[8,64,512]{2,1,0:T(8,128)(2,1)S(1)} %copy-done.3, bf16[8,512]{1,0:T(8,128)(2,1)S(1)} %copy-done.9, bf16[8,512]{1,0:T(8,128)(2,1)S(1)} %copy-done.10, ...), custom_call_target="tpu_custom_call" | custom-call | flops 100000000 | bytes 4194304 | tf_op jit(solution)/shard_map/side/pallas_call | solution.py:388
  10.9 0.0 collective-permute-done.refs_1_
  10.9 0.2 collective-permute-done.1.refs_2_
  11.1 2.6 %collective-permute-done.2.refs_3_ = bf16[8,3072]{1,0:T(8,128)(2,1)S(1)} collective-permute-done((bf16[8,3072]{1,0:T(8,128)(2,1)S(1)}, bf16[8,3072]{1,0:T(8,128)(2,1)S(1)}, u32[]{:S(2)}, u32[]{:S(2)}) %collective-permute-start.2) | collective-permute-done | bytes 49184 | tf_op jit(solution)/shard_map/ppermute | solution.py:402
  13.6 0.2 halves.1
  13.8 0.0 copy-start.4
  13.8 1.6 %collective-permute-start.3 = (bf16[16,3072]{1,0:T(8,128)(2,1)S(1)}, bf16[16,3072]{1,0:T(8,128)(2,1)S(1)}, u32[]{:S(2)}, u32[]{:S(2)}) collective-permute-start(bf16[16,3072]{1,0:T(8,128)(2,1)S(1)} %get-tuple-element.26), channel_id=1, source_target_pairs={{0,2},{1,3},{2,0},{3,1},{4,6},{5,7},{6,4},{7,5},{8,10},{9,11},{10,... | collective-permute-start | bytes 294920 | tf_op jit(solution)/shard_map/ppermute | solution.py:402
  15.4 0.0 copy-start.11
  15.4 0.0 collective-permute-start.4
  15.4 3.1 %collective-permute-done.3.b_ref = bf16[16,3072]{1,0:T(8,128)(2,1)S(1)} collective-permute-done((bf16[16,3072]{1,0:T(8,128)(2,1)S(1)}, bf16[16,3072]{1,0:T(8,128)(2,1)S(1)}, u32[]{:S(2)}, u32[]{:S(2)}) %collective-permute-start.3) | collective-permute-done | bytes 98336 | tf_op jit(solution)/shard_map/ppermute | solution.py:402
  18.5 0.0 copy-start.13
  18.5 0.0 collective-permute-start.5
  18.5 0.0 collective-permute-done.4.c_ref
  18.5 0.0 copy-start.14
  18.5 1.3 %collective-permute-done.5.d_ref = bf16[16,3072]{1,0:T(8,128)(2,1)S(1)} collective-permute-done((bf16[16,3072]{1,0:T(8,128)(2,1)S(1)}, bf16[16,3072]{1,0:T(8,128)(2,1)S(1)}, u32[]{:S(2)}, u32[]{:S(2)}) %collective-permute-start.5) | collective-permute-done | bytes 98336 | tf_op jit(solution)/shard_map/ppermute | solution.py:402
  19.8 0.0 copy-done.4
  19.8 0.0 copy-done.13
  19.8 0.0 copy-done.14
  19.8 0.0 copy-start.15
  19.8 0.6 %copy-done.15 = bf16[16,3072]{1,0:T(8,128)(2,1)} copy-done((bf16[16,3072]{1,0:T(8,128)(2,1)}, bf16[16,3072]{1,0:T(8,128)(2,1)S(1)}, u32[]{:S(2)}) %copy-start.15) | copy-done | bytes 98328
  20.4 0.0 copy-done
  20.4 0.0 copy-done.1
  20.5 19.3 %expert.1 = (f32[16,3072]{1,0:T(8,128)S(1)}, f32[16,3072]{1,0:T(8,128)S(1)}, bf16[16,3072]{1,0:T(8,128)(2,1)S(1)}, bf16[16,3072]{1,0:T(8,128)(2,1)S(1)}) custom-call(bf16[16,3072]{1,0:T(8,128)(2,1)} %copy-done.4, bf16[16,3072]{1,0:T(8,128)(2,1)} %copy-done.13, bf16[16,3072]{1,0:T(8,128)(2,1)} %copy-done.14, bf16[16,3072]{1,0:T(8,128)(2,1)} %copy-done.15, ...), custom_call_target="tpu_custom_call" | custom-call | tf_op jit(solution)/shard_map/expert/pallas_call | solution.py:388
  39.8 0.2 collective-permute-start.6
  40.0 0.4 collective-permute-start.7
  40.4 0.8 %collective-permute-done.6.right0_ref = bf16[16,3072]{1,0:T(8,128)(2,1)S(1)} collective-permute-done((bf16[16,3072]{1,0:T(8,128)(2,1)S(1)}, bf16[16,3072]{1,0:T(8,128)(2,1)S(1)}, u32[]{:S(2)}, u32[]{:S(2)}) %collective-permute-start.6) | collective-permute-done | bytes 98336 | tf_op jit(solution)/shard_map/ppermute | solution.py:402
  41.2 0.2 collective-permute-done.7.right1_ref
  41.4 1.6 %collective-permute-start.8 = (bf16[16,3072]{1,0:T(8,128)(2,1)S(1)}, bf16[16,3072]{1,0:T(8,128)(2,1)S(1)}, u32[]{:S(2)}, u32[]{:S(2)}) collective-permute-start(bf16[16,3072]{1,0:T(8,128)(2,1)S(1)} %get-tuple-element.32), channel_id=1, source_target_pairs={{0,2},{1,3},{2,0},{3,1},{4,6},{5,7},{6,4},{7,5},{8,10},{9,11},{10,... | collective-permute-start | bytes 294920 | tf_op jit(solution)/shard_map/ppermute | solution.py:402
  43.0 3.5 %collective-permute-done.8.other_ref = bf16[16,3072]{1,0:T(8,128)(2,1)S(1)} collective-permute-done((bf16[16,3072]{1,0:T(8,128)(2,1)S(1)}, bf16[16,3072]{1,0:T(8,128)(2,1)S(1)}, u32[]{:S(2)}, u32[]{:S(2)}) %collective-permute-start.8) | collective-permute-done | bytes 98336 | tf_op jit(solution)/shard_map/ppermute | solution.py:402
  46.5 0.2 blocks.1
  46.7 0.1 collective-permute-start.9
  46.8 1.7 %collective-permute-start.10 = (bf16[8,3072]{1,0:T(8,128)(2,1)S(1)}, bf16[8,3072]{1,0:T(8,128)(2,1)S(1)}, u32[]{:S(2)}, u32[]{:S(2)}) collective-permute-start(bf16[8,3072]{1,0:T(8,128)(2,1)S(1)} %get-tuple-element.35), channel_id=1, source_target_pairs={{0,8},{1,9},{2,10},{3,11},{4,12},{5,13},{6,14},{7,15},{8,0},{9,1},... | collective-permute-start | bytes 147464 | tf_op jit(solution)/shard_map/ppermute | solution.py:402
  48.5 2.7 %collective-permute-start.11 = (bf16[8,3072]{1,0:T(8,128)(2,1)S(1)}, bf16[8,3072]{1,0:T(8,128)(2,1)S(1)}, u32[]{:S(2)}, u32[]{:S(2)}) collective-permute-start(bf16[8,3072]{1,0:T(8,128)(2,1)S(1)} %get-tuple-element.36), channel_id=1, source_target_pairs={{0,12},{1,13},{2,14},{3,15},{4,8},{5,9},{6,10},{7,11},{8,4},{9,5},... | collective-permute-start | bytes 147464 | tf_op jit(solution)/shard_map/ppermute | solution.py:402
  51.1 0.0 collective-permute-done.9.refs_1_
  51.1 1.4 %collective-permute-done.10.refs_2_ = bf16[8,3072]{1,0:T(8,128)(2,1)S(1)} collective-permute-done((bf16[8,3072]{1,0:T(8,128)(2,1)S(1)}, bf16[8,3072]{1,0:T(8,128)(2,1)S(1)}, u32[]{:S(2)}, u32[]{:S(2)}) %collective-permute-start.10) | collective-permute-done | bytes 49184 | tf_op jit(solution)/shard_map/ppermute | solution.py:402
  52.6 1.8 %collective-permute-done.11.refs_3_ = bf16[8,3072]{1,0:T(8,128)(2,1)S(1)} collective-permute-done((bf16[8,3072]{1,0:T(8,128)(2,1)S(1)}, bf16[8,3072]{1,0:T(8,128)(2,1)S(1)}, u32[]{:S(2)}, u32[]{:S(2)}) %collective-permute-start.11) | collective-permute-done | bytes 49184 | tf_op jit(solution)/shard_map/ppermute | solution.py:402
  54.4 0.0 copy-done.11
  54.4 1.0 %combine.1 = bf16[8,3072]{1,0:T(8,128)(2,1)} custom-call(s32[2,8]{1,0:T(2,128)S(1)} %bitcast.4, f32[8,8]{1,0:T(8,128)S(1)} %get-tuple-element.20.refs_4_.logits_ref, bf16[8,3072]{1,0:T(8,128)(2,1)S(1)} %get-tuple-element.33.refs_0_, bf16[8,3072]{1,0:T(8,128)(2,1)S(1)} %collective-permute-done.9.refs_1_, bf16[8,3072]{1,0:T(8,128)(2,1)S(1)} %collective-permute-done.10.refs_2_, ...), custom_call_target="tpu_custom_call" | custom-call | tf_op jit(solution)/shard_map/combine/pallas_call | solution.py:388
  (1 shorter events, 0.0 us)
Async XLA Ops:
  0.6 7.1 %copy-start.2 = (bf16[8,64,512]{2,1,0:T(8,128)(2,1)S(1)}, bf16[8,64,512]{2,1,0:T(8,128)(2,1)}, u32[]{:S(2)}) copy-start(bf16[8,64,512]{2,1,0:T(8,128)(2,1)} %k_hbm.1) | copy-start | bytes 1572868
  0.6 7.1 %copy-start.3 = (bf16[8,64,512]{2,1,0:T(8,128)(2,1)S(1)}, bf16[8,64,512]{2,1,0:T(8,128)(2,1)}, u32[]{:S(2)}) copy-start(bf16[8,64,512]{2,1,0:T(8,128)(2,1)} %v_hbm.1) | copy-start | bytes 1572868
  0.7 7.1 %copy-start.5 = (bf16[8,3072]{1,0:T(8,128)(2,1)S(1)}, bf16[8,3072]{1,0:T(8,128)(2,1)}, u32[]{:S(2)}) copy-start(bf16[8,3072]{1,0:T(8,128)(2,1)} %q_ref.1) | copy-start | bytes 147460
  0.7 7.1 %copy-start.6 = (bf16[8,3072]{1,0:T(8,128)(2,1)S(1)}, bf16[8,3072]{1,0:T(8,128)(2,1)}, u32[]{:S(2)}) copy-start(bf16[8,3072]{1,0:T(8,128)(2,1)} %x_hbm.1) | copy-start | bytes 147460
  0.7 7.1 %copy-start.7 = (bf16[3072,8]{0,1:T(8,128)(2,1)S(1)}, bf16[3072,8]{0,1:T(8,128)(2,1)}, u32[]{:S(2)}) copy-start(bf16[3072,8]{0,1:T(8,128)(2,1)} %param.15) | copy-start | bytes 147460
  0.7 7.1 %copy-start.8 = (bf16[3072]{0:T(1024)(128)(2,1)S(1)}, bf16[3072]{0:T(1024)(128)(2,1)}, u32[]{:S(2)}) copy-start(bf16[3072]{0:T(1024)(128)(2,1)} %gain_ref.3) | copy-start | bytes 18436
  0.7 7.1 %copy-start.9 = (bf16[8,512]{1,0:T(8,128)(2,1)S(1)}, bf16[8,512]{1,0:T(8,128)(2,1)}, u32[]{:S(2)}) copy-start(bf16[8,512]{1,0:T(8,128)(2,1)} %nk_ref.1) | copy-start | bytes 24580
  0.7 7.1 %copy-start.10 = (bf16[8,512]{1,0:T(8,128)(2,1)S(1)}, bf16[8,512]{1,0:T(8,128)(2,1)}, u32[]{:S(2)}) copy-start(bf16[8,512]{1,0:T(8,128)(2,1)} %nv_ref.1) | copy-start | bytes 24580
  0.7 7.1 %copy-start.12 = (s32[8]{0:T(128)S(1)}, s32[8]{0:T(128)}, u32[]{:S(2)}) copy-start(s32[8]{0:T(128)} %lengths_ref.1) | copy-start | bytes 100
  0.7 19.7 %copy-start = (bf16[1,3072,4096]{2,1,0:T(8,128)(2,1)S(1)}, bf16[1,3072,4096]{2,1,0:T(8,128)(2,1)}, u32[]{:S(2)}) copy-start(bf16[1,3072,4096]{2,1,0:T(8,128)(2,1)} %gate_ref.1) | copy-start | bytes 75497472
  0.7 19.7 %copy-start.1 = (bf16[1,3072,4096]{2,1,0:T(8,128)(2,1)S(1)}, bf16[1,3072,4096]{2,1,0:T(8,128)(2,1)}, u32[]{:S(2)}) copy-start(bf16[1,3072,4096]{2,1,0:T(8,128)(2,1)} %up_ref.1) | copy-start | bytes 75497472
  2.0 8.8 %collective-permute-start = (bf16[8,3072]{1,0:T(8,128)(2,1)S(1)}, bf16[8,3072]{1,0:T(8,128)(2,1)S(1)}, u32[]{:S(2)}, u32[]{:S(2)}) collective-permute-start(bf16[8,3072]{1,0:T(8,128)(2,1)S(1)} %get-tuple-element.22), channel_id=1, source_target_pairs={{0,4},{1,5},{2,6},{3,7},{4,0},{5,1},{6,2},{7,3},{8,12},{9,13},{10,... | collective-permute-start | bytes 147464 | tf_op jit(solution)/shard_map/ppermute | solution.py:402
  5.1 5.9 %collective-permute-start.1 = (bf16[8,3072]{1,0:T(8,128)(2,1)S(1)}, bf16[8,3072]{1,0:T(8,128)(2,1)S(1)}, u32[]{:S(2)}, u32[]{:S(2)}) collective-permute-start(bf16[8,3072]{1,0:T(8,128)(2,1)S(1)} %get-tuple-element.23), channel_id=1, source_target_pairs={{0,8},{1,9},{2,10},{3,11},{4,12},{5,13},{6,14},{7,15},{8,0},{9,1},... | collective-permute-start | bytes 147464 | tf_op jit(solution)/shard_map/ppermute | solution.py:402
  7.7 5.9 %collective-permute-start.2 = (bf16[8,3072]{1,0:T(8,128)(2,1)S(1)}, bf16[8,3072]{1,0:T(8,128)(2,1)S(1)}, u32[]{:S(2)}, u32[]{:S(2)}) collective-permute-start(bf16[8,3072]{1,0:T(8,128)(2,1)S(1)} %get-tuple-element.24), channel_id=1, source_target_pairs={{0,12},{1,13},{2,14},{3,15},{4,8},{5,9},{6,10},{7,11},{8,4},{9,5},... | collective-permute-start | bytes 147464 | tf_op jit(solution)/shard_map/ppermute | solution.py:402
  13.8 6.0 %copy-start.4 = (bf16[16,3072]{1,0:T(8,128)(2,1)}, bf16[16,3072]{1,0:T(8,128)(2,1)S(1)}, u32[]{:S(2)}) copy-start(bf16[16,3072]{1,0:T(8,128)(2,1)S(1)} %get-tuple-element.25.a_ref) | copy-start | bytes 294916
  13.8 4.7 %collective-permute-start.3 = (bf16[16,3072]{1,0:T(8,128)(2,1)S(1)}, bf16[16,3072]{1,0:T(8,128)(2,1)S(1)}, u32[]{:S(2)}, u32[]{:S(2)}) collective-permute-start(bf16[16,3072]{1,0:T(8,128)(2,1)S(1)} %get-tuple-element.26), channel_id=1, source_target_pairs={{0,2},{1,3},{2,0},{3,1},{4,6},{5,7},{6,4},{7,5},{8,10},{9,11},{10,... | collective-permute-start | bytes 294920 | tf_op jit(solution)/shard_map/ppermute | solution.py:402
  15.4 39.0 %copy-start.11 = (s32[8,2]{0,1:T(2,128)S(1)}, s32[8,2]{0,1:T(2,128)}, u32[]{:S(2)}) copy-start(s32[8,2]{0,1:T(2,128)} %param.16) | copy-start | bytes 196
  15.4 3.1 %collective-permute-start.4 = (bf16[16,3072]{1,0:T(8,128)(2,1)S(1)}, bf16[16,3072]{1,0:T(8,128)(2,1)S(1)}, u32[]{:S(2)}, u32[]{:S(2)}) collective-permute-start(bf16[16,3072]{1,0:T(8,128)(2,1)S(1)} %get-tuple-element.25.a_ref), channel_id=1, source_target_pairs={{0,1},{1,0},{2,3},{3,2},{4,5},{5,4},{6,7},{7,6},{8,9},{9,8},{10,11... | collective-permute-start | bytes 294920 | tf_op jit(solution)/shard_map/ppermute | solution.py:402
  18.5 1.3 %copy-start.13 = (bf16[16,3072]{1,0:T(8,128)(2,1)}, bf16[16,3072]{1,0:T(8,128)(2,1)S(1)}, u32[]{:S(2)}) copy-start(bf16[16,3072]{1,0:T(8,128)(2,1)S(1)} %collective-permute-done.3.b_ref) | copy-start | bytes 294916
  18.5 1.3 %collective-permute-start.5 = (bf16[16,3072]{1,0:T(8,128)(2,1)S(1)}, bf16[16,3072]{1,0:T(8,128)(2,1)S(1)}, u32[]{:S(2)}, u32[]{:S(2)}) collective-permute-start(bf16[16,3072]{1,0:T(8,128)(2,1)S(1)} %collective-permute-done.3.b_ref), channel_id=1, source_target_pairs={{0,1},{1,0},{2,3},{3,2},{4,5},{5,4},{6,7},{7,6},{8,9},{9,8},{10,11... | collective-permute-start | bytes 294920 | tf_op jit(solution)/shard_map/ppermute | solution.py:402
  18.5 1.3 %copy-start.14 = (bf16[16,3072]{1,0:T(8,128)(2,1)}, bf16[16,3072]{1,0:T(8,128)(2,1)S(1)}, u32[]{:S(2)}) copy-start(bf16[16,3072]{1,0:T(8,128)(2,1)S(1)} %collective-permute-done.4.c_ref) | copy-start | bytes 294916
  19.8 0.6 %copy-start.15 = (bf16[16,3072]{1,0:T(8,128)(2,1)}, bf16[16,3072]{1,0:T(8,128)(2,1)S(1)}, u32[]{:S(2)}) copy-start(bf16[16,3072]{1,0:T(8,128)(2,1)S(1)} %collective-permute-done.5.d_ref) | copy-start | bytes 294916
  39.8 1.4 %collective-permute-start.6 = (bf16[16,3072]{1,0:T(8,128)(2,1)S(1)}, bf16[16,3072]{1,0:T(8,128)(2,1)S(1)}, u32[]{:S(2)}, u32[]{:S(2)}) collective-permute-start(bf16[16,3072]{1,0:T(8,128)(2,1)S(1)} %get-tuple-element.29), channel_id=1, source_target_pairs={{0,1},{1,0},{2,3},{3,2},{4,5},{5,4},{6,7},{7,6},{8,9},{9,8},{10,11... | collective-permute-start | bytes 294920 | tf_op jit(solution)/shard_map/ppermute | solution.py:402
  40.0 1.3 %collective-permute-start.7 = (bf16[16,3072]{1,0:T(8,128)(2,1)S(1)}, bf16[16,3072]{1,0:T(8,128)(2,1)S(1)}, u32[]{:S(2)}, u32[]{:S(2)}) collective-permute-start(bf16[16,3072]{1,0:T(8,128)(2,1)S(1)} %get-tuple-element.30), channel_id=1, source_target_pairs={{0,1},{1,0},{2,3},{3,2},{4,5},{5,4},{6,7},{7,6},{8,9},{9,8},{10,11... | collective-permute-start | bytes 294920 | tf_op jit(solution)/shard_map/ppermute | solution.py:402
  41.4 5.1 %collective-permute-start.8 = (bf16[16,3072]{1,0:T(8,128)(2,1)S(1)}, bf16[16,3072]{1,0:T(8,128)(2,1)S(1)}, u32[]{:S(2)}, u32[]{:S(2)}) collective-permute-start(bf16[16,3072]{1,0:T(8,128)(2,1)S(1)} %get-tuple-element.32), channel_id=1, source_target_pairs={{0,2},{1,3},{2,0},{3,1},{4,6},{5,7},{6,4},{7,5},{8,10},{9,11},{10,... | collective-permute-start | bytes 294920 | tf_op jit(solution)/shard_map/ppermute | solution.py:402
  46.7 4.5 %collective-permute-start.9 = (bf16[8,3072]{1,0:T(8,128)(2,1)S(1)}, bf16[8,3072]{1,0:T(8,128)(2,1)S(1)}, u32[]{:S(2)}, u32[]{:S(2)}) collective-permute-start(bf16[8,3072]{1,0:T(8,128)(2,1)S(1)} %get-tuple-element.34), channel_id=1, source_target_pairs={{0,4},{1,5},{2,6},{3,7},{4,0},{5,1},{6,2},{7,3},{8,12},{9,13},{10,... | collective-permute-start | bytes 147464 | tf_op jit(solution)/shard_map/ppermute | solution.py:402
  46.8 5.8 %collective-permute-start.10 = (bf16[8,3072]{1,0:T(8,128)(2,1)S(1)}, bf16[8,3072]{1,0:T(8,128)(2,1)S(1)}, u32[]{:S(2)}, u32[]{:S(2)}) collective-permute-start(bf16[8,3072]{1,0:T(8,128)(2,1)S(1)} %get-tuple-element.35), channel_id=1, source_target_pairs={{0,8},{1,9},{2,10},{3,11},{4,12},{5,13},{6,14},{7,15},{8,0},{9,1},... | collective-permute-start | bytes 147464 | tf_op jit(solution)/shard_map/ppermute | solution.py:402
  48.5 5.9 %collective-permute-start.11 = (bf16[8,3072]{1,0:T(8,128)(2,1)S(1)}, bf16[8,3072]{1,0:T(8,128)(2,1)S(1)}, u32[]{:S(2)}, u32[]{:S(2)}) collective-permute-start(bf16[8,3072]{1,0:T(8,128)(2,1)S(1)} %get-tuple-element.36), channel_id=1, source_target_pairs={{0,12},{1,13},{2,14},{3,15},{4,8},{5,9},{6,10},{7,11},{8,4},{9,5},... | collective-permute-start | bytes 147464 | tf_op jit(solution)/shard_map/ppermute | solution.py:402

commit v2 on v1

--- a/solution.py
+++ b/solution.py
@@ -11,7 +11,7 @@
 KVH = 4
 HD = 128
 GROUP = 6
-TILE = 256
+TILE = 512
 MIB = 1 << 20
 F32 = jnp.float32
 BF16 = jnp.bfloat16
@@ -320,39 +320,53 @@
     far0_ref,
     far1_ref,
     x_buf,
+    hidden,
     total,
     down_buf,
     sems,
 ):
     tiles = gate_ref.shape[2] // TILE
     part = a_ref.shape[0]
+    lines = total.shape[0]
     for tile in range(min(slots, tiles)):
         down_copy(down_ref, down_buf, sems, tile, tile).start()
     for i, ref in enumerate((a_ref, b_ref, c_ref, d_ref)):
         x_buf[i * part : (i + 1) * part, :] = rms(ref[...], gain_ref[...])
+    x_buf[lines:, :] = jnp.zeros_like(x_buf[lines:, :])
     total[...] = jnp.zeros_like(total)
 
-    def step(tile, carry):
-        slot = lax.rem(tile, slots)
+    def activate(tile):
         cols = pl.ds(pl.multiple_of(tile * TILE, TILE), TILE)
         x = x_buf[...]
         gated = jnp.dot(x, gate_ref[0, :, cols], preferred_element_type=F32)
         upper = jnp.dot(x, up_ref[0, :, cols], preferred_element_type=F32)
-        hidden = (gated / (1.0 + jnp.exp(-gated)) * upper).astype(BF16)
+        return (gated / (1.0 + jnp.exp(-gated)) * upper).astype(BF16)
+
+    def project(tile):
+        slot = lax.rem(tile, slots)
         down_copy(down_ref, down_buf, sems, tile, slot).wait()
-        total[...] += jnp.dot(hidden, down_buf[slot], preferred_element_type=F32)
-
+        return jnp.dot(hidden[lax.rem(tile, 2)], down_buf[slot], preferred_element_type=F32)
+
+    def refill(tile):
         @pl.when(tile + slots < tiles)
         def _():
-            down_copy(down_ref, down_buf, sems, tile + slots, slot).start()
-
+            down_copy(down_ref, down_buf, sems, tile + slots, lax.rem(tile, slots)).start()
+
+    hidden[0] = activate(0)
+
+    def step(tile, carry):
+        product = project(tile - 1)
+        hidden[lax.rem(tile, 2)] = activate(tile)
+        total[...] += product[:lines]
+        refill(tile - 1)
         return carry
 
-    lax.fori_loop(0, tiles, step, 0)
-    own0_ref[...] = total[:part]
-    own1_ref[...] = total[part : 2 * part]
-    far0_ref[...] = total[2 * part : 3 * part].astype(BF16)
-    far1_ref[...] = total[3 * part :].astype(BF16)
+    lax.fori_loop(1, tiles, step, 0)
+    result = total[...] + project(tiles - 1)[:lines]
+    own0_ref[...] = result[:part]
+    own1_ref[...] = result[part : 2 * part]
+    far0_ref[...] = result[2 * part : 3 * part].astype(BF16)
+    far1_ref[...] = result[3 * part :].astype(BF16)
 
 
 def combine_kernel(capacity, routes_ref, logits_ref, *refs):
@@ -479,29 +493,31 @@
     far_keep = exchange(keep, 1)
     across = exchange(send, 2)
     far_across = exchange(across, 1)
-    slots = 3
+    slots = 2
+    lines = max(4 * half, 128)
     own0, own1, far0, far1 = call(
         functools.partial(expert_kernel, slots),
         "expert",
         (held(half, F32), held(half, F32), held(half), held(half)),
         [WHOLE] * 7 + [ANY],
         (
-            keep,
-            across,
-            far_keep,
-            far_across,
+            *[
+                pltpu.with_memory_space_constraint(part, pltpu.VMEM)
+                for part in (keep, across, far_keep, far_across)
+            ],
             gain,
             pltpu.with_memory_space_constraint(gate_weight, pltpu.VMEM),
             pltpu.with_memory_space_constraint(up_weight, pltpu.VMEM),
             down_weight,
         ),
         [
-            pltpu.VMEM((4 * half, width), BF16),
+            pltpu.VMEM((lines, width), BF16),
+            pltpu.VMEM((2, lines, TILE), BF16),
             pltpu.VMEM((4 * half, width), F32),
             pltpu.VMEM((slots, TILE, width), BF16),
             pltpu.SemaphoreType.DMA((slots,)),
         ],
-        limit=9,
+        limit=12,
     )
     back0, back1 = exchange(far0, 1), exchange(far1, 1)
     sum0, sum1 = call(

time: 55.6 us -> 49.5 us (0.89)
  Pallas kernels: 25.1 us -> 19.1 us
  local copies, waits for them, and re-layouts: 0.69 us -> 0.05 us
  waiting for transfers between devices: 14.8 us -> 15.4 us
    pallas_call x7, Pallas kernels: 25.1 us -> 19.1 us  [call(): pl.pallas_call(kernel, out_shape=outs, in_specs=ins, out_specs=tuple((WHO...]
    unnamed x32 -> x24, local copies, waits for them, and re-layouts: 0.69 us -> 0.05 us
    ppermute x12, waiting for transfers between devices: 14.8 us -> 15.4 us  [exchange(): return lax.ppermute(values, 'node', [(i, i ^ bits) for i in range(size)])]
where the time goes in v2:
time: 49.5 us; the launch traced here: 49.3 us
  Pallas kernels  19.1 us (39%)
  waiting for transfers between devices  15.4 us (31%)
  starting transfers between devices  13.9 us (28%)
  between operations  0.85 us (2%)
    pallas_call x7, Pallas kernels, call(): pl.pallas_call(kernel, out_shape=outs, in_specs=ins, out_specs=tuple((WHO...  19.1 us
    ppermute x12, waiting for transfers between devices, exchange(): return lax.ppermute(values, 'node', [(i, i ^ bits) for i in range(size)])  15.4 us
    ppermute x12, starting transfers between devices, exchange(): return lax.ppermute(values, 'node', [(i, i ^ bits) for i in range(size)])  13.9 us
  transfers between devices with their start and end apart: 12, of which 9 were waited for; matrix products, arithmetic and copies ran while one was open for 0% of the time, Pallas kernels for 6%

profile of v2, /device:TPU:0, one launch (start us, length us, event | category | flops | bytes accessed | tf_op | source)
XLA Modules:
  0.0 49.3 jit_solution(4535119657120156532)
XLA Ops:
  0.6 0.0 copy-start.2
  0.6 0.0 copy-start.3
  0.7 0.0 copy-start.4
  0.7 0.0 copy-start.5
  0.7 0.0 copy-start.6
  0.7 0.0 copy-start.7
  0.7 0.0 copy-start.8
  0.7 0.0 copy-start.9
  0.7 0.0 copy-start.11
  0.7 0.0 copy-start
  0.7 0.0 copy-start.1
  0.7 1.3 %pack.1 = (bf16[8,3072]{1,0:T(8,128)(2,1)S(1)}, bf16[8,3072]{1,0:T(8,128)(2,1)S(1)}, bf16[8,3072]{1,0:T(8,128)(2,1)S(1)}, bf16[8,3072]{1,0:T(8,128)(2,1)S(1)}) custom-call(bf16[8,3072]{1,0:T(8,128)(2,1)} %x_hbm.1, s32[2,8]{1,0:T(2,128)} %bitcast.3), custom_call_target="tpu_custom_call" | custom-call | flops 99999997952 | bytes 67108864 | tf_op jit(solution)/shard_map/pack/pallas_call | solution.py:402
  2.0 3.1 %collective-permute-start = (bf16[8,3072]{1,0:T(8,128)(2,1)S(1)}, bf16[8,3072]{1,0:T(8,128)(2,1)S(1)}, u32[]{:S(2)}, u32[]{:S(2)}) collective-permute-start(bf16[8,3072]{1,0:T(8,128)(2,1)S(1)} %get-tuple-element.22), channel_id=1, source_target_pairs={{0,4},{1,5},{2,6},{3,7},{4,0},{5,1},{6,2},{7,3},{8,12},{9,13},{10,... | collective-permute-start | bytes 147464 | tf_op jit(solution)/shard_map/ppermute | solution.py:416
  5.1 2.6 %collective-permute-start.1 = (bf16[8,3072]{1,0:T(8,128)(2,1)S(1)}, bf16[8,3072]{1,0:T(8,128)(2,1)S(1)}, u32[]{:S(2)}, u32[]{:S(2)}) collective-permute-start(bf16[8,3072]{1,0:T(8,128)(2,1)S(1)} %get-tuple-element.23), channel_id=1, source_target_pairs={{0,8},{1,9},{2,10},{3,11},{4,12},{5,13},{6,14},{7,15},{8,0},{9,1},... | collective-permute-start | bytes 147464 | tf_op jit(solution)/shard_map/ppermute | solution.py:416
  7.7 0.0 collective-permute-start.2
  7.7 0.0 copy-done.2
  7.7 0.0 copy-done.3
  7.7 0.0 copy-done.4
  7.7 0.0 copy-done.5
  7.8 0.0 copy-done.6
  7.8 0.0 copy-done.7
  7.8 0.0 copy-done.8
  7.8 0.0 copy-done.9
  7.8 0.0 copy-done.11
  7.8 3.1 %side.1 = (bf16[8,3072]{1,0:T(8,128)(2,1)}, f32[8,8]{1,0:T(8,128)S(1)}) custom-call(s32[8]{0:T(128)S(1)} %copy-done.11, bf16[8,3072]{1,0:T(8,128)(2,1)S(1)} %copy-done.4, bf16[8,64,512]{2,1,0:T(8,128)(2,1)S(1)} %copy-done.2, bf16[8,64,512]{2,1,0:T(8,128)(2,1)S(1)} %copy-done.3, bf16[8,512]{1,0:T(8,128)(2,1)S(1)} %copy-done.8, bf16[8,512]{1,0:T(8,128)(2,1)S(1)} %copy-done.9, ...), custom_call_target="tpu_custom_call" | custom-call | flops 100000000 | bytes 4194304 | tf_op jit(solution)/shard_map/side/pallas_call | solution.py:402
  10.9 0.0 collective-permute-done.refs_1_
  10.9 0.2 collective-permute-done.1.refs_2_
  11.1 2.6 %collective-permute-done.2.refs_3_ = bf16[8,3072]{1,0:T(8,128)(2,1)S(1)} collective-permute-done((bf16[8,3072]{1,0:T(8,128)(2,1)S(1)}, bf16[8,3072]{1,0:T(8,128)(2,1)S(1)}, u32[]{:S(2)}, u32[]{:S(2)}) %collective-permute-start.2) | collective-permute-done | bytes 49184 | tf_op jit(solution)/shard_map/ppermute | solution.py:416
  13.6 0.2 halves.1
  13.8 1.6 %collective-permute-start.3 = (bf16[16,3072]{1,0:T(8,128)(2,1)S(1)}, bf16[16,3072]{1,0:T(8,128)(2,1)S(1)}, u32[]{:S(2)}, u32[]{:S(2)}) collective-permute-start(bf16[16,3072]{1,0:T(8,128)(2,1)S(1)} %get-tuple-element.26), channel_id=1, source_target_pairs={{0,2},{1,3},{2,0},{3,1},{4,6},{5,7},{6,4},{7,5},{8,10},{9,11},{10,... | collective-permute-start | bytes 294920 | tf_op jit(solution)/shard_map/ppermute | solution.py:416
  15.4 0.0 copy-start.10
  15.4 0.0 collective-permute-start.4
  15.4 3.1 %collective-permute-done.3.b_ref = bf16[16,3072]{1,0:T(8,128)(2,1)S(1)} collective-permute-done((bf16[16,3072]{1,0:T(8,128)(2,1)S(1)}, bf16[16,3072]{1,0:T(8,128)(2,1)S(1)}, u32[]{:S(2)}, u32[]{:S(2)}) %collective-permute-start.3) | collective-permute-done | bytes 98336 | tf_op jit(solution)/shard_map/ppermute | solution.py:416
  18.5 0.0 collective-permute-start.5
  18.5 0.0 collective-permute-done.4.c_ref
  18.5 1.3 %collective-permute-done.5.d_ref = bf16[16,3072]{1,0:T(8,128)(2,1)S(1)} collective-permute-done((bf16[16,3072]{1,0:T(8,128)(2,1)S(1)}, bf16[16,3072]{1,0:T(8,128)(2,1)S(1)}, u32[]{:S(2)}, u32[]{:S(2)}) %collective-permute-start.5) | collective-permute-done | bytes 98336 | tf_op jit(solution)/shard_map/ppermute | solution.py:416
  19.8 0.0 copy-done
  19.8 0.0 copy-done.1
  19.8 13.3 %expert.1 = (f32[16,3072]{1,0:T(8,128)S(1)}, f32[16,3072]{1,0:T(8,128)S(1)}, bf16[16,3072]{1,0:T(8,128)(2,1)S(1)}, bf16[16,3072]{1,0:T(8,128)(2,1)S(1)}) custom-call(bf16[16,3072]{1,0:T(8,128)(2,1)S(1)} %get-tuple-element.25.a_ref, bf16[16,3072]{1,0:T(8,128)(2,1)S(1)} %collective-permute-done.3.b_ref, bf16[16,3072]{1,0:T(8,128)(2,1)S(1)} %collective-permute-done.4.c_ref, ...), custom_call_target="tpu_custom_call" | custom-call | tf_op jit(solution)/shard_map/expert/pallas_call | solution.py:402
  33.1 0.2 collective-permute-start.6
  33.4 0.4 collective-permute-start.7
  33.7 0.8 %collective-permute-done.6.right0_ref = bf16[16,3072]{1,0:T(8,128)(2,1)S(1)} collective-permute-done((bf16[16,3072]{1,0:T(8,128)(2,1)S(1)}, bf16[16,3072]{1,0:T(8,128)(2,1)S(1)}, u32[]{:S(2)}, u32[]{:S(2)}) %collective-permute-start.6) | collective-permute-done | bytes 98336 | tf_op jit(solution)/shard_map/ppermute | solution.py:416
  34.5 0.2 collective-permute-done.7.right1_ref
  34.7 1.6 %collective-permute-start.8 = (bf16[16,3072]{1,0:T(8,128)(2,1)S(1)}, bf16[16,3072]{1,0:T(8,128)(2,1)S(1)}, u32[]{:S(2)}, u32[]{:S(2)}) collective-permute-start(bf16[16,3072]{1,0:T(8,128)(2,1)S(1)} %get-tuple-element.32), channel_id=1, source_target_pairs={{0,2},{1,3},{2,0},{3,1},{4,6},{5,7},{6,4},{7,5},{8,10},{9,11},{10,... | collective-permute-start | bytes 294920 | tf_op jit(solution)/shard_map/ppermute | solution.py:416
  36.3 3.5 %collective-permute-done.8.other_ref = bf16[16,3072]{1,0:T(8,128)(2,1)S(1)} collective-permute-done((bf16[16,3072]{1,0:T(8,128)(2,1)S(1)}, bf16[16,3072]{1,0:T(8,128)(2,1)S(1)}, u32[]{:S(2)}, u32[]{:S(2)}) %collective-permute-start.8) | collective-permute-done | bytes 98336 | tf_op jit(solution)/shard_map/ppermute | solution.py:416
  39.8 0.2 blocks.1
  40.0 0.1 collective-permute-start.9
  40.1 2.3 %collective-permute-start.10 = (bf16[8,3072]{1,0:T(8,128)(2,1)S(1)}, bf16[8,3072]{1,0:T(8,128)(2,1)S(1)}, u32[]{:S(2)}, u32[]{:S(2)}) collective-permute-start(bf16[8,3072]{1,0:T(8,128)(2,1)S(1)} %get-tuple-element.35), channel_id=1, source_target_pairs={{0,8},{1,9},{2,10},{3,11},{4,12},{5,13},{6,14},{7,15},{8,0},{9,1},... | collective-permute-start | bytes 147464 | tf_op jit(solution)/shard_map/ppermute | solution.py:416
  42.4 2.1 %collective-permute-start.11 = (bf16[8,3072]{1,0:T(8,128)(2,1)S(1)}, bf16[8,3072]{1,0:T(8,128)(2,1)S(1)}, u32[]{:S(2)}, u32[]{:S(2)}) collective-permute-start(bf16[8,3072]{1,0:T(8,128)(2,1)S(1)} %get-tuple-element.36), channel_id=1, source_target_pairs={{0,12},{1,13},{2,14},{3,15},{4,8},{5,9},{6,10},{7,11},{8,4},{9,5},... | collective-permute-start | bytes 147464 | tf_op jit(solution)/shard_map/ppermute | solution.py:416
  44.5 0.0 collective-permute-done.9.refs_1_
  44.5 0.9 %collective-permute-done.10.refs_2_ = bf16[8,3072]{1,0:T(8,128)(2,1)S(1)} collective-permute-done((bf16[8,3072]{1,0:T(8,128)(2,1)S(1)}, bf16[8,3072]{1,0:T(8,128)(2,1)S(1)}, u32[]{:S(2)}, u32[]{:S(2)}) %collective-permute-start.10) | collective-permute-done | bytes 49184 | tf_op jit(solution)/shard_map/ppermute | solution.py:416
  45.4 2.8 %collective-permute-done.11.refs_3_ = bf16[8,3072]{1,0:T(8,128)(2,1)S(1)} collective-permute-done((bf16[8,3072]{1,0:T(8,128)(2,1)S(1)}, bf16[8,3072]{1,0:T(8,128)(2,1)S(1)}, u32[]{:S(2)}, u32[]{:S(2)}) %collective-permute-start.11) | collective-permute-done | bytes 49184 | tf_op jit(solution)/shard_map/ppermute | solution.py:416
  48.3 0.0 copy-done.10
  48.3 1.0 %combine.1 = bf16[8,3072]{1,0:T(8,128)(2,1)} custom-call(s32[2,8]{1,0:T(2,128)S(1)} %bitcast.4, f32[8,8]{1,0:T(8,128)S(1)} %get-tuple-element.20.refs_4_.logits_ref, bf16[8,3072]{1,0:T(8,128)(2,1)S(1)} %get-tuple-element.33.refs_0_, bf16[8,3072]{1,0:T(8,128)(2,1)S(1)} %collective-permute-done.9.refs_1_, bf16[8,3072]{1,0:T(8,128)(2,1)S(1)} %collective-permute-done.10.refs_2_, ...), custom_call_target="tpu_custom_call" | custom-call | tf_op jit(solution)/shard_map/combine/pallas_call | solution.py:402
  (1 shorter events, 0.0 us)
Async XLA Ops:
  0.6 7.1 %copy-start.2 = (bf16[8,64,512]{2,1,0:T(8,128)(2,1)S(1)}, bf16[8,64,512]{2,1,0:T(8,128)(2,1)}, u32[]{:S(2)}) copy-start(bf16[8,64,512]{2,1,0:T(8,128)(2,1)} %k_hbm.1) | copy-start | bytes 1572868
  0.6 7.1 %copy-start.3 = (bf16[8,64,512]{2,1,0:T(8,128)(2,1)S(1)}, bf16[8,64,512]{2,1,0:T(8,128)(2,1)}, u32[]{:S(2)}) copy-start(bf16[8,64,512]{2,1,0:T(8,128)(2,1)} %v_hbm.1) | copy-start | bytes 1572868
  0.7 7.1 %copy-start.4 = (bf16[8,3072]{1,0:T(8,128)(2,1)S(1)}, bf16[8,3072]{1,0:T(8,128)(2,1)}, u32[]{:S(2)}) copy-start(bf16[8,3072]{1,0:T(8,128)(2,1)} %q_ref.1) | copy-start | bytes 147460
  0.7 7.1 %copy-start.5 = (bf16[8,3072]{1,0:T(8,128)(2,1)S(1)}, bf16[8,3072]{1,0:T(8,128)(2,1)}, u32[]{:S(2)}) copy-start(bf16[8,3072]{1,0:T(8,128)(2,1)} %x_hbm.1) | copy-start | bytes 147460
  0.7 7.1 %copy-start.6 = (bf16[3072,8]{0,1:T(8,128)(2,1)S(1)}, bf16[3072,8]{0,1:T(8,128)(2,1)}, u32[]{:S(2)}) copy-start(bf16[3072,8]{0,1:T(8,128)(2,1)} %param.15) | copy-start | bytes 147460
  0.7 7.1 %copy-start.7 = (bf16[3072]{0:T(1024)(128)(2,1)S(1)}, bf16[3072]{0:T(1024)(128)(2,1)}, u32[]{:S(2)}) copy-start(bf16[3072]{0:T(1024)(128)(2,1)} %gain_ref.3) | copy-start | bytes 18436
  0.7 7.1 %copy-start.8 = (bf16[8,512]{1,0:T(8,128)(2,1)S(1)}, bf16[8,512]{1,0:T(8,128)(2,1)}, u32[]{:S(2)}) copy-start(bf16[8,512]{1,0:T(8,128)(2,1)} %nk_ref.1) | copy-start | bytes 24580
  0.7 7.1 %copy-start.9 = (bf16[8,512]{1,0:T(8,128)(2,1)S(1)}, bf16[8,512]{1,0:T(8,128)(2,1)}, u32[]{:S(2)}) copy-start(bf16[8,512]{1,0:T(8,128)(2,1)} %nv_ref.1) | copy-start | bytes 24580
  0.7 7.1 %copy-start.11 = (s32[8]{0:T(128)S(1)}, s32[8]{0:T(128)}, u32[]{:S(2)}) copy-start(s32[8]{0:T(128)} %lengths_ref.1) | copy-start | bytes 100
  0.7 19.1 %copy-start = (bf16[1,3072,4096]{2,1,0:T(8,128)(2,1)S(1)}, bf16[1,3072,4096]{2,1,0:T(8,128)(2,1)}, u32[]{:S(2)}) copy-start(bf16[1,3072,4096]{2,1,0:T(8,128)(2,1)} %gate_ref.1) | copy-start | bytes 75497472
  0.7 19.1 %copy-start.1 = (bf16[1,3072,4096]{2,1,0:T(8,128)(2,1)S(1)}, bf16[1,3072,4096]{2,1,0:T(8,128)(2,1)}, u32[]{:S(2)}) copy-start(bf16[1,3072,4096]{2,1,0:T(8,128)(2,1)} %up_ref.1) | copy-start | bytes 75497472
  2.0 8.8 %collective-permute-start = (bf16[8,3072]{1,0:T(8,128)(2,1)S(1)}, bf16[8,3072]{1,0:T(8,128)(2,1)S(1)}, u32[]{:S(2)}, u32[]{:S(2)}) collective-permute-start(bf16[8,3072]{1,0:T(8,128)(2,1)S(1)} %get-tuple-element.22), channel_id=1, source_target_pairs={{0,4},{1,5},{2,6},{3,7},{4,0},{5,1},{6,2},{7,3},{8,12},{9,13},{10,... | collective-permute-start | bytes 147464 | tf_op jit(solution)/shard_map/ppermute | solution.py:416
  5.1 5.9 %collective-permute-start.1 = (bf16[8,3072]{1,0:T(8,128)(2,1)S(1)}, bf16[8,3072]{1,0:T(8,128)(2,1)S(1)}, u32[]{:S(2)}, u32[]{:S(2)}) collective-permute-start(bf16[8,3072]{1,0:T(8,128)(2,1)S(1)} %get-tuple-element.23), channel_id=1, source_target_pairs={{0,8},{1,9},{2,10},{3,11},{4,12},{5,13},{6,14},{7,15},{8,0},{9,1},... | collective-permute-start | bytes 147464 | tf_op jit(solution)/shard_map/ppermute | solution.py:416
  7.7 5.9 %collective-permute-start.2 = (bf16[8,3072]{1,0:T(8,128)(2,1)S(1)}, bf16[8,3072]{1,0:T(8,128)(2,1)S(1)}, u32[]{:S(2)}, u32[]{:S(2)}) collective-permute-start(bf16[8,3072]{1,0:T(8,128)(2,1)S(1)} %get-tuple-element.24), channel_id=1, source_target_pairs={{0,12},{1,13},{2,14},{3,15},{4,8},{5,9},{6,10},{7,11},{8,4},{9,5},... | collective-permute-start | bytes 147464 | tf_op jit(solution)/shard_map/ppermute | solution.py:416
  13.8 4.7 %collective-permute-start.3 = (bf16[16,3072]{1,0:T(8,128)(2,1)S(1)}, bf16[16,3072]{1,0:T(8,128)(2,1)S(1)}, u32[]{:S(2)}, u32[]{:S(2)}) collective-permute-start(bf16[16,3072]{1,0:T(8,128)(2,1)S(1)} %get-tuple-element.26), channel_id=1, source_target_pairs={{0,2},{1,3},{2,0},{3,1},{4,6},{5,7},{6,4},{7,5},{8,10},{9,11},{10,... | collective-permute-start | bytes 294920 | tf_op jit(solution)/shard_map/ppermute | solution.py:416
  15.4 32.9 %copy-start.10 = (s32[8,2]{0,1:T(2,128)S(1)}, s32[8,2]{0,1:T(2,128)}, u32[]{:S(2)}) copy-start(s32[8,2]{0,1:T(2,128)} %param.16) | copy-start | bytes 196
  15.4 3.1 %collective-permute-start.4 = (bf16[16,3072]{1,0:T(8,128)(2,1)S(1)}, bf16[16,3072]{1,0:T(8,128)(2,1)S(1)}, u32[]{:S(2)}, u32[]{:S(2)}) collective-permute-start(bf16[16,3072]{1,0:T(8,128)(2,1)S(1)} %get-tuple-element.25.a_ref), channel_id=1, source_target_pairs={{0,1},{1,0},{2,3},{3,2},{4,5},{5,4},{6,7},{7,6},{8,9},{9,8},{10,11... | collective-permute-start | bytes 294920 | tf_op jit(solution)/shard_map/ppermute | solution.py:416
  18.5 1.3 %collective-permute-start.5 = (bf16[16,3072]{1,0:T(8,128)(2,1)S(1)}, bf16[16,3072]{1,0:T(8,128)(2,1)S(1)}, u32[]{:S(2)}, u32[]{:S(2)}) collective-permute-start(bf16[16,3072]{1,0:T(8,128)(2,1)S(1)} %collective-permute-done.3.b_ref), channel_id=1, source_target_pairs={{0,1},{1,0},{2,3},{3,2},{4,5},{5,4},{6,7},{7,6},{8,9},{9,8},{10,11... | collective-permute-start | bytes 294920 | tf_op jit(solution)/shard_map/ppermute | solution.py:416
  33.1 1.4 %collective-permute-start.6 = (bf16[16,3072]{1,0:T(8,128)(2,1)S(1)}, bf16[16,3072]{1,0:T(8,128)(2,1)S(1)}, u32[]{:S(2)}, u32[]{:S(2)}) collective-permute-start(bf16[16,3072]{1,0:T(8,128)(2,1)S(1)} %get-tuple-element.29), channel_id=1, source_target_pairs={{0,1},{1,0},{2,3},{3,2},{4,5},{5,4},{6,7},{7,6},{8,9},{9,8},{10,11... | collective-permute-start | bytes 294920 | tf_op jit(solution)/shard_map/ppermute | solution.py:416
  33.4 1.3 %collective-permute-start.7 = (bf16[16,3072]{1,0:T(8,128)(2,1)S(1)}, bf16[16,3072]{1,0:T(8,128)(2,1)S(1)}, u32[]{:S(2)}, u32[]{:S(2)}) collective-permute-start(bf16[16,3072]{1,0:T(8,128)(2,1)S(1)} %get-tuple-element.30), channel_id=1, source_target_pairs={{0,1},{1,0},{2,3},{3,2},{4,5},{5,4},{6,7},{7,6},{8,9},{9,8},{10,11... | collective-permute-start | bytes 294920 | tf_op jit(solution)/shard_map/ppermute | solution.py:416
  34.7 5.1 %collective-permute-start.8 = (bf16[16,3072]{1,0:T(8,128)(2,1)S(1)}, bf16[16,3072]{1,0:T(8,128)(2,1)S(1)}, u32[]{:S(2)}, u32[]{:S(2)}) collective-permute-start(bf16[16,3072]{1,0:T(8,128)(2,1)S(1)} %get-tuple-element.32), channel_id=1, source_target_pairs={{0,2},{1,3},{2,0},{3,1},{4,6},{5,7},{6,4},{7,5},{8,10},{9,11},{10,... | collective-permute-start | bytes 294920 | tf_op jit(solution)/shard_map/ppermute | solution.py:416
  40.0 4.5 %collective-permute-start.9 = (bf16[8,3072]{1,0:T(8,128)(2,1)S(1)}, bf16[8,3072]{1,0:T(8,128)(2,1)S(1)}, u32[]{:S(2)}, u32[]{:S(2)}) collective-permute-start(bf16[8,3072]{1,0:T(8,128)(2,1)S(1)} %get-tuple-element.34), channel_id=1, source_target_pairs={{0,4},{1,5},{2,6},{3,7},{4,0},{5,1},{6,2},{7,3},{8,12},{9,13},{10,... | collective-permute-start | bytes 147464 | tf_op jit(solution)/shard_map/ppermute | solution.py:416
  40.1 5.3 %collective-permute-start.10 = (bf16[8,3072]{1,0:T(8,128)(2,1)S(1)}, bf16[8,3072]{1,0:T(8,128)(2,1)S(1)}, u32[]{:S(2)}, u32[]{:S(2)}) collective-permute-start(bf16[8,3072]{1,0:T(8,128)(2,1)S(1)} %get-tuple-element.35), channel_id=1, source_target_pairs={{0,8},{1,9},{2,10},{3,11},{4,12},{5,13},{6,14},{7,15},{8,0},{9,1},... | collective-permute-start | bytes 147464 | tf_op jit(solution)/shard_map/ppermute | solution.py:416
  42.4 5.9 %collective-permute-start.11 = (bf16[8,3072]{1,0:T(8,128)(2,1)S(1)}, bf16[8,3072]{1,0:T(8,128)(2,1)S(1)}, u32[]{:S(2)}, u32[]{:S(2)}) collective-permute-start(bf16[8,3072]{1,0:T(8,128)(2,1)S(1)} %get-tuple-element.36), channel_id=1, source_target_pairs={{0,12},{1,13},{2,14},{3,15},{4,8},{5,9},{6,10},{7,11},{8,4},{9,5},... | collective-permute-start | bytes 147464 | tf_op jit(solution)/shard_map/ppermute | solution.py:416

commit v3 on v2

--- a/solution.py
+++ b/solution.py
@@ -197,25 +197,18 @@
     send_ref[...] = moved[half:].astype(BF16)
 
 
-def blocks_kernel(capacity, mine_ref, other_ref, *out_refs):
-    mine = (lax.axis_index("node") // 2) % 2
+def merge_kernel(capacity, own_ref, far_ref, *out_refs):
     block = 2 * capacity
     lines = block * len(out_refs)
-    half = lines // 2
     out_line = lax.broadcasted_iota(jnp.int32, (lines, lines), 0)
     in_line = lax.broadcasted_iota(jnp.int32, (lines, lines), 1)
-    which = jnp.where((out_line % block) // capacity == mine, 0, 1)
-    source = which * half + (out_line // block) * capacity + out_line % capacity
+    which = (out_line % block) // capacity
+    source = which * (lines // 2) + (out_line // block) * capacity + out_line % capacity
     move = jnp.where(in_line == source, 1.0, 0.0).astype(BF16)
-    values = jnp.concatenate([mine_ref[...], other_ref[...]], axis=0)
+    values = (own_ref[...] + far_ref[...].astype(F32)).astype(BF16)
     moved = jnp.dot(move, values, preferred_element_type=F32)
     for k, out_ref in enumerate(out_refs):
         out_ref[...] = moved[k * block : (k + 1) * block].astype(BF16)
-
-
-def add_kernel(left0_ref, left1_ref, right0_ref, right1_ref, out0_ref, out1_ref):
-    out0_ref[...] = (left0_ref[...] + right0_ref[...].astype(F32)).astype(BF16)
-    out1_ref[...] = (left1_ref[...] + right1_ref[...].astype(F32)).astype(BF16)
 
 
 def rms(values, gain):
@@ -265,6 +258,7 @@
 
 
 def side_kernel(
+    capacity,
     lengths_ref,
     q_ref,
     k_hbm,
@@ -274,8 +268,9 @@
     x_ref,
     gain_ref,
     router_ref,
+    routes_ref,
     out_ref,
-    logits_ref,
+    table_ref,
     k_ref,
     v_ref,
     sems,
@@ -286,12 +281,13 @@
     ]
     for copy in copies:
         copy.start()
-    logits_ref[...] = lax.dot_general(
+    logits = lax.dot_general(
         router_ref[...],
         rms(x_ref[...], gain_ref[...]),
         (((1,), (1,)), ((), ())),
         preferred_element_type=F32,
     )
+    table_ref[...] = slot_weights(capacity, routes_ref[...], logits, table_ref.shape[0])
     for copy in copies:
         copy.wait()
     attention(lengths_ref, q_ref, k_ref, v_ref, nk_ref, nv_ref, out_ref)
@@ -315,10 +311,8 @@
     gate_ref,
     up_ref,
     down_ref,
-    own0_ref,
-    own1_ref,
-    far0_ref,
-    far1_ref,
+    own_ref,
+    far_ref,
     x_buf,
     hidden,
     total,
@@ -363,29 +357,40 @@
 
     lax.fori_loop(1, tiles, step, 0)
     result = total[...] + project(tiles - 1)[:lines]
-    own0_ref[...] = result[:part]
-    own1_ref[...] = result[part : 2 * part]
-    far0_ref[...] = result[2 * part : 3 * part].astype(BF16)
-    far1_ref[...] = result[3 * part :].astype(BF16)
-
-
-def combine_kernel(capacity, routes_ref, logits_ref, *refs):
-    *in_refs, out_ref = refs
-    column = lax.axis_index("node") // 4
-    routes = routes_ref[...]
-    logits = logits_ref[...]
+    own_ref[...] = result[: 2 * part]
+    far_ref[...] = result[2 * part :].astype(BF16)
+
+
+def slot_weights(capacity, routes, logits, lines):
+    column, mine = lax.axis_index("node") // 4, (lax.axis_index("node") // 2) % 2
+    shape = (lines, routes.shape[1])
+    line = lax.broadcasted_iota(jnp.int32, shape, 0)
+    block = 2 * capacity
+    which = (line % block) // capacity
+    experts = ((line // block) ^ column) * 2 + jnp.where(which == 0, mine, 1 - mine)
     expert = lax.broadcasted_iota(jnp.int32, logits.shape, 0)
     picked = [
         jnp.sum(jnp.where(routes[k : k + 1, :] == expert, logits, 0.0), axis=0, keepdims=True)
         for k in range(2)
     ]
-    block, rows = in_refs[0].shape[0], routes.shape[1]
-    lines = block * len(in_refs)
-    hits = select_slots(routes, line_experts(column, capacity, lines, rows), capacity)
-    table = jnp.zeros(hits[0].shape, F32)
+    hits = select_slots(routes, experts, capacity)
+    table = jnp.zeros(shape, F32)
     for k in range(2):
         weight = 1.0 / (1.0 + jnp.exp(picked[1 - k] - picked[k]))
         table += jnp.where(hits[k], weight, 0.0)
+    return table
+
+
+def mix_kernel(capacity, table_ref, other_ref, *refs):
+    *in_refs, own_ref, send_ref = refs
+    which = lax.broadcasted_iota(jnp.int32, table_ref.shape, 0) % (2 * capacity) // capacity
+    table = jnp.concatenate(
+        [
+            jnp.where(which == 0, table_ref[...], 0.0),
+            jnp.where(which == 1, other_ref[...], 0.0),
+        ],
+        axis=1,
+    )
     high = table.astype(BF16)
     rest = table - high.astype(F32)
     middle = rest.astype(BF16)
@@ -395,7 +400,14 @@
         lax.dot_general(term, values, (((0,), (0,)), ((), ())), preferred_element_type=F32)
         for term in (low, middle, high)
     ]
-    out_ref[...] = (terms[0] + terms[1] + terms[2]).astype(BF16)
+    mixed = terms[0] + terms[1] + terms[2]
+    rows = own_ref.shape[0]
+    own_ref[...] = mixed[:rows]
+    send_ref[...] = mixed[rows:].astype(BF16)
+
+
+def final_kernel(own_ref, other_ref, out_ref):
+    out_ref[...] = (own_ref[...] + other_ref[...].astype(F32)).astype(BF16)
 
 
 def call(kernel, name, outs, ins, operands, scratch=(), limit=4, cost=None):
@@ -432,7 +444,6 @@
     cache_lengths,
 ):
     rows, width = moe_input.shape
-    experts = router_weight.shape[1]
     capacity = rows // 2
     columns = lax.axis_size("node") // 4
     block = 2 * capacity
@@ -460,11 +471,11 @@
         cost=pl.CostEstimate(flops=10**11, bytes_accessed=64 * MIB, transcendentals=0),
     )
     blocks = [packed[0]] + [exchange(packed[k], 4 * k) for k in range(1, columns)]
-    attended, logits = call(
-        side_kernel,
+    attended, table = call(
+        functools.partial(side_kernel, capacity),
         "side",
-        (like(rows), jax.ShapeDtypeStruct((experts, rows), F32)),
-        [pl.BlockSpec(memory_space=pltpu.SMEM), WHOLE, ANY, ANY] + [WHOLE] * 5,
+        (like(rows), jax.ShapeDtypeStruct((columns * block, rows), F32)),
+        [pl.BlockSpec(memory_space=pltpu.SMEM), WHOLE, ANY, ANY] + [WHOLE] * 6,
         (
             cache_lengths,
             queries,
@@ -475,6 +486,7 @@
             moe_input,
             gain,
             router_weight.T,
+            named,
         ),
         [
             pltpu.VMEM(key_cache.shape, BF16),
@@ -488,17 +500,18 @@
         "halves",
         (like(half),) * 2,
         [WHOLE] * columns + [ANY],
-        (*blocks, logits),
+        (*blocks, table),
     )
     far_keep = exchange(keep, 1)
     across = exchange(send, 2)
+    other_table = exchange(table, 2)
     far_across = exchange(across, 1)
     slots = 2
     lines = max(4 * half, 128)
-    own0, own1, far0, far1 = call(
+    own, far = call(
         functools.partial(expert_kernel, slots),
         "expert",
-        (held(half, F32), held(half, F32), held(half), held(half)),
+        (held(2 * half, F32), held(2 * half)),
         [WHOLE] * 7 + [ANY],
         (
             *[
@@ -519,34 +532,27 @@
         ],
         limit=12,
     )
-    back0, back1 = exchange(far0, 1), exchange(far1, 1)
-    sum0, sum1 = call(
-        add_kernel,
-        "add",
-        (like(half),) * 2,
-        [WHOLE] * 4,
-        (
-            pltpu.with_memory_space_constraint(own0, pltpu.VMEM),
-            pltpu.with_memory_space_constraint(own1, pltpu.VMEM),
-            back0,
-            back1,
-        ),
-    )
-    other = exchange(sum1, 2)
-    results = call(
-        functools.partial(blocks_kernel, capacity),
-        "blocks",
+    sums = call(
+        functools.partial(merge_kernel, capacity),
+        "merge",
         (like(block),) * columns,
         [WHOLE] * 2,
-        (sum0, other),
-    )
-    results = [results[0]] + [exchange(results[k], 4 * k) for k in range(1, columns)]
+        (pltpu.with_memory_space_constraint(own, pltpu.VMEM), exchange(far, 1)),
+    )
+    results = [sums[0]] + [exchange(sums[k], 4 * k) for k in range(1, columns)]
+    mine, theirs = call(
+        functools.partial(mix_kernel, capacity),
+        "mix",
+        (held(rows, F32), like(rows)),
+        [WHOLE] * (2 + columns),
+        (table, other_table, *results),
+    )
     moe_output = call(
-        functools.partial(combine_kernel, capacity),
-        "combine",
+        final_kernel,
+        "final",
         like(rows),
-        [WHOLE] * (2 + columns),
-        (named, logits, *results),
+        [WHOLE] * 2,
+        (pltpu.with_memory_space_constraint(mine, pltpu.VMEM), exchange(theirs, 2)),
     )
     return moe_output, attended
 

time: 49.5 us -> 48.5 us (0.980)
  waiting for transfers between devices: 15.4 us -> 13.2 us
  starting transfers between devices: 13.9 us -> 15 us
    ppermute x12, waiting for transfers between devices: 15.4 us -> 13.2 us  [exchange(): return lax.ppermute(values, 'node', [(i, i ^ bits) for i in range(size)])]
    ppermute x12, starting transfers between devices: 13.9 us -> 15 us  [exchange(): return lax.ppermute(values, 'node', [(i, i ^ bits) for i in range(size)])]
  transfers between devices with their start and end apart: 12 -> 12, of which waited for: 9 -> 7; matrix products, arithmetic and copies ran while one was open for 0% -> 0% of each run, Pallas kernels for 6% -> 6%
where the time goes in v3:
time: 48.5 us; the launch traced here: 48.3 us
  Pallas kernels  19.1 us (39%)
  starting transfers between devices  15 us (31%)
  waiting for transfers between devices  13.2 us (27%)
  between operations  0.86 us (2%)
    pallas_call x7, Pallas kernels, call(): pl.pallas_call(kernel, out_shape=outs, in_specs=ins, out_specs=tuple((WHO...  19.1 us
    ppermute x12, starting transfers between devices, exchange(): return lax.ppermute(values, 'node', [(i, i ^ bits) for i in range(size)])  15 us
    ppermute x12, waiting for transfers between devices, exchange(): return lax.ppermute(values, 'node', [(i, i ^ bits) for i in range(size)])  13.2 us
  transfers between devices with their start and end apart: 12, of which 7 were waited for; matrix products, arithmetic and copies ran while one was open for 0% of the time, Pallas kernels for 6%

profile of v3, /device:TPU:0, one launch (start us, length us, event | category | flops | bytes accessed | tf_op | source)
XLA Modules:
  0.0 48.3 jit_solution(11858536318819641218)
XLA Ops:
  0.6 0.0 copy-start.2
  0.6 0.0 copy-start.3
  0.7 0.0 copy-start.4
  0.7 0.0 copy-start.5
  0.7 0.0 copy-start.6
  0.7 0.0 copy-start.7
  0.7 0.0 copy-start.8
  0.7 0.0 copy-start.9
  0.7 0.0 copy-start.10
  0.7 0.0 copy-start.11
  0.7 0.0 copy-start
  0.7 0.0 copy-start.1
  0.8 1.3 %pack.1 = (bf16[8,3072]{1,0:T(8,128)(2,1)S(1)}, bf16[8,3072]{1,0:T(8,128)(2,1)S(1)}, bf16[8,3072]{1,0:T(8,128)(2,1)S(1)}, bf16[8,3072]{1,0:T(8,128)(2,1)S(1)}) custom-call(bf16[8,3072]{1,0:T(8,128)(2,1)} %x_hbm.1, s32[2,8]{1,0:T(2,128)} %bitcast.3), custom_call_target="tpu_custom_call" | custom-call | flops 99999997952 | bytes 67108864 | tf_op jit(solution)/shard_map/pack/pallas_call | solution.py:414
  2.0 3.1 %collective-permute-start.1 = (bf16[8,3072]{1,0:T(8,128)(2,1)S(1)}, bf16[8,3072]{1,0:T(8,128)(2,1)S(1)}, u32[]{:S(2)}, u32[]{:S(2)}) collective-permute-start(bf16[8,3072]{1,0:T(8,128)(2,1)S(1)} %get-tuple-element.20), channel_id=1, source_target_pairs={{0,4},{1,5},{2,6},{3,7},{4,0},{5,1},{6,2},{7,3},{8,12},{9,13},{10,... | collective-permute-start | bytes 147464 | tf_op jit(solution)/shard_map/ppermute | solution.py:428
  5.1 2.6 %collective-permute-start.2 = (bf16[8,3072]{1,0:T(8,128)(2,1)S(1)}, bf16[8,3072]{1,0:T(8,128)(2,1)S(1)}, u32[]{:S(2)}, u32[]{:S(2)}) collective-permute-start(bf16[8,3072]{1,0:T(8,128)(2,1)S(1)} %get-tuple-element.21), channel_id=1, source_target_pairs={{0,8},{1,9},{2,10},{3,11},{4,12},{5,13},{6,14},{7,15},{8,0},{9,1},... | collective-permute-start | bytes 147464 | tf_op jit(solution)/shard_map/ppermute | solution.py:428
  7.7 0.0 collective-permute-start.3
  7.7 0.0 copy-done.2
  7.7 0.0 copy-done.3
  7.7 0.0 copy-done.4
  7.7 0.0 copy-done.5
  7.8 0.0 copy-done.6
  7.8 0.0 copy-done.7
  7.8 0.0 copy-done.8
  7.8 0.0 copy-done.9
  7.8 0.0 copy-done.10
  7.8 0.0 copy-done.11
  7.8 3.1 %side.1 = (bf16[8,3072]{1,0:T(8,128)(2,1)}, f32[32,8]{1,0:T(8,128)S(1)}) custom-call(s32[8]{0:T(128)S(1)} %copy-done.11, bf16[8,3072]{1,0:T(8,128)(2,1)S(1)} %copy-done.4, bf16[8,64,512]{2,1,0:T(8,128)(2,1)S(1)} %copy-done.2, bf16[8,64,512]{2,1,0:T(8,128)(2,1)S(1)} %copy-done.3, bf16[8,512]{1,0:T(8,128)(2,1)S(1)} %copy-done.8, bf16[8,512]{1,0:T(8,128)(2,1)S(1)} %copy-done.9, ...), custom_call_target="tpu_custom_call" | custom-call | flops 100000000 | bytes 4194304 | tf_op jit(solution)/shard_map/side/pallas_call | solution.py:414
  10.9 0.0 collective-permute-done.1.refs_1_
  10.9 0.1 collective-permute-done.2.refs_2_
  11.1 2.6 %collective-permute-done.3.refs_3_ = bf16[8,3072]{1,0:T(8,128)(2,1)S(1)} collective-permute-done((bf16[8,3072]{1,0:T(8,128)(2,1)S(1)}, bf16[8,3072]{1,0:T(8,128)(2,1)S(1)}, u32[]{:S(2)}, u32[]{:S(2)}) %collective-permute-start.3) | collective-permute-done | bytes 49184 | tf_op jit(solution)/shard_map/ppermute | solution.py:428
  13.6 0.2 halves.1
  13.8 1.6 %collective-permute-start.4 = (bf16[16,3072]{1,0:T(8,128)(2,1)S(1)}, bf16[16,3072]{1,0:T(8,128)(2,1)S(1)}, u32[]{:S(2)}, u32[]{:S(2)}) collective-permute-start(bf16[16,3072]{1,0:T(8,128)(2,1)S(1)} %get-tuple-element.24), channel_id=1, source_target_pairs={{0,2},{1,3},{2,0},{3,1},{4,6},{5,7},{6,4},{7,5},{8,10},{9,11},{10,... | collective-permute-start | bytes 294920 | tf_op jit(solution)/shard_map/ppermute | solution.py:428
  15.4 0.0 collective-permute-start.5
  15.4 3.1 %collective-permute-done.4.b_ref = bf16[16,3072]{1,0:T(8,128)(2,1)S(1)} collective-permute-done((bf16[16,3072]{1,0:T(8,128)(2,1)S(1)}, bf16[16,3072]{1,0:T(8,128)(2,1)S(1)}, u32[]{:S(2)}, u32[]{:S(2)}) %collective-permute-start.4) | collective-permute-done | bytes 98336 | tf_op jit(solution)/shard_map/ppermute | solution.py:428
  18.5 0.0 collective-permute-start.6
  18.5 0.0 collective-permute-done.5.c_ref
  18.5 1.3 %collective-permute-done.6.d_ref = bf16[16,3072]{1,0:T(8,128)(2,1)S(1)} collective-permute-done((bf16[16,3072]{1,0:T(8,128)(2,1)S(1)}, bf16[16,3072]{1,0:T(8,128)(2,1)S(1)}, u32[]{:S(2)}, u32[]{:S(2)}) %collective-permute-start.6) | collective-permute-done | bytes 98336 | tf_op jit(solution)/shard_map/ppermute | solution.py:428
  19.8 0.0 copy-done
  19.8 0.0 copy-done.1
  19.8 13.4 %expert.1 = (f32[32,3072]{1,0:T(8,128)S(1)}, bf16[32,3072]{1,0:T(8,128)(2,1)S(1)}) custom-call(bf16[16,3072]{1,0:T(8,128)(2,1)S(1)} %get-tuple-element.23.a_ref, bf16[16,3072]{1,0:T(8,128)(2,1)S(1)} %collective-permute-done.4.b_ref, bf16[16,3072]{1,0:T(8,128)(2,1)S(1)} %collective-permute-done.5.c_ref, bf16[16,3072]{1,0:T(8,128)(2,1)S(1)} %collective-permute-done.6.d_ref, ...), custom_call_target="tpu_custom_call" | custom-call | tf_op jit(solution)/shard_map/expert/pallas_call | solution.py:414
  33.2 0.2 collective-permute-start.7
  33.4 1.3 %collective-permute-done.7.far_ref = bf16[32,3072]{1,0:T(8,128)(2,1)S(1)} collective-permute-done((bf16[32,3072]{1,0:T(8,128)(2,1)S(1)}, bf16[32,3072]{1,0:T(8,128)(2,1)S(1)}, u32[]{:S(2)}, u32[]{:S(2)}) %collective-permute-start.7) | collective-permute-done | bytes 196640 | tf_op jit(solution)/shard_map/ppermute | solution.py:428
  34.7 0.2 merge.1
  34.9 1.8 %collective-permute-start.10 = (bf16[8,3072]{1,0:T(8,128)(2,1)S(1)}, bf16[8,3072]{1,0:T(8,128)(2,1)S(1)}, u32[]{:S(2)}, u32[]{:S(2)}) collective-permute-start(bf16[8,3072]{1,0:T(8,128)(2,1)S(1)} %get-tuple-element.30), channel_id=1, source_target_pairs={{0,12},{1,13},{2,14},{3,15},{4,8},{5,9},{6,10},{7,11},{8,4},{9,5},... | collective-permute-start | bytes 147464 | tf_op jit(solution)/shard_map/ppermute | solution.py:428
  36.7 0.0 collective-permute-start.8
  36.7 2.7 %collective-permute-start.9 = (bf16[8,3072]{1,0:T(8,128)(2,1)S(1)}, bf16[8,3072]{1,0:T(8,128)(2,1)S(1)}, u32[]{:S(2)}, u32[]{:S(2)}) collective-permute-start(bf16[8,3072]{1,0:T(8,128)(2,1)S(1)} %get-tuple-element.29), channel_id=1, source_target_pairs={{0,8},{1,9},{2,10},{3,11},{4,12},{5,13},{6,14},{7,15},{8,0},{9,1},... | collective-permute-start | bytes 147464 | tf_op jit(solution)/shard_map/ppermute | solution.py:428
  39.4 1.5 %collective-permute-start = (f32[32,8]{1,0:T(8,128)S(1)}, f32[32,8]{1,0:T(8,128)S(1)}, u32[]{:S(2)}, u32[]{:S(2)}) collective-permute-start(f32[32,8]{1,0:T(8,128)S(1)} %get-tuple-element.18.refs_4_.table_ref), channel_id=1, source_target_pairs={{0,2},{1,3},{2,0},{3,1},{4,6},{5,7},{6,4},{7,5},{8,10},{9,11},{10,... | collective-permute-start | bytes 3080 | tf_op jit(solution)/shard_map/ppermute | solution.py:428
  40.9 2.2 %collective-permute-done.other_ref = f32[32,8]{1,0:T(8,128)S(1)} collective-permute-done((f32[32,8]{1,0:T(8,128)S(1)}, f32[32,8]{1,0:T(8,128)S(1)}, u32[]{:S(2)}, u32[]{:S(2)}) %collective-permute-start) | collective-permute-done | bytes 1056 | tf_op jit(solution)/shard_map/ppermute | solution.py:428
  43.1 0.0 collective-permute-done.10.refs_3_
  43.1 0.0 collective-permute-done.8.refs_1_
  43.1 0.0 collective-permute-done.9.refs_2_
  43.1 0.3 mix.1
  43.5 1.6 %collective-permute-start.11 = (bf16[8,3072]{1,0:T(8,128)(2,1)S(1)}, bf16[8,3072]{1,0:T(8,128)(2,1)S(1)}, u32[]{:S(2)}, u32[]{:S(2)}) collective-permute-start(bf16[8,3072]{1,0:T(8,128)(2,1)S(1)} %get-tuple-element.32), channel_id=1, source_target_pairs={{0,2},{1,3},{2,0},{3,1},{4,6},{5,7},{6,4},{7,5},{8,10},{9,11},{10,... | collective-permute-start | bytes 147464 | tf_op jit(solution)/shard_map/ppermute | solution.py:428
  45.1 2.6 %collective-permute-done.11.other_ref = bf16[8,3072]{1,0:T(8,128)(2,1)S(1)} collective-permute-done((bf16[8,3072]{1,0:T(8,128)(2,1)S(1)}, bf16[8,3072]{1,0:T(8,128)(2,1)S(1)}, u32[]{:S(2)}, u32[]{:S(2)}) %collective-permute-start.11) | collective-permute-done | bytes 49184 | tf_op jit(solution)/shard_map/ppermute | solution.py:428
  47.6 0.6 %final.1 = bf16[8,3072]{1,0:T(8,128)(2,1)} custom-call(f32[8,3072]{1,0:T(8,128)S(1)} %get-tuple-element.31.own_ref, bf16[8,3072]{1,0:T(8,128)(2,1)S(1)} %collective-permute-done.11.other_ref), custom_call_target="tpu_custom_call" | custom-call | tf_op jit(solution)/shard_map/final/pallas_call | solution.py:414
Async XLA Ops:
  0.6 7.1 %copy-start.2 = (bf16[8,64,512]{2,1,0:T(8,128)(2,1)S(1)}, bf16[8,64,512]{2,1,0:T(8,128)(2,1)}, u32[]{:S(2)}) copy-start(bf16[8,64,512]{2,1,0:T(8,128)(2,1)} %k_hbm.1) | copy-start | bytes 1572868
  0.6 7.1 %copy-start.3 = (bf16[8,64,512]{2,1,0:T(8,128)(2,1)S(1)}, bf16[8,64,512]{2,1,0:T(8,128)(2,1)}, u32[]{:S(2)}) copy-start(bf16[8,64,512]{2,1,0:T(8,128)(2,1)} %v_hbm.1) | copy-start | bytes 1572868
  0.7 7.1 %copy-start.4 = (bf16[8,3072]{1,0:T(8,128)(2,1)S(1)}, bf16[8,3072]{1,0:T(8,128)(2,1)}, u32[]{:S(2)}) copy-start(bf16[8,3072]{1,0:T(8,128)(2,1)} %q_ref.1) | copy-start | bytes 147460
  0.7 7.1 %copy-start.5 = (bf16[8,3072]{1,0:T(8,128)(2,1)S(1)}, bf16[8,3072]{1,0:T(8,128)(2,1)}, u32[]{:S(2)}) copy-start(bf16[8,3072]{1,0:T(8,128)(2,1)} %x_hbm.1) | copy-start | bytes 147460
  0.7 7.1 %copy-start.6 = (bf16[3072,8]{0,1:T(8,128)(2,1)S(1)}, bf16[3072,8]{0,1:T(8,128)(2,1)}, u32[]{:S(2)}) copy-start(bf16[3072,8]{0,1:T(8,128)(2,1)} %param.15) | copy-start | bytes 147460
  0.7 7.1 %copy-start.7 = (bf16[3072]{0:T(1024)(128)(2,1)S(1)}, bf16[3072]{0:T(1024)(128)(2,1)}, u32[]{:S(2)}) copy-start(bf16[3072]{0:T(1024)(128)(2,1)} %gain_ref.3) | copy-start | bytes 18436
  0.7 7.1 %copy-start.8 = (bf16[8,512]{1,0:T(8,128)(2,1)S(1)}, bf16[8,512]{1,0:T(8,128)(2,1)}, u32[]{:S(2)}) copy-start(bf16[8,512]{1,0:T(8,128)(2,1)} %nk_ref.1) | copy-start | bytes 24580
  0.7 7.1 %copy-start.9 = (bf16[8,512]{1,0:T(8,128)(2,1)S(1)}, bf16[8,512]{1,0:T(8,128)(2,1)}, u32[]{:S(2)}) copy-start(bf16[8,512]{1,0:T(8,128)(2,1)} %nv_ref.1) | copy-start | bytes 24580
  0.7 7.1 %copy-start.10 = (s32[8,2]{0,1:T(2,128)S(1)}, s32[8,2]{0,1:T(2,128)}, u32[]{:S(2)}) copy-start(s32[8,2]{0,1:T(2,128)} %param.16) | copy-start | bytes 196
  0.7 7.1 %copy-start.11 = (s32[8]{0:T(128)S(1)}, s32[8]{0:T(128)}, u32[]{:S(2)}) copy-start(s32[8]{0:T(128)} %lengths_ref.1) | copy-start | bytes 100
  0.7 19.1 %copy-start = (bf16[1,3072,4096]{2,1,0:T(8,128)(2,1)S(1)}, bf16[1,3072,4096]{2,1,0:T(8,128)(2,1)}, u32[]{:S(2)}) copy-start(bf16[1,3072,4096]{2,1,0:T(8,128)(2,1)} %gate_ref.1) | copy-start | bytes 75497472
  0.7 19.1 %copy-start.1 = (bf16[1,3072,4096]{2,1,0:T(8,128)(2,1)S(1)}, bf16[1,3072,4096]{2,1,0:T(8,128)(2,1)}, u32[]{:S(2)}) copy-start(bf16[1,3072,4096]{2,1,0:T(8,128)(2,1)} %up_ref.1) | copy-start | bytes 75497472
  2.0 8.9 %collective-permute-start.1 = (bf16[8,3072]{1,0:T(8,128)(2,1)S(1)}, bf16[8,3072]{1,0:T(8,128)(2,1)S(1)}, u32[]{:S(2)}, u32[]{:S(2)}) collective-permute-start(bf16[8,3072]{1,0:T(8,128)(2,1)S(1)} %get-tuple-element.20), channel_id=1, source_target_pairs={{0,4},{1,5},{2,6},{3,7},{4,0},{5,1},{6,2},{7,3},{8,12},{9,13},{10,... | collective-permute-start | bytes 147464 | tf_op jit(solution)/shard_map/ppermute | solution.py:428
  5.1 5.9 %collective-permute-start.2 = (bf16[8,3072]{1,0:T(8,128)(2,1)S(1)}, bf16[8,3072]{1,0:T(8,128)(2,1)S(1)}, u32[]{:S(2)}, u32[]{:S(2)}) collective-permute-start(bf16[8,3072]{1,0:T(8,128)(2,1)S(1)} %get-tuple-element.21), channel_id=1, source_target_pairs={{0,8},{1,9},{2,10},{3,11},{4,12},{5,13},{6,14},{7,15},{8,0},{9,1},... | collective-permute-start | bytes 147464 | tf_op jit(solution)/shard_map/ppermute | solution.py:428
  7.7 5.9 %collective-permute-start.3 = (bf16[8,3072]{1,0:T(8,128)(2,1)S(1)}, bf16[8,3072]{1,0:T(8,128)(2,1)S(1)}, u32[]{:S(2)}, u32[]{:S(2)}) collective-permute-start(bf16[8,3072]{1,0:T(8,128)(2,1)S(1)} %get-tuple-element.22), channel_id=1, source_target_pairs={{0,12},{1,13},{2,14},{3,15},{4,8},{5,9},{6,10},{7,11},{8,4},{9,5},... | collective-permute-start | bytes 147464 | tf_op jit(solution)/shard_map/ppermute | solution.py:428
  13.8 4.7 %collective-permute-start.4 = (bf16[16,3072]{1,0:T(8,128)(2,1)S(1)}, bf16[16,3072]{1,0:T(8,128)(2,1)S(1)}, u32[]{:S(2)}, u32[]{:S(2)}) collective-permute-start(bf16[16,3072]{1,0:T(8,128)(2,1)S(1)} %get-tuple-element.24), channel_id=1, source_target_pairs={{0,2},{1,3},{2,0},{3,1},{4,6},{5,7},{6,4},{7,5},{8,10},{9,11},{10,... | collective-permute-start | bytes 294920 | tf_op jit(solution)/shard_map/ppermute | solution.py:428
  15.4 3.1 %collective-permute-start.5 = (bf16[16,3072]{1,0:T(8,128)(2,1)S(1)}, bf16[16,3072]{1,0:T(8,128)(2,1)S(1)}, u32[]{:S(2)}, u32[]{:S(2)}) collective-permute-start(bf16[16,3072]{1,0:T(8,128)(2,1)S(1)} %get-tuple-element.23.a_ref), channel_id=1, source_target_pairs={{0,1},{1,0},{2,3},{3,2},{4,5},{5,4},{6,7},{7,6},{8,9},{9,8},{10,11... | collective-permute-start | bytes 294920 | tf_op jit(solution)/shard_map/ppermute | solution.py:428
  18.5 1.3 %collective-permute-start.6 = (bf16[16,3072]{1,0:T(8,128)(2,1)S(1)}, bf16[16,3072]{1,0:T(8,128)(2,1)S(1)}, u32[]{:S(2)}, u32[]{:S(2)}) collective-permute-start(bf16[16,3072]{1,0:T(8,128)(2,1)S(1)} %collective-permute-done.4.b_ref), channel_id=1, source_target_pairs={{0,1},{1,0},{2,3},{3,2},{4,5},{5,4},{6,7},{7,6},{8,9},{9,8},{10,11... | collective-permute-start | bytes 294920 | tf_op jit(solution)/shard_map/ppermute | solution.py:428
  33.2 1.5 %collective-permute-start.7 = (bf16[32,3072]{1,0:T(8,128)(2,1)S(1)}, bf16[32,3072]{1,0:T(8,128)(2,1)S(1)}, u32[]{:S(2)}, u32[]{:S(2)}) collective-permute-start(bf16[32,3072]{1,0:T(8,128)(2,1)S(1)} %get-tuple-element.26), channel_id=1, source_target_pairs={{0,1},{1,0},{2,3},{3,2},{4,5},{5,4},{6,7},{7,6},{8,9},{9,8},{10,11... | collective-permute-start | bytes 589832 | tf_op jit(solution)/shard_map/ppermute | solution.py:428
  34.9 8.2 %collective-permute-start.10 = (bf16[8,3072]{1,0:T(8,128)(2,1)S(1)}, bf16[8,3072]{1,0:T(8,128)(2,1)S(1)}, u32[]{:S(2)}, u32[]{:S(2)}) collective-permute-start(bf16[8,3072]{1,0:T(8,128)(2,1)S(1)} %get-tuple-element.30), channel_id=1, source_target_pairs={{0,12},{1,13},{2,14},{3,15},{4,8},{5,9},{6,10},{7,11},{8,4},{9,5},... | collective-permute-start | bytes 147464 | tf_op jit(solution)/shard_map/ppermute | solution.py:428
  36.7 6.4 %collective-permute-start.8 = (bf16[8,3072]{1,0:T(8,128)(2,1)S(1)}, bf16[8,3072]{1,0:T(8,128)(2,1)S(1)}, u32[]{:S(2)}, u32[]{:S(2)}) collective-permute-start(bf16[8,3072]{1,0:T(8,128)(2,1)S(1)} %get-tuple-element.28), channel_id=1, source_target_pairs={{0,4},{1,5},{2,6},{3,7},{4,0},{5,1},{6,2},{7,3},{8,12},{9,13},{10,... | collective-permute-start | bytes 147464 | tf_op jit(solution)/shard_map/ppermute | solution.py:428
  36.7 6.4 %collective-permute-start.9 = (bf16[8,3072]{1,0:T(8,128)(2,1)S(1)}, bf16[8,3072]{1,0:T(8,128)(2,1)S(1)}, u32[]{:S(2)}, u32[]{:S(2)}) collective-permute-start(bf16[8,3072]{1,0:T(8,128)(2,1)S(1)} %get-tuple-element.29), channel_id=1, source_target_pairs={{0,8},{1,9},{2,10},{3,11},{4,12},{5,13},{6,14},{7,15},{8,0},{9,1},... | collective-permute-start | bytes 147464 | tf_op jit(solution)/shard_map/ppermute | solution.py:428
  39.4 3.7 %collective-permute-start = (f32[32,8]{1,0:T(8,128)S(1)}, f32[32,8]{1,0:T(8,128)S(1)}, u32[]{:S(2)}, u32[]{:S(2)}) collective-permute-start(f32[32,8]{1,0:T(8,128)S(1)} %get-tuple-element.18.refs_4_.table_ref), channel_id=1, source_target_pairs={{0,2},{1,3},{2,0},{3,1},{4,6},{5,7},{6,4},{7,5},{8,10},{9,11},{10,... | collective-permute-start | bytes 3080 | tf_op jit(solution)/shard_map/ppermute | solution.py:428
  43.5 4.2 %collective-permute-start.11 = (bf16[8,3072]{1,0:T(8,128)(2,1)S(1)}, bf16[8,3072]{1,0:T(8,128)(2,1)S(1)}, u32[]{:S(2)}, u32[]{:S(2)}) collective-permute-start(bf16[8,3072]{1,0:T(8,128)(2,1)S(1)} %get-tuple-element.32), channel_id=1, source_target_pairs={{0,2},{1,3},{2,0},{3,1},{4,6},{5,7},{6,4},{7,5},{8,10},{9,11},{10,... | collective-permute-start | bytes 147464 | tf_op jit(solution)/shard_map/ppermute | solution.py:428

commit v4 on v3

--- a/solution.py
+++ b/solution.py
@@ -179,6 +179,15 @@
         out_ref[...] = packed[k * block : (k + 1) * block].astype(BF16)
 
 
+def far_first(columns):
+    return sorted(range(columns), key=lambda k: (k < columns // 2, -k))
+
+
+def back_order(columns):
+    order = far_first(columns)
+    return [order[0], order[2], order[1], *order[3:]]
+
+
 def halves_kernel(capacity, *refs):
     *in_refs, _, keep_ref, send_ref = refs
     mine = (lax.axis_index("node") // 2) % 2
@@ -191,7 +200,8 @@
     within = out_line % half
     source = (within // capacity) * block + which * capacity + within % capacity
     move = jnp.where(in_line == source, 1.0, 0.0).astype(BF16)
-    values = jnp.concatenate([ref[...] for ref in in_refs], axis=0)
+    order = far_first(len(in_refs))
+    values = jnp.concatenate([in_refs[order.index(k)][...] for k in range(len(order))], axis=0)
     moved = jnp.dot(move, values, preferred_element_type=F32)
     keep_ref[...] = moved[:half].astype(BF16)
     send_ref[...] = moved[half:].astype(BF16)
@@ -395,7 +405,8 @@
     rest = table - high.astype(F32)
     middle = rest.astype(BF16)
     low = (rest - middle.astype(F32)).astype(BF16)
-    values = jnp.concatenate([ref[...] for ref in in_refs], axis=0)
+    order = back_order(len(in_refs))
+    values = jnp.concatenate([in_refs[order.index(k)][...] for k in range(len(order))], axis=0)
     terms = [
         lax.dot_general(term, values, (((0,), (0,)), ((), ())), preferred_element_type=F32)
         for term in (low, middle, high)
@@ -470,7 +481,7 @@
         ],
         cost=pl.CostEstimate(flops=10**11, bytes_accessed=64 * MIB, transcendentals=0),
     )
-    blocks = [packed[0]] + [exchange(packed[k], 4 * k) for k in range(1, columns)]
+    blocks = [exchange(packed[k], 4 * k) if k else packed[k] for k in far_first(columns)]
     attended, table = call(
         functools.partial(side_kernel, capacity),
         "side",
@@ -539,7 +550,7 @@
         [WHOLE] * 2,
         (pltpu.with_memory_space_constraint(own, pltpu.VMEM), exchange(far, 1)),
     )
-    results = [sums[0]] + [exchange(sums[k], 4 * k) for k in range(1, columns)]
+    results = [exchange(sums[k], 4 * k) if k else sums[k] for k in back_order(columns)]
     mine, theirs = call(
         functools.partial(mix_kernel, capacity),
         "mix",
@@ -561,7 +572,7 @@
     experts = arrays[2].shape[1]
     devices = lax.axis_size("node")
     units = arrays[4].shape[2]
-    if devices == 2 * experts and devices % 8 == 0 and units % TILE == 0 and arrays[0].shape[0] == 8:
+    if devices == 2 * experts and devices % 16 == 0 and units % TILE == 0 and arrays[0].shape[0] == 8:
         return paired_shards(*arrays)
     return plain_shards(*arrays)
 

time: 48.5 us -> 47 us (0.969)
  waiting for transfers between devices: 13.2 us -> 12.3 us
  starting transfers between devices: 15 us -> 14.5 us
    ppermute x12, waiting for transfers between devices: 13.2 us -> 12.3 us  [exchange(): return lax.ppermute(values, 'node', [(i, i ^ bits) for i in range(size)])]
    ppermute x12, starting transfers between devices: 15 us -> 14.5 us  [exchange(): return lax.ppermute(values, 'node', [(i, i ^ bits) for i in range(size)])]
  transfers between devices with their start and end apart: 12 -> 12, of which waited for: 7 -> 7; matrix products, arithmetic and copies ran while one was open for 0% -> 0% of each run, Pallas kernels for 6% -> 7%
where the time goes in v4:
time: 47 us; the launch traced here: 46.8 us
  Pallas kernels  19.1 us (41%)
  starting transfers between devices  14.5 us (31%)
  waiting for transfers between devices  12.3 us (26%)
  between operations  0.85 us (2%)
    pallas_call x7, Pallas kernels, call(): pl.pallas_call(kernel, out_shape=outs, in_specs=ins, out_specs=tuple((WHO...  19.1 us
    ppermute x12, starting transfers between devices, exchange(): return lax.ppermute(values, 'node', [(i, i ^ bits) for i in range(size)])  14.5 us
    ppermute x12, waiting for transfers between devices, exchange(): return lax.ppermute(values, 'node', [(i, i ^ bits) for i in range(size)])  12.3 us
  transfers between devices with their start and end apart: 12, of which 7 were waited for; matrix products, arithmetic and copies ran while one was open for 0% of the time, Pallas kernels for 7%

profile of v4, /device:TPU:0, one launch (start us, length us, event | category | flops | bytes accessed | tf_op | source)
XLA Modules:
  0.0 46.8 jit_solution(6235064017642012655)
XLA Ops:
  0.6 0.0 copy-start.2
  0.6 0.0 copy-start.3
  0.7 0.0 copy-start.4
  0.7 0.0 copy-start.5
  0.7 0.0 copy-start.6
  0.7 0.0 copy-start.7
  0.7 0.0 copy-start.8
  0.7 0.0 copy-start.9
  0.7 0.0 copy-start.10
  0.7 0.0 copy-start.11
  0.7 0.0 copy-start
  0.7 0.0 copy-start.1
  0.8 1.3 %pack.1 = (bf16[8,3072]{1,0:T(8,128)(2,1)S(1)}, bf16[8,3072]{1,0:T(8,128)(2,1)S(1)}, bf16[8,3072]{1,0:T(8,128)(2,1)S(1)}, bf16[8,3072]{1,0:T(8,128)(2,1)S(1)}) custom-call(bf16[8,3072]{1,0:T(8,128)(2,1)} %x_hbm.1, s32[2,8]{1,0:T(2,128)} %bitcast.3), custom_call_target="tpu_custom_call" | custom-call | flops 99999997952 | bytes 67108864 | tf_op jit(solution)/shard_map/pack/pallas_call | solution.py:425
  2.0 5.1 %collective-permute-start.1 = (bf16[8,3072]{1,0:T(8,128)(2,1)S(1)}, bf16[8,3072]{1,0:T(8,128)(2,1)S(1)}, u32[]{:S(2)}, u32[]{:S(2)}) collective-permute-start(bf16[8,3072]{1,0:T(8,128)(2,1)S(1)} %get-tuple-element.19), channel_id=1, source_target_pairs={{0,12},{1,13},{2,14},{3,15},{4,8},{5,9},{6,10},{7,11},{8,4},{9,5},... | collective-permute-start | bytes 147464 | tf_op jit(solution)/shard_map/ppermute | solution.py:439
  7.2 0.0 collective-permute-start.2
  7.2 0.6 %collective-permute-start.3 = (bf16[8,3072]{1,0:T(8,128)(2,1)S(1)}, bf16[8,3072]{1,0:T(8,128)(2,1)S(1)}, u32[]{:S(2)}, u32[]{:S(2)}) collective-permute-start(bf16[8,3072]{1,0:T(8,128)(2,1)S(1)} %get-tuple-element.21), channel_id=1, source_target_pairs={{0,4},{1,5},{2,6},{3,7},{4,0},{5,1},{6,2},{7,3},{8,12},{9,13},{10,... | collective-permute-start | bytes 147464 | tf_op jit(solution)/shard_map/ppermute | solution.py:439
  7.8 0.0 copy-done.2
  7.8 0.0 copy-done.3
  7.8 0.0 copy-done.4
  7.8 0.0 copy-done.5
  7.8 0.0 copy-done.6
  7.8 0.0 copy-done.7
  7.8 0.0 copy-done.8
  7.8 0.0 copy-done.9
  7.9 0.0 copy-done.10
  7.9 0.0 copy-done.11
  7.9 3.1 %side.1 = (bf16[8,3072]{1,0:T(8,128)(2,1)}, f32[32,8]{1,0:T(8,128)S(1)}) custom-call(s32[8]{0:T(128)S(1)} %copy-done.11, bf16[8,3072]{1,0:T(8,128)(2,1)S(1)} %copy-done.4, bf16[8,64,512]{2,1,0:T(8,128)(2,1)S(1)} %copy-done.2, bf16[8,64,512]{2,1,0:T(8,128)(2,1)S(1)} %copy-done.3, bf16[8,512]{1,0:T(8,128)(2,1)S(1)} %copy-done.8, bf16[8,512]{1,0:T(8,128)(2,1)S(1)} %copy-done.9, ...), custom_call_target="tpu_custom_call" | custom-call | flops 100000000 | bytes 4194304 | tf_op jit(solution)/shard_map/side/pallas_call | solution.py:425
  11.0 0.0 collective-permute-done.1.refs_0_
  11.0 1.2 %collective-permute-done.2.refs_1_ = bf16[8,3072]{1,0:T(8,128)(2,1)S(1)} collective-permute-done((bf16[8,3072]{1,0:T(8,128)(2,1)S(1)}, bf16[8,3072]{1,0:T(8,128)(2,1)S(1)}, u32[]{:S(2)}, u32[]{:S(2)}) %collective-permute-start.2) | collective-permute-done | bytes 49184 | tf_op jit(solution)/shard_map/ppermute | solution.py:439
  12.2 0.0 collective-permute-done.3.refs_2_
  12.2 0.2 halves.1
  12.4 1.6 %collective-permute-start.4 = (bf16[16,3072]{1,0:T(8,128)(2,1)S(1)}, bf16[16,3072]{1,0:T(8,128)(2,1)S(1)}, u32[]{:S(2)}, u32[]{:S(2)}) collective-permute-start(bf16[16,3072]{1,0:T(8,128)(2,1)S(1)} %get-tuple-element.24), channel_id=1, source_target_pairs={{0,2},{1,3},{2,0},{3,1},{4,6},{5,7},{6,4},{7,5},{8,10},{9,11},{10,... | collective-permute-start | bytes 294920 | tf_op jit(solution)/shard_map/ppermute | solution.py:439
  13.9 0.0 collective-permute-start.5
  13.9 3.1 %collective-permute-done.4.b_ref = bf16[16,3072]{1,0:T(8,128)(2,1)S(1)} collective-permute-done((bf16[16,3072]{1,0:T(8,128)(2,1)S(1)}, bf16[16,3072]{1,0:T(8,128)(2,1)S(1)}, u32[]{:S(2)}, u32[]{:S(2)}) %collective-permute-start.4) | collective-permute-done | bytes 98336 | tf_op jit(solution)/shard_map/ppermute | solution.py:439
  17.0 0.0 collective-permute-start.6
  17.0 0.0 collective-permute-done.5.c_ref
  17.0 1.3 %collective-permute-done.6.d_ref = bf16[16,3072]{1,0:T(8,128)(2,1)S(1)} collective-permute-done((bf16[16,3072]{1,0:T(8,128)(2,1)S(1)}, bf16[16,3072]{1,0:T(8,128)(2,1)S(1)}, u32[]{:S(2)}, u32[]{:S(2)}) %collective-permute-start.6) | collective-permute-done | bytes 98336 | tf_op jit(solution)/shard_map/ppermute | solution.py:439
  18.3 0.0 copy-done
  18.3 0.0 copy-done.1
  18.3 13.4 %expert.1 = (f32[32,3072]{1,0:T(8,128)S(1)}, bf16[32,3072]{1,0:T(8,128)(2,1)S(1)}) custom-call(bf16[16,3072]{1,0:T(8,128)(2,1)S(1)} %get-tuple-element.23.a_ref, bf16[16,3072]{1,0:T(8,128)(2,1)S(1)} %collective-permute-done.4.b_ref, bf16[16,3072]{1,0:T(8,128)(2,1)S(1)} %collective-permute-done.5.c_ref, bf16[16,3072]{1,0:T(8,128)(2,1)S(1)} %collective-permute-done.6.d_ref, ...), custom_call_target="tpu_custom_call" | custom-call | tf_op jit(solution)/shard_map/expert/pallas_call | solution.py:425
  31.8 0.2 collective-permute-start.7
  32.0 1.3 %collective-permute-done.7.far_ref = bf16[32,3072]{1,0:T(8,128)(2,1)S(1)} collective-permute-done((bf16[32,3072]{1,0:T(8,128)(2,1)S(1)}, bf16[32,3072]{1,0:T(8,128)(2,1)S(1)}, u32[]{:S(2)}, u32[]{:S(2)}) %collective-permute-start.7) | collective-permute-done | bytes 196640 | tf_op jit(solution)/shard_map/ppermute | solution.py:439
  33.3 0.2 merge.1
  33.5 2.2 %collective-permute-start.10 = (bf16[8,3072]{1,0:T(8,128)(2,1)S(1)}, bf16[8,3072]{1,0:T(8,128)(2,1)S(1)}, u32[]{:S(2)}, u32[]{:S(2)}) collective-permute-start(bf16[8,3072]{1,0:T(8,128)(2,1)S(1)} %get-tuple-element.29), channel_id=1, source_target_pairs={{0,8},{1,9},{2,10},{3,11},{4,12},{5,13},{6,14},{7,15},{8,0},{9,1},... | collective-permute-start | bytes 147464 | tf_op jit(solution)/shard_map/ppermute | solution.py:439
  35.7 1.4 %collective-permute-start.8 = (bf16[8,3072]{1,0:T(8,128)(2,1)S(1)}, bf16[8,3072]{1,0:T(8,128)(2,1)S(1)}, u32[]{:S(2)}, u32[]{:S(2)}) collective-permute-start(bf16[8,3072]{1,0:T(8,128)(2,1)S(1)} %get-tuple-element.27), channel_id=1, source_target_pairs={{0,12},{1,13},{2,14},{3,15},{4,8},{5,9},{6,10},{7,11},{8,4},{9,5},... | collective-permute-start | bytes 147464 | tf_op jit(solution)/shard_map/ppermute | solution.py:439
  37.0 0.2 collective-permute-start.9
  37.3 1.5 %collective-permute-start = (f32[32,8]{1,0:T(8,128)S(1)}, f32[32,8]{1,0:T(8,128)S(1)}, u32[]{:S(2)}, u32[]{:S(2)}) collective-permute-start(f32[32,8]{1,0:T(8,128)S(1)} %get-tuple-element.18.refs_4_.table_ref), channel_id=1, source_target_pairs={{0,2},{1,3},{2,0},{3,1},{4,6},{5,7},{6,4},{7,5},{8,10},{9,11},{10,... | collective-permute-start | bytes 3080 | tf_op jit(solution)/shard_map/ppermute | solution.py:439
  38.8 2.2 %collective-permute-done.other_ref = f32[32,8]{1,0:T(8,128)S(1)} collective-permute-done((f32[32,8]{1,0:T(8,128)S(1)}, f32[32,8]{1,0:T(8,128)S(1)}, u32[]{:S(2)}, u32[]{:S(2)}) %collective-permute-start) | collective-permute-done | bytes 1056 | tf_op jit(solution)/shard_map/ppermute | solution.py:439
  41.0 0.0 collective-permute-done.10.refs_2_
  41.0 0.6 %collective-permute-done.8.refs_0_ = bf16[8,3072]{1,0:T(8,128)(2,1)S(1)} collective-permute-done((bf16[8,3072]{1,0:T(8,128)(2,1)S(1)}, bf16[8,3072]{1,0:T(8,128)(2,1)S(1)}, u32[]{:S(2)}, u32[]{:S(2)}) %collective-permute-start.8) | collective-permute-done | bytes 49184 | tf_op jit(solution)/shard_map/ppermute | solution.py:439
  41.7 0.0 collective-permute-done.9.refs_1_
  41.7 0.3 mix.1
  42.0 1.6 %collective-permute-start.11 = (bf16[8,3072]{1,0:T(8,128)(2,1)S(1)}, bf16[8,3072]{1,0:T(8,128)(2,1)S(1)}, u32[]{:S(2)}, u32[]{:S(2)}) collective-permute-start(bf16[8,3072]{1,0:T(8,128)(2,1)S(1)} %get-tuple-element.32), channel_id=1, source_target_pairs={{0,2},{1,3},{2,0},{3,1},{4,6},{5,7},{6,4},{7,5},{8,10},{9,11},{10,... | collective-permute-start | bytes 147464 | tf_op jit(solution)/shard_map/ppermute | solution.py:439
  43.6 2.6 %collective-permute-done.11.other_ref = bf16[8,3072]{1,0:T(8,128)(2,1)S(1)} collective-permute-done((bf16[8,3072]{1,0:T(8,128)(2,1)S(1)}, bf16[8,3072]{1,0:T(8,128)(2,1)S(1)}, u32[]{:S(2)}, u32[]{:S(2)}) %collective-permute-start.11) | collective-permute-done | bytes 49184 | tf_op jit(solution)/shard_map/ppermute | solution.py:439
  46.2 0.6 %final.1 = bf16[8,3072]{1,0:T(8,128)(2,1)} custom-call(f32[8,3072]{1,0:T(8,128)S(1)} %get-tuple-element.31.own_ref, bf16[8,3072]{1,0:T(8,128)(2,1)S(1)} %collective-permute-done.11.other_ref), custom_call_target="tpu_custom_call" | custom-call | tf_op jit(solution)/shard_map/final/pallas_call | solution.py:425
Async XLA Ops:
  0.6 7.2 %copy-start.2 = (bf16[8,64,512]{2,1,0:T(8,128)(2,1)S(1)}, bf16[8,64,512]{2,1,0:T(8,128)(2,1)}, u32[]{:S(2)}) copy-start(bf16[8,64,512]{2,1,0:T(8,128)(2,1)} %k_hbm.1) | copy-start | bytes 1572868
  0.6 7.2 %copy-start.3 = (bf16[8,64,512]{2,1,0:T(8,128)(2,1)S(1)}, bf16[8,64,512]{2,1,0:T(8,128)(2,1)}, u32[]{:S(2)}) copy-start(bf16[8,64,512]{2,1,0:T(8,128)(2,1)} %v_hbm.1) | copy-start | bytes 1572868
  0.7 7.2 %copy-start.4 = (bf16[8,3072]{1,0:T(8,128)(2,1)S(1)}, bf16[8,3072]{1,0:T(8,128)(2,1)}, u32[]{:S(2)}) copy-start(bf16[8,3072]{1,0:T(8,128)(2,1)} %q_ref.1) | copy-start | bytes 147460
  0.7 7.2 %copy-start.5 = (bf16[8,3072]{1,0:T(8,128)(2,1)S(1)}, bf16[8,3072]{1,0:T(8,128)(2,1)}, u32[]{:S(2)}) copy-start(bf16[8,3072]{1,0:T(8,128)(2,1)} %x_hbm.1) | copy-start | bytes 147460
  0.7 7.1 %copy-start.6 = (bf16[3072,8]{0,1:T(8,128)(2,1)S(1)}, bf16[3072,8]{0,1:T(8,128)(2,1)}, u32[]{:S(2)}) copy-start(bf16[3072,8]{0,1:T(8,128)(2,1)} %param.15) | copy-start | bytes 147460
  0.7 7.1 %copy-start.7 = (bf16[3072]{0:T(1024)(128)(2,1)S(1)}, bf16[3072]{0:T(1024)(128)(2,1)}, u32[]{:S(2)}) copy-start(bf16[3072]{0:T(1024)(128)(2,1)} %gain_ref.3) | copy-start | bytes 18436
  0.7 7.1 %copy-start.8 = (bf16[8,512]{1,0:T(8,128)(2,1)S(1)}, bf16[8,512]{1,0:T(8,128)(2,1)}, u32[]{:S(2)}) copy-start(bf16[8,512]{1,0:T(8,128)(2,1)} %nk_ref.1) | copy-start | bytes 24580
  0.7 7.1 %copy-start.9 = (bf16[8,512]{1,0:T(8,128)(2,1)S(1)}, bf16[8,512]{1,0:T(8,128)(2,1)}, u32[]{:S(2)}) copy-start(bf16[8,512]{1,0:T(8,128)(2,1)} %nv_ref.1) | copy-start | bytes 24580
  0.7 7.1 %copy-start.10 = (s32[8,2]{0,1:T(2,128)S(1)}, s32[8,2]{0,1:T(2,128)}, u32[]{:S(2)}) copy-start(s32[8,2]{0,1:T(2,128)} %param.16) | copy-start | bytes 196
  0.7 7.1 %copy-start.11 = (s32[8]{0:T(128)S(1)}, s32[8]{0:T(128)}, u32[]{:S(2)}) copy-start(s32[8]{0:T(128)} %lengths_ref.1) | copy-start | bytes 100
  0.7 17.6 %copy-start = (bf16[1,3072,4096]{2,1,0:T(8,128)(2,1)S(1)}, bf16[1,3072,4096]{2,1,0:T(8,128)(2,1)}, u32[]{:S(2)}) copy-start(bf16[1,3072,4096]{2,1,0:T(8,128)(2,1)} %gate_ref.1) | copy-start | bytes 75497472
  0.7 17.6 %copy-start.1 = (bf16[1,3072,4096]{2,1,0:T(8,128)(2,1)S(1)}, bf16[1,3072,4096]{2,1,0:T(8,128)(2,1)}, u32[]{:S(2)}) copy-start(bf16[1,3072,4096]{2,1,0:T(8,128)(2,1)} %up_ref.1) | copy-start | bytes 75497472
  2.0 8.9 %collective-permute-start.1 = (bf16[8,3072]{1,0:T(8,128)(2,1)S(1)}, bf16[8,3072]{1,0:T(8,128)(2,1)S(1)}, u32[]{:S(2)}, u32[]{:S(2)}) collective-permute-start(bf16[8,3072]{1,0:T(8,128)(2,1)S(1)} %get-tuple-element.19), channel_id=1, source_target_pairs={{0,12},{1,13},{2,14},{3,15},{4,8},{5,9},{6,10},{7,11},{8,4},{9,5},... | collective-permute-start | bytes 147464 | tf_op jit(solution)/shard_map/ppermute | solution.py:439
  7.2 5.0 %collective-permute-start.2 = (bf16[8,3072]{1,0:T(8,128)(2,1)S(1)}, bf16[8,3072]{1,0:T(8,128)(2,1)S(1)}, u32[]{:S(2)}, u32[]{:S(2)}) collective-permute-start(bf16[8,3072]{1,0:T(8,128)(2,1)S(1)} %get-tuple-element.20), channel_id=1, source_target_pairs={{0,8},{1,9},{2,10},{3,11},{4,12},{5,13},{6,14},{7,15},{8,0},{9,1},... | collective-permute-start | bytes 147464 | tf_op jit(solution)/shard_map/ppermute | solution.py:439
  7.2 5.0 %collective-permute-start.3 = (bf16[8,3072]{1,0:T(8,128)(2,1)S(1)}, bf16[8,3072]{1,0:T(8,128)(2,1)S(1)}, u32[]{:S(2)}, u32[]{:S(2)}) collective-permute-start(bf16[8,3072]{1,0:T(8,128)(2,1)S(1)} %get-tuple-element.21), channel_id=1, source_target_pairs={{0,4},{1,5},{2,6},{3,7},{4,0},{5,1},{6,2},{7,3},{8,12},{9,13},{10,... | collective-permute-start | bytes 147464 | tf_op jit(solution)/shard_map/ppermute | solution.py:439
  12.4 4.7 %collective-permute-start.4 = (bf16[16,3072]{1,0:T(8,128)(2,1)S(1)}, bf16[16,3072]{1,0:T(8,128)(2,1)S(1)}, u32[]{:S(2)}, u32[]{:S(2)}) collective-permute-start(bf16[16,3072]{1,0:T(8,128)(2,1)S(1)} %get-tuple-element.24), channel_id=1, source_target_pairs={{0,2},{1,3},{2,0},{3,1},{4,6},{5,7},{6,4},{7,5},{8,10},{9,11},{10,... | collective-permute-start | bytes 294920 | tf_op jit(solution)/shard_map/ppermute | solution.py:439
  13.9 3.1 %collective-permute-start.5 = (bf16[16,3072]{1,0:T(8,128)(2,1)S(1)}, bf16[16,3072]{1,0:T(8,128)(2,1)S(1)}, u32[]{:S(2)}, u32[]{:S(2)}) collective-permute-start(bf16[16,3072]{1,0:T(8,128)(2,1)S(1)} %get-tuple-element.23.a_ref), channel_id=1, source_target_pairs={{0,1},{1,0},{2,3},{3,2},{4,5},{5,4},{6,7},{7,6},{8,9},{9,8},{10,11... | collective-permute-start | bytes 294920 | tf_op jit(solution)/shard_map/ppermute | solution.py:439
  17.0 1.3 %collective-permute-start.6 = (bf16[16,3072]{1,0:T(8,128)(2,1)S(1)}, bf16[16,3072]{1,0:T(8,128)(2,1)S(1)}, u32[]{:S(2)}, u32[]{:S(2)}) collective-permute-start(bf16[16,3072]{1,0:T(8,128)(2,1)S(1)} %collective-permute-done.4.b_ref), channel_id=1, source_target_pairs={{0,1},{1,0},{2,3},{3,2},{4,5},{5,4},{6,7},{7,6},{8,9},{9,8},{10,11... | collective-permute-start | bytes 294920 | tf_op jit(solution)/shard_map/ppermute | solution.py:439
  31.8 1.5 %collective-permute-start.7 = (bf16[32,3072]{1,0:T(8,128)(2,1)S(1)}, bf16[32,3072]{1,0:T(8,128)(2,1)S(1)}, u32[]{:S(2)}, u32[]{:S(2)}) collective-permute-start(bf16[32,3072]{1,0:T(8,128)(2,1)S(1)} %get-tuple-element.26), channel_id=1, source_target_pairs={{0,1},{1,0},{2,3},{3,2},{4,5},{5,4},{6,7},{7,6},{8,9},{9,8},{10,11... | collective-permute-start | bytes 589832 | tf_op jit(solution)/shard_map/ppermute | solution.py:439
  33.5 7.6 %collective-permute-start.10 = (bf16[8,3072]{1,0:T(8,128)(2,1)S(1)}, bf16[8,3072]{1,0:T(8,128)(2,1)S(1)}, u32[]{:S(2)}, u32[]{:S(2)}) collective-permute-start(bf16[8,3072]{1,0:T(8,128)(2,1)S(1)} %get-tuple-element.29), channel_id=1, source_target_pairs={{0,8},{1,9},{2,10},{3,11},{4,12},{5,13},{6,14},{7,15},{8,0},{9,1},... | collective-permute-start | bytes 147464 | tf_op jit(solution)/shard_map/ppermute | solution.py:439
  35.7 6.0 %collective-permute-start.8 = (bf16[8,3072]{1,0:T(8,128)(2,1)S(1)}, bf16[8,3072]{1,0:T(8,128)(2,1)S(1)}, u32[]{:S(2)}, u32[]{:S(2)}) collective-permute-start(bf16[8,3072]{1,0:T(8,128)(2,1)S(1)} %get-tuple-element.27), channel_id=1, source_target_pairs={{0,12},{1,13},{2,14},{3,15},{4,8},{5,9},{6,10},{7,11},{8,4},{9,5},... | collective-permute-start | bytes 147464 | tf_op jit(solution)/shard_map/ppermute | solution.py:439
  37.0 4.6 %collective-permute-start.9 = (bf16[8,3072]{1,0:T(8,128)(2,1)S(1)}, bf16[8,3072]{1,0:T(8,128)(2,1)S(1)}, u32[]{:S(2)}, u32[]{:S(2)}) collective-permute-start(bf16[8,3072]{1,0:T(8,128)(2,1)S(1)} %get-tuple-element.28), channel_id=1, source_target_pairs={{0,4},{1,5},{2,6},{3,7},{4,0},{5,1},{6,2},{7,3},{8,12},{9,13},{10,... | collective-permute-start | bytes 147464 | tf_op jit(solution)/shard_map/ppermute | solution.py:439
  37.3 3.7 %collective-permute-start = (f32[32,8]{1,0:T(8,128)S(1)}, f32[32,8]{1,0:T(8,128)S(1)}, u32[]{:S(2)}, u32[]{:S(2)}) collective-permute-start(f32[32,8]{1,0:T(8,128)S(1)} %get-tuple-element.18.refs_4_.table_ref), channel_id=1, source_target_pairs={{0,2},{1,3},{2,0},{3,1},{4,6},{5,7},{6,4},{7,5},{8,10},{9,11},{10,... | collective-permute-start | bytes 3080 | tf_op jit(solution)/shard_map/ppermute | solution.py:439
  42.0 4.2 %collective-permute-start.11 = (bf16[8,3072]{1,0:T(8,128)(2,1)S(1)}, bf16[8,3072]{1,0:T(8,128)(2,1)S(1)}, u32[]{:S(2)}, u32[]{:S(2)}) collective-permute-start(bf16[8,3072]{1,0:T(8,128)(2,1)S(1)} %get-tuple-element.32), channel_id=1, source_target_pairs={{0,2},{1,3},{2,0},{3,1},{4,6},{5,7},{6,4},{7,5},{8,10},{9,11},{10,... | collective-permute-start | bytes 147464 | tf_op jit(solution)/shard_map/ppermute | solution.py:439

commit v5 on v4

--- a/solution.py
+++ b/solution.py
@@ -267,30 +267,11 @@
             out_ref[:, head] = mixed[j * rows : (j + 1) * rows].astype(BF16)
 
 
-def side_kernel(
-    capacity,
-    lengths_ref,
-    q_ref,
-    k_hbm,
-    v_hbm,
-    nk_ref,
-    nv_ref,
-    x_ref,
-    gain_ref,
-    router_ref,
-    routes_ref,
-    out_ref,
-    table_ref,
-    k_ref,
-    v_ref,
-    sems,
-):
-    copies = [
-        pltpu.make_async_copy(k_hbm, k_ref, sems.at[0]),
-        pltpu.make_async_copy(v_hbm, v_ref, sems.at[1]),
-    ]
-    for copy in copies:
-        copy.start()
+def attend_kernel(lengths_ref, q_ref, k_ref, v_ref, nk_ref, nv_ref, _, out_ref):
+    attention(lengths_ref, q_ref, k_ref, v_ref, nk_ref, nv_ref, out_ref)
+
+
+def weigh_kernel(capacity, x_ref, gain_ref, router_ref, routes_ref, table_ref):
     logits = lax.dot_general(
         router_ref[...],
         rms(x_ref[...], gain_ref[...]),
@@ -298,9 +279,6 @@
         preferred_element_type=F32,
     )
     table_ref[...] = slot_weights(capacity, routes_ref[...], logits, table_ref.shape[0])
-    for copy in copies:
-        copy.wait()
-    attention(lengths_ref, q_ref, k_ref, v_ref, nk_ref, nv_ref, out_ref)
 
 
 def down_copy(down_ref, buf, sems, tile, slot):
@@ -417,7 +395,7 @@
     send_ref[...] = mixed[rows:].astype(BF16)
 
 
-def final_kernel(own_ref, other_ref, out_ref):
+def final_kernel(own_ref, other_ref, _, out_ref):
     out_ref[...] = (own_ref[...] + other_ref[...].astype(F32)).astype(BF16)
 
 
@@ -482,29 +460,12 @@
         cost=pl.CostEstimate(flops=10**11, bytes_accessed=64 * MIB, transcendentals=0),
     )
     blocks = [exchange(packed[k], 4 * k) if k else packed[k] for k in far_first(columns)]
-    attended, table = call(
-        functools.partial(side_kernel, capacity),
-        "side",
-        (like(rows), jax.ShapeDtypeStruct((columns * block, rows), F32)),
-        [pl.BlockSpec(memory_space=pltpu.SMEM), WHOLE, ANY, ANY] + [WHOLE] * 6,
-        (
-            cache_lengths,
-            queries,
-            key_cache,
-            value_cache,
-            new_keys,
-            new_values,
-            moe_input,
-            gain,
-            router_weight.T,
-            named,
-        ),
-        [
-            pltpu.VMEM(key_cache.shape, BF16),
-            pltpu.VMEM(value_cache.shape, BF16),
-            pltpu.SemaphoreType.DMA((2,)),
-        ],
-        cost=pl.CostEstimate(flops=10**8, bytes_accessed=4 * MIB, transcendentals=0),
+    (table,) = call(
+        functools.partial(weigh_kernel, capacity),
+        "weigh",
+        (jax.ShapeDtypeStruct((columns * block, rows), F32),),
+        [WHOLE] * 4,
+        (moe_input, gain, router_weight.T, named),
     )
     keep, send = call(
         functools.partial(halves_kernel, capacity),
@@ -558,12 +519,24 @@
         [WHOLE] * (2 + columns),
         (table, other_table, *results),
     )
+    (attended,) = call(
+        attend_kernel,
+        "attend",
+        (pltpu.HBM((rows, width), BF16),),
+        [pl.BlockSpec(memory_space=pltpu.SMEM)] + [WHOLE] * 5 + [ANY],
+        (cache_lengths, queries, key_cache, value_cache, new_keys, new_values, theirs),
+        cost=pl.CostEstimate(flops=10**8, bytes_accessed=4 * MIB, transcendentals=0),
+    )
     moe_output = call(
         final_kernel,
         "final",
         like(rows),
-        [WHOLE] * 2,
-        (pltpu.with_memory_space_constraint(mine, pltpu.VMEM), exchange(theirs, 2)),
+        [WHOLE] * 2 + [pl.BlockSpec(memory_space=pltpu.HBM)],
+        (
+            pltpu.with_memory_space_constraint(mine, pltpu.VMEM),
+            exchange(theirs, 2),
+            pltpu.with_memory_space_constraint(attended, pltpu.HBM),
+        ),
     )
     return moe_output, attended
 

time: 47 us -> 46.8 us (level)
    pallas_call x7 -> x8, Pallas kernels: 19.1 us -> 19 us  [call(): pl.pallas_call(kernel, out_shape=outs, in_specs=ins, out_specs=tuple((WHO...]
  transfers between devices with their start and end apart: 12 -> 12, of which waited for: 7 -> 7; matrix products, arithmetic and copies ran while one was open for 0% -> 0% of each run, Pallas kernels for 7% -> 6%
where the time goes in v5:
time: 46.8 us; the launch traced here: 46.6 us
  Pallas kernels  19 us (41%)
  starting transfers between devices  14.3 us (31%)
  waiting for transfers between devices  12.5 us (27%)
  between operations  0.79 us (2%)
    pallas_call x8, Pallas kernels, call(): pl.pallas_call(kernel, out_shape=outs, in_specs=ins, out_specs=tuple((WHO...  19 us
    ppermute x12, starting transfers between devices, exchange(): return lax.ppermute(values, 'node', [(i, i ^ bits) for i in range(size)])  14.3 us
    ppermute x12, waiting for transfers between devices, exchange(): return lax.ppermute(values, 'node', [(i, i ^ bits) for i in range(size)])  12.5 us
  transfers between devices with their start and end apart: 12, of which 7 were waited for; matrix products, arithmetic and copies ran while one was open for 0% of the time, Pallas kernels for 6%

profile of v5, /device:TPU:0, one launch (start us, length us, event | category | flops | bytes accessed | tf_op | source)
XLA Modules:
  0.0 46.6 jit_solution(10690667095245948801)
XLA Ops:
  0.6 0.0 copy-start.5
  0.6 0.0 copy-start.6
  0.7 0.0 copy-start.7
  0.7 0.0 copy-start.10
  0.7 0.0 copy-start
  0.7 0.0 copy-start.1
  0.7 1.3 %pack.1 = (bf16[8,3072]{1,0:T(8,128)(2,1)S(1)}, bf16[8,3072]{1,0:T(8,128)(2,1)S(1)}, bf16[8,3072]{1,0:T(8,128)(2,1)S(1)}, bf16[8,3072]{1,0:T(8,128)(2,1)S(1)}) custom-call(bf16[8,3072]{1,0:T(8,128)(2,1)} %x_hbm.1, s32[2,8]{1,0:T(2,128)} %bitcast.3), custom_call_target="tpu_custom_call" | custom-call | flops 99999997952 | bytes 67108864 | tf_op jit(solution)/shard_map/pack/pallas_call | solution.py:403
  2.0 5.1 %collective-permute-start.1 = (bf16[8,3072]{1,0:T(8,128)(2,1)S(1)}, bf16[8,3072]{1,0:T(8,128)(2,1)S(1)}, u32[]{:S(2)}, u32[]{:S(2)}) collective-permute-start(bf16[8,3072]{1,0:T(8,128)(2,1)S(1)} %get-tuple-element.16), channel_id=1, source_target_pairs={{0,12},{1,13},{2,14},{3,15},{4,8},{5,9},{6,10},{7,11},{8,4},{9,5},... | collective-permute-start | bytes 147464 | tf_op jit(solution)/shard_map/ppermute | solution.py:417
  7.1 0.0 collective-permute-start.2
  7.1 0.6 %collective-permute-start.3 = (bf16[8,3072]{1,0:T(8,128)(2,1)S(1)}, bf16[8,3072]{1,0:T(8,128)(2,1)S(1)}, u32[]{:S(2)}, u32[]{:S(2)}) collective-permute-start(bf16[8,3072]{1,0:T(8,128)(2,1)S(1)} %get-tuple-element.18), channel_id=1, source_target_pairs={{0,4},{1,5},{2,6},{3,7},{4,0},{5,1},{6,2},{7,3},{8,12},{9,13},{10,... | collective-permute-start | bytes 147464 | tf_op jit(solution)/shard_map/ppermute | solution.py:417
  7.8 0.0 copy-done.5
  7.8 0.0 copy-done.6
  7.8 0.0 copy-done.7
  7.8 0.0 copy-done.10
  7.8 0.3 weigh.1.refs_4_.table_ref
  8.1 1.3 %collective-permute-done.1.refs_0_ = bf16[8,3072]{1,0:T(8,128)(2,1)S(1)} collective-permute-done((bf16[8,3072]{1,0:T(8,128)(2,1)S(1)}, bf16[8,3072]{1,0:T(8,128)(2,1)S(1)}, u32[]{:S(2)}, u32[]{:S(2)}) %collective-permute-start.1) | collective-permute-done | bytes 49184 | tf_op jit(solution)/shard_map/ppermute | solution.py:417
  9.3 2.8 %collective-permute-done.2.refs_1_ = bf16[8,3072]{1,0:T(8,128)(2,1)S(1)} collective-permute-done((bf16[8,3072]{1,0:T(8,128)(2,1)S(1)}, bf16[8,3072]{1,0:T(8,128)(2,1)S(1)}, u32[]{:S(2)}, u32[]{:S(2)}) %collective-permute-start.2) | collective-permute-done | bytes 49184 | tf_op jit(solution)/shard_map/ppermute | solution.py:417
  12.1 0.0 collective-permute-done.3.refs_2_
  12.1 0.2 halves.1
  12.3 1.6 %collective-permute-start.4 = (bf16[16,3072]{1,0:T(8,128)(2,1)S(1)}, bf16[16,3072]{1,0:T(8,128)(2,1)S(1)}, u32[]{:S(2)}, u32[]{:S(2)}) collective-permute-start(bf16[16,3072]{1,0:T(8,128)(2,1)S(1)} %get-tuple-element.21), channel_id=1, source_target_pairs={{0,2},{1,3},{2,0},{3,1},{4,6},{5,7},{6,4},{7,5},{8,10},{9,11},{10,... | collective-permute-start | bytes 294920 | tf_op jit(solution)/shard_map/ppermute | solution.py:417
  13.9 0.0 copy-start.2
  13.9 0.0 copy-start.3
  13.9 0.0 copy-start.4
  13.9 0.0 copy-start.8
  13.9 0.0 copy-start.9
  13.9 0.0 copy-start.11
  13.9 0.1 collective-permute-start.5
  14.0 3.0 %collective-permute-done.4.b_ref = bf16[16,3072]{1,0:T(8,128)(2,1)S(1)} collective-permute-done((bf16[16,3072]{1,0:T(8,128)(2,1)S(1)}, bf16[16,3072]{1,0:T(8,128)(2,1)S(1)}, u32[]{:S(2)}, u32[]{:S(2)}) %collective-permute-start.4) | collective-permute-done | bytes 98336 | tf_op jit(solution)/shard_map/ppermute | solution.py:417
  17.0 0.0 collective-permute-start.6
  17.0 0.0 collective-permute-done.5.c_ref
  17.0 1.3 %collective-permute-done.6.d_ref = bf16[16,3072]{1,0:T(8,128)(2,1)S(1)} collective-permute-done((bf16[16,3072]{1,0:T(8,128)(2,1)S(1)}, bf16[16,3072]{1,0:T(8,128)(2,1)S(1)}, u32[]{:S(2)}, u32[]{:S(2)}) %collective-permute-start.6) | collective-permute-done | bytes 98336 | tf_op jit(solution)/shard_map/ppermute | solution.py:417
  18.3 0.0 copy-done
  18.3 0.0 copy-done.1
  18.3 13.4 %expert.1 = (f32[32,3072]{1,0:T(8,128)S(1)}, bf16[32,3072]{1,0:T(8,128)(2,1)S(1)}) custom-call(bf16[16,3072]{1,0:T(8,128)(2,1)S(1)} %get-tuple-element.20.a_ref, bf16[16,3072]{1,0:T(8,128)(2,1)S(1)} %collective-permute-done.4.b_ref, bf16[16,3072]{1,0:T(8,128)(2,1)S(1)} %collective-permute-done.5.c_ref, bf16[16,3072]{1,0:T(8,128)(2,1)S(1)} %collective-permute-done.6.d_ref, ...), custom_call_target="tpu_custom_call" | custom-call | tf_op jit(solution)/shard_map/expert/pallas_call | solution.py:403
  31.7 0.2 collective-permute-start.7
  31.9 1.3 %collective-permute-done.7.far_ref = bf16[32,3072]{1,0:T(8,128)(2,1)S(1)} collective-permute-done((bf16[32,3072]{1,0:T(8,128)(2,1)S(1)}, bf16[32,3072]{1,0:T(8,128)(2,1)S(1)}, u32[]{:S(2)}, u32[]{:S(2)}) %collective-permute-start.7) | collective-permute-done | bytes 196640 | tf_op jit(solution)/shard_map/ppermute | solution.py:417
  33.2 0.2 merge.1
  33.4 2.1 %collective-permute-start.10 = (bf16[8,3072]{1,0:T(8,128)(2,1)S(1)}, bf16[8,3072]{1,0:T(8,128)(2,1)S(1)}, u32[]{:S(2)}, u32[]{:S(2)}) collective-permute-start(bf16[8,3072]{1,0:T(8,128)(2,1)S(1)} %get-tuple-element.26), channel_id=1, source_target_pairs={{0,8},{1,9},{2,10},{3,11},{4,12},{5,13},{6,14},{7,15},{8,0},{9,1},... | collective-permute-start | bytes 147464 | tf_op jit(solution)/shard_map/ppermute | solution.py:417
  35.5 1.1 %collective-permute-start.8 = (bf16[8,3072]{1,0:T(8,128)(2,1)S(1)}, bf16[8,3072]{1,0:T(8,128)(2,1)S(1)}, u32[]{:S(2)}, u32[]{:S(2)}) collective-permute-start(bf16[8,3072]{1,0:T(8,128)(2,1)S(1)} %get-tuple-element.24), channel_id=1, source_target_pairs={{0,12},{1,13},{2,14},{3,15},{4,8},{5,9},{6,10},{7,11},{8,4},{9,5},... | collective-permute-start | bytes 147464 | tf_op jit(solution)/shard_map/ppermute | solution.py:417
  36.6 0.3 collective-permute-start.9
  37.0 1.5 %collective-permute-start = (f32[32,8]{1,0:T(8,128)S(1)}, f32[32,8]{1,0:T(8,128)S(1)}, u32[]{:S(2)}, u32[]{:S(2)}) collective-permute-start(f32[32,8]{1,0:T(8,128)S(1)} %weigh.1.refs_4_.table_ref), channel_id=1, source_target_pairs={{0,2},{1,3},{2,0},{3,1},{4,6},{5,7},{6,4},{7,5},{8,10},{9,11},{10,... | collective-permute-start | bytes 3080 | tf_op jit(solution)/shard_map/ppermute | solution.py:417
  38.5 2.2 %collective-permute-done.other_ref = f32[32,8]{1,0:T(8,128)S(1)} collective-permute-done((f32[32,8]{1,0:T(8,128)S(1)}, f32[32,8]{1,0:T(8,128)S(1)}, u32[]{:S(2)}, u32[]{:S(2)}) %collective-permute-start) | collective-permute-done | bytes 1056 | tf_op jit(solution)/shard_map/ppermute | solution.py:417
  40.7 0.0 collective-permute-done.10.refs_2_
  40.7 0.7 %collective-permute-done.8.refs_0_ = bf16[8,3072]{1,0:T(8,128)(2,1)S(1)} collective-permute-done((bf16[8,3072]{1,0:T(8,128)(2,1)S(1)}, bf16[8,3072]{1,0:T(8,128)(2,1)S(1)}, u32[]{:S(2)}, u32[]{:S(2)}) %collective-permute-start.8) | collective-permute-done | bytes 49184 | tf_op jit(solution)/shard_map/ppermute | solution.py:417
  41.4 0.0 collective-permute-done.9.refs_1_
  41.4 0.3 mix.1
  41.8 1.6 %collective-permute-start.11 = (bf16[8,3072]{1,0:T(8,128)(2,1)S(1)}, bf16[8,3072]{1,0:T(8,128)(2,1)S(1)}, u32[]{:S(2)}, u32[]{:S(2)}) collective-permute-start(bf16[8,3072]{1,0:T(8,128)(2,1)S(1)} %get-tuple-element.29._), channel_id=1, source_target_pairs={{0,2},{1,3},{2,0},{3,1},{4,6},{5,7},{6,4},{7,5},{8,10},{9,11},{10,... | collective-permute-start | bytes 147464 | tf_op jit(solution)/shard_map/ppermute | solution.py:417
  43.3 0.0 copy-done.2
  43.3 0.0 copy-done.3
  43.3 0.0 copy-done.4
  43.3 0.0 copy-done.8
  43.4 0.0 copy-done.9
  43.4 0.0 copy-done.11
  43.4 2.6 %attend.1._ = bf16[8,3072]{1,0:T(8,128)(2,1)} custom-call(s32[8]{0:T(128)S(1)} %copy-done.11, bf16[8,3072]{1,0:T(8,128)(2,1)S(1)} %copy-done.4, bf16[8,64,512]{2,1,0:T(8,128)(2,1)S(1)} %copy-done.2, bf16[8,64,512]{2,1,0:T(8,128)(2,1)S(1)} %copy-done.3, bf16[8,512]{1,0:T(8,128)(2,1)S(1)} %copy-done.8, bf16[8,512]{1,0:T(8,128)(2,1)S(1)} %copy-done.9, ...), custom_call_target="tpu_custom_call" | custom-call | flops 100000000 | bytes 4194304 | tf_op jit(solution)/shard_map/attend/pallas_call | solution.py:403
  46.0 0.0 collective-permute-done.11.other_ref
  46.0 0.6 %final.1 = bf16[8,3072]{1,0:T(8,128)(2,1)} custom-call(f32[8,3072]{1,0:T(8,128)S(1)} %get-tuple-element.28.own_ref, bf16[8,3072]{1,0:T(8,128)(2,1)S(1)} %collective-permute-done.11.other_ref, bf16[8,3072]{1,0:T(8,128)(2,1)} %attend.1._), custom_call_target="tpu_custom_call" | custom-call | tf_op jit(solution)/shard_map/final/pallas_call | solution.py:403
Async XLA Ops:
  0.6 7.1 %copy-start.5 = (bf16[8,3072]{1,0:T(8,128)(2,1)S(1)}, bf16[8,3072]{1,0:T(8,128)(2,1)}, u32[]{:S(2)}) copy-start(bf16[8,3072]{1,0:T(8,128)(2,1)} %x_hbm.1) | copy-start | bytes 147460
  0.6 7.1 %copy-start.6 = (bf16[3072,8]{0,1:T(8,128)(2,1)S(1)}, bf16[3072,8]{0,1:T(8,128)(2,1)}, u32[]{:S(2)}) copy-start(bf16[3072,8]{0,1:T(8,128)(2,1)} %param.15) | copy-start | bytes 147460
  0.7 7.1 %copy-start.7 = (bf16[3072]{0:T(1024)(128)(2,1)S(1)}, bf16[3072]{0:T(1024)(128)(2,1)}, u32[]{:S(2)}) copy-start(bf16[3072]{0:T(1024)(128)(2,1)} %gain_ref.3) | copy-start | bytes 18436
  0.7 7.1 %copy-start.10 = (s32[8,2]{0,1:T(2,128)S(1)}, s32[8,2]{0,1:T(2,128)}, u32[]{:S(2)}) copy-start(s32[8,2]{0,1:T(2,128)} %param.16) | copy-start | bytes 196
  0.7 17.6 %copy-start = (bf16[1,3072,4096]{2,1,0:T(8,128)(2,1)S(1)}, bf16[1,3072,4096]{2,1,0:T(8,128)(2,1)}, u32[]{:S(2)}) copy-start(bf16[1,3072,4096]{2,1,0:T(8,128)(2,1)} %gate_ref.1) | copy-start | bytes 75497472
  0.7 17.6 %copy-start.1 = (bf16[1,3072,4096]{2,1,0:T(8,128)(2,1)S(1)}, bf16[1,3072,4096]{2,1,0:T(8,128)(2,1)}, u32[]{:S(2)}) copy-start(bf16[1,3072,4096]{2,1,0:T(8,128)(2,1)} %up_ref.1) | copy-start | bytes 75497472
  2.0 7.3 %collective-permute-start.1 = (bf16[8,3072]{1,0:T(8,128)(2,1)S(1)}, bf16[8,3072]{1,0:T(8,128)(2,1)S(1)}, u32[]{:S(2)}, u32[]{:S(2)}) collective-permute-start(bf16[8,3072]{1,0:T(8,128)(2,1)S(1)} %get-tuple-element.16), channel_id=1, source_target_pairs={{0,12},{1,13},{2,14},{3,15},{4,8},{5,9},{6,10},{7,11},{8,4},{9,5},... | collective-permute-start | bytes 147464 | tf_op jit(solution)/shard_map/ppermute | solution.py:417
  7.1 5.0 %collective-permute-start.2 = (bf16[8,3072]{1,0:T(8,128)(2,1)S(1)}, bf16[8,3072]{1,0:T(8,128)(2,1)S(1)}, u32[]{:S(2)}, u32[]{:S(2)}) collective-permute-start(bf16[8,3072]{1,0:T(8,128)(2,1)S(1)} %get-tuple-element.17), channel_id=1, source_target_pairs={{0,8},{1,9},{2,10},{3,11},{4,12},{5,13},{6,14},{7,15},{8,0},{9,1},... | collective-permute-start | bytes 147464 | tf_op jit(solution)/shard_map/ppermute | solution.py:417
  7.1 5.0 %collective-permute-start.3 = (bf16[8,3072]{1,0:T(8,128)(2,1)S(1)}, bf16[8,3072]{1,0:T(8,128)(2,1)S(1)}, u32[]{:S(2)}, u32[]{:S(2)}) collective-permute-start(bf16[8,3072]{1,0:T(8,128)(2,1)S(1)} %get-tuple-element.18), channel_id=1, source_target_pairs={{0,4},{1,5},{2,6},{3,7},{4,0},{5,1},{6,2},{7,3},{8,12},{9,13},{10,... | collective-permute-start | bytes 147464 | tf_op jit(solution)/shard_map/ppermute | solution.py:417
  12.3 4.7 %collective-permute-start.4 = (bf16[16,3072]{1,0:T(8,128)(2,1)S(1)}, bf16[16,3072]{1,0:T(8,128)(2,1)S(1)}, u32[]{:S(2)}, u32[]{:S(2)}) collective-permute-start(bf16[16,3072]{1,0:T(8,128)(2,1)S(1)} %get-tuple-element.21), channel_id=1, source_target_pairs={{0,2},{1,3},{2,0},{3,1},{4,6},{5,7},{6,4},{7,5},{8,10},{9,11},{10,... | collective-permute-start | bytes 294920 | tf_op jit(solution)/shard_map/ppermute | solution.py:417
  13.9 29.4 %copy-start.2 = (bf16[8,64,512]{2,1,0:T(8,128)(2,1)S(1)}, bf16[8,64,512]{2,1,0:T(8,128)(2,1)}, u32[]{:S(2)}) copy-start(bf16[8,64,512]{2,1,0:T(8,128)(2,1)} %k_ref.1) | copy-start | bytes 1572868
  13.9 29.4 %copy-start.3 = (bf16[8,64,512]{2,1,0:T(8,128)(2,1)S(1)}, bf16[8,64,512]{2,1,0:T(8,128)(2,1)}, u32[]{:S(2)}) copy-start(bf16[8,64,512]{2,1,0:T(8,128)(2,1)} %v_ref.1) | copy-start | bytes 1572868
  13.9 29.4 %copy-start.4 = (bf16[8,3072]{1,0:T(8,128)(2,1)S(1)}, bf16[8,3072]{1,0:T(8,128)(2,1)}, u32[]{:S(2)}) copy-start(bf16[8,3072]{1,0:T(8,128)(2,1)} %q_ref.1) | copy-start | bytes 147460
  13.9 29.4 %copy-start.8 = (bf16[8,512]{1,0:T(8,128)(2,1)S(1)}, bf16[8,512]{1,0:T(8,128)(2,1)}, u32[]{:S(2)}) copy-start(bf16[8,512]{1,0:T(8,128)(2,1)} %nk_ref.1) | copy-start | bytes 24580
  13.9 29.4 %copy-start.9 = (bf16[8,512]{1,0:T(8,128)(2,1)S(1)}, bf16[8,512]{1,0:T(8,128)(2,1)}, u32[]{:S(2)}) copy-start(bf16[8,512]{1,0:T(8,128)(2,1)} %nv_ref.1) | copy-start | bytes 24580
  13.9 29.4 %copy-start.11 = (s32[8]{0:T(128)S(1)}, s32[8]{0:T(128)}, u32[]{:S(2)}) copy-start(s32[8]{0:T(128)} %lengths_ref.1) | copy-start | bytes 100
  13.9 3.1 %collective-permute-start.5 = (bf16[16,3072]{1,0:T(8,128)(2,1)S(1)}, bf16[16,3072]{1,0:T(8,128)(2,1)S(1)}, u32[]{:S(2)}, u32[]{:S(2)}) collective-permute-start(bf16[16,3072]{1,0:T(8,128)(2,1)S(1)} %get-tuple-element.20.a_ref), channel_id=1, source_target_pairs={{0,1},{1,0},{2,3},{3,2},{4,5},{5,4},{6,7},{7,6},{8,9},{9,8},{10,11... | collective-permute-start | bytes 294920 | tf_op jit(solution)/shard_map/ppermute | solution.py:417
  17.0 1.3 %collective-permute-start.6 = (bf16[16,3072]{1,0:T(8,128)(2,1)S(1)}, bf16[16,3072]{1,0:T(8,128)(2,1)S(1)}, u32[]{:S(2)}, u32[]{:S(2)}) collective-permute-start(bf16[16,3072]{1,0:T(8,128)(2,1)S(1)} %collective-permute-done.4.b_ref), channel_id=1, source_target_pairs={{0,1},{1,0},{2,3},{3,2},{4,5},{5,4},{6,7},{7,6},{8,9},{9,8},{10,11... | collective-permute-start | bytes 294920 | tf_op jit(solution)/shard_map/ppermute | solution.py:417
  31.7 1.5 %collective-permute-start.7 = (bf16[32,3072]{1,0:T(8,128)(2,1)S(1)}, bf16[32,3072]{1,0:T(8,128)(2,1)S(1)}, u32[]{:S(2)}, u32[]{:S(2)}) collective-permute-start(bf16[32,3072]{1,0:T(8,128)(2,1)S(1)} %get-tuple-element.23), channel_id=1, source_target_pairs={{0,1},{1,0},{2,3},{3,2},{4,5},{5,4},{6,7},{7,6},{8,9},{9,8},{10,11... | collective-permute-start | bytes 589832 | tf_op jit(solution)/shard_map/ppermute | solution.py:417
  33.4 7.3 %collective-permute-start.10 = (bf16[8,3072]{1,0:T(8,128)(2,1)S(1)}, bf16[8,3072]{1,0:T(8,128)(2,1)S(1)}, u32[]{:S(2)}, u32[]{:S(2)}) collective-permute-start(bf16[8,3072]{1,0:T(8,128)(2,1)S(1)} %get-tuple-element.26), channel_id=1, source_target_pairs={{0,8},{1,9},{2,10},{3,11},{4,12},{5,13},{6,14},{7,15},{8,0},{9,1},... | collective-permute-start | bytes 147464 | tf_op jit(solution)/shard_map/ppermute | solution.py:417
  35.5 5.9 %collective-permute-start.8 = (bf16[8,3072]{1,0:T(8,128)(2,1)S(1)}, bf16[8,3072]{1,0:T(8,128)(2,1)S(1)}, u32[]{:S(2)}, u32[]{:S(2)}) collective-permute-start(bf16[8,3072]{1,0:T(8,128)(2,1)S(1)} %get-tuple-element.24), channel_id=1, source_target_pairs={{0,12},{1,13},{2,14},{3,15},{4,8},{5,9},{6,10},{7,11},{8,4},{9,5},... | collective-permute-start | bytes 147464 | tf_op jit(solution)/shard_map/ppermute | solution.py:417
  36.6 4.8 %collective-permute-start.9 = (bf16[8,3072]{1,0:T(8,128)(2,1)S(1)}, bf16[8,3072]{1,0:T(8,128)(2,1)S(1)}, u32[]{:S(2)}, u32[]{:S(2)}) collective-permute-start(bf16[8,3072]{1,0:T(8,128)(2,1)S(1)} %get-tuple-element.25), channel_id=1, source_target_pairs={{0,4},{1,5},{2,6},{3,7},{4,0},{5,1},{6,2},{7,3},{8,12},{9,13},{10,... | collective-permute-start | bytes 147464 | tf_op jit(solution)/shard_map/ppermute | solution.py:417
  37.0 3.7 %collective-permute-start = (f32[32,8]{1,0:T(8,128)S(1)}, f32[32,8]{1,0:T(8,128)S(1)}, u32[]{:S(2)}, u32[]{:S(2)}) collective-permute-start(f32[32,8]{1,0:T(8,128)S(1)} %weigh.1.refs_4_.table_ref), channel_id=1, source_target_pairs={{0,2},{1,3},{2,0},{3,1},{4,6},{5,7},{6,4},{7,5},{8,10},{9,11},{10,... | collective-permute-start | bytes 3080 | tf_op jit(solution)/shard_map/ppermute | solution.py:417
  41.8 4.3 %collective-permute-start.11 = (bf16[8,3072]{1,0:T(8,128)(2,1)S(1)}, bf16[8,3072]{1,0:T(8,128)(2,1)S(1)}, u32[]{:S(2)}, u32[]{:S(2)}) collective-permute-start(bf16[8,3072]{1,0:T(8,128)(2,1)S(1)} %get-tuple-element.29._), channel_id=1, source_target_pairs={{0,2},{1,3},{2,0},{3,1},{4,6},{5,7},{6,4},{7,5},{8,10},{9,11},{10,... | collective-permute-start | bytes 147464 | tf_op jit(solution)/shard_map/ppermute | solution.py:417

commit v6 on v5

--- a/solution.py
+++ b/solution.py
@@ -302,7 +302,6 @@
     own_ref,
     far_ref,
     x_buf,
-    hidden,
     total,
     down_buf,
     sems,
@@ -315,36 +314,24 @@
     for i, ref in enumerate((a_ref, b_ref, c_ref, d_ref)):
         x_buf[i * part : (i + 1) * part, :] = rms(ref[...], gain_ref[...])
     x_buf[lines:, :] = jnp.zeros_like(x_buf[lines:, :])
-    total[...] = jnp.zeros_like(total)
 
     def activate(tile):
-        cols = pl.ds(pl.multiple_of(tile * TILE, TILE), TILE)
+        cols = slice(tile * TILE, (tile + 1) * TILE)
         x = x_buf[...]
         gated = jnp.dot(x, gate_ref[0, :, cols], preferred_element_type=F32)
         upper = jnp.dot(x, up_ref[0, :, cols], preferred_element_type=F32)
         return (gated / (1.0 + jnp.exp(-gated)) * upper).astype(BF16)
 
-    def project(tile):
-        slot = lax.rem(tile, slots)
-        down_copy(down_ref, down_buf, sems, tile, slot).wait()
-        return jnp.dot(hidden[lax.rem(tile, 2)], down_buf[slot], preferred_element_type=F32)
-
-    def refill(tile):
-        @pl.when(tile + slots < tiles)
-        def _():
-            down_copy(down_ref, down_buf, sems, tile + slots, lax.rem(tile, slots)).start()
-
-    hidden[0] = activate(0)
-
-    def step(tile, carry):
-        product = project(tile - 1)
-        hidden[lax.rem(tile, 2)] = activate(tile)
-        total[...] += product[:lines]
-        refill(tile - 1)
-        return carry
-
-    lax.fori_loop(1, tiles, step, 0)
-    result = total[...] + project(tiles - 1)[:lines]
+    ready = activate(0)
+    for tile in range(tiles):
+        down_copy(down_ref, down_buf, sems, tile, tile % slots).wait()
+        product = jnp.dot(ready, down_buf[tile % slots], preferred_element_type=F32)[:lines]
+        if tile + 1 < tiles:
+            ready = activate(tile + 1)
+            total[...] = product if tile == 0 else total[...] + product
+        if tile + slots < tiles:
+            down_copy(down_ref, down_buf, sems, tile + slots, tile % slots).start()
+    result = total[...] + product if tiles > 1 else product
     own_ref[...] = result[: 2 * part]
     far_ref[...] = result[2 * part :].astype(BF16)
 
@@ -497,7 +484,6 @@
         ),
         [
             pltpu.VMEM((lines, width), BF16),
-            pltpu.VMEM((2, lines, TILE), BF16),
             pltpu.VMEM((4 * half, width), F32),
             pltpu.VMEM((slots, TILE, width), BF16),
             pltpu.SemaphoreType.DMA((slots,)),

time: 46.8 us -> 46.4 us (level)
  no operation moved by 1% of the time
where the time goes in v6:
time: 46.4 us; the launch traced here: 46.2 us
  Pallas kernels  18.6 us (40%)
  starting transfers between devices  14.3 us (31%)
  waiting for transfers between devices  12.5 us (27%)
  between operations  0.79 us (2%)
    pallas_call x8, Pallas kernels, call(): pl.pallas_call(kernel, out_shape=outs, in_specs=ins, out_specs=tuple((WHO...  18.6 us
    ppermute x12, starting transfers between devices, exchange(): return lax.ppermute(values, 'node', [(i, i ^ bits) for i in range(size)])  14.3 us
    ppermute x12, waiting for transfers between devices, exchange(): return lax.ppermute(values, 'node', [(i, i ^ bits) for i in range(size)])  12.5 us
  transfers between devices with their start and end apart: 12, of which 7 were waited for; matrix products, arithmetic and copies ran while one was open for 0% of the time, Pallas kernels for 6%

profile of v6, /device:TPU:0, one launch (start us, length us, event | category | flops | bytes accessed | tf_op | source)
XLA Modules:
  0.0 46.2 jit_solution(7757785843389857681)
XLA Ops:
  0.6 0.0 copy-start.5
  0.6 0.0 copy-start.6
  0.7 0.0 copy-start.7
  0.7 0.0 copy-start.10
  0.7 0.0 copy-start
  0.7 0.0 copy-start.1
  0.7 1.3 %pack.1 = (bf16[8,3072]{1,0:T(8,128)(2,1)S(1)}, bf16[8,3072]{1,0:T(8,128)(2,1)S(1)}, bf16[8,3072]{1,0:T(8,128)(2,1)S(1)}, bf16[8,3072]{1,0:T(8,128)(2,1)S(1)}) custom-call(bf16[8,3072]{1,0:T(8,128)(2,1)} %x_hbm.1, s32[2,8]{1,0:T(2,128)} %bitcast.3), custom_call_target="tpu_custom_call" | custom-call | flops 99999997952 | bytes 67108864 | tf_op jit(solution)/shard_map/pack/pallas_call | solution.py:390
  2.0 5.1 %collective-permute-start.1 = (bf16[8,3072]{1,0:T(8,128)(2,1)S(1)}, bf16[8,3072]{1,0:T(8,128)(2,1)S(1)}, u32[]{:S(2)}, u32[]{:S(2)}) collective-permute-start(bf16[8,3072]{1,0:T(8,128)(2,1)S(1)} %get-tuple-element.16), channel_id=1, source_target_pairs={{0,12},{1,13},{2,14},{3,15},{4,8},{5,9},{6,10},{7,11},{8,4},{9,5},... | collective-permute-start | bytes 147464 | tf_op jit(solution)/shard_map/ppermute | solution.py:404
  7.1 0.0 collective-permute-start.2
  7.1 0.6 %collective-permute-start.3 = (bf16[8,3072]{1,0:T(8,128)(2,1)S(1)}, bf16[8,3072]{1,0:T(8,128)(2,1)S(1)}, u32[]{:S(2)}, u32[]{:S(2)}) collective-permute-start(bf16[8,3072]{1,0:T(8,128)(2,1)S(1)} %get-tuple-element.18), channel_id=1, source_target_pairs={{0,4},{1,5},{2,6},{3,7},{4,0},{5,1},{6,2},{7,3},{8,12},{9,13},{10,... | collective-permute-start | bytes 147464 | tf_op jit(solution)/shard_map/ppermute | solution.py:404
  7.8 0.0 copy-done.5
  7.8 0.0 copy-done.6
  7.8 0.0 copy-done.7
  7.8 0.0 copy-done.10
  7.8 0.3 weigh.1.refs_4_.table_ref
  8.1 1.3 %collective-permute-done.1.refs_0_ = bf16[8,3072]{1,0:T(8,128)(2,1)S(1)} collective-permute-done((bf16[8,3072]{1,0:T(8,128)(2,1)S(1)}, bf16[8,3072]{1,0:T(8,128)(2,1)S(1)}, u32[]{:S(2)}, u32[]{:S(2)}) %collective-permute-start.1) | collective-permute-done | bytes 49184 | tf_op jit(solution)/shard_map/ppermute | solution.py:404
  9.3 2.8 %collective-permute-done.2.refs_1_ = bf16[8,3072]{1,0:T(8,128)(2,1)S(1)} collective-permute-done((bf16[8,3072]{1,0:T(8,128)(2,1)S(1)}, bf16[8,3072]{1,0:T(8,128)(2,1)S(1)}, u32[]{:S(2)}, u32[]{:S(2)}) %collective-permute-start.2) | collective-permute-done | bytes 49184 | tf_op jit(solution)/shard_map/ppermute | solution.py:404
  12.1 0.0 collective-permute-done.3.refs_2_
  12.1 0.2 halves.1
  12.3 1.6 %collective-permute-start.4 = (bf16[16,3072]{1,0:T(8,128)(2,1)S(1)}, bf16[16,3072]{1,0:T(8,128)(2,1)S(1)}, u32[]{:S(2)}, u32[]{:S(2)}) collective-permute-start(bf16[16,3072]{1,0:T(8,128)(2,1)S(1)} %get-tuple-element.21), channel_id=1, source_target_pairs={{0,2},{1,3},{2,0},{3,1},{4,6},{5,7},{6,4},{7,5},{8,10},{9,11},{10,... | collective-permute-start | bytes 294920 | tf_op jit(solution)/shard_map/ppermute | solution.py:404
  13.9 0.0 copy-start.2
  13.9 0.0 copy-start.3
  13.9 0.0 copy-start.4
  13.9 0.0 copy-start.8
  13.9 0.0 copy-start.9
  13.9 0.0 copy-start.11
  13.9 0.1 collective-permute-start.5
  14.0 3.0 %collective-permute-done.4.b_ref = bf16[16,3072]{1,0:T(8,128)(2,1)S(1)} collective-permute-done((bf16[16,3072]{1,0:T(8,128)(2,1)S(1)}, bf16[16,3072]{1,0:T(8,128)(2,1)S(1)}, u32[]{:S(2)}, u32[]{:S(2)}) %collective-permute-start.4) | collective-permute-done | bytes 98336 | tf_op jit(solution)/shard_map/ppermute | solution.py:404
  17.0 0.0 collective-permute-start.6
  17.0 0.0 collective-permute-done.5.c_ref
  17.0 1.3 %collective-permute-done.6.d_ref = bf16[16,3072]{1,0:T(8,128)(2,1)S(1)} collective-permute-done((bf16[16,3072]{1,0:T(8,128)(2,1)S(1)}, bf16[16,3072]{1,0:T(8,128)(2,1)S(1)}, u32[]{:S(2)}, u32[]{:S(2)}) %collective-permute-start.6) | collective-permute-done | bytes 98336 | tf_op jit(solution)/shard_map/ppermute | solution.py:404
  18.3 0.0 copy-done
  18.3 0.0 copy-done.1
  18.3 13.0 %expert.1 = (f32[32,3072]{1,0:T(8,128)S(1)}, bf16[32,3072]{1,0:T(8,128)(2,1)S(1)}) custom-call(bf16[16,3072]{1,0:T(8,128)(2,1)S(1)} %get-tuple-element.20.a_ref, bf16[16,3072]{1,0:T(8,128)(2,1)S(1)} %collective-permute-done.4.b_ref, bf16[16,3072]{1,0:T(8,128)(2,1)S(1)} %collective-permute-done.5.c_ref, bf16[16,3072]{1,0:T(8,128)(2,1)S(1)} %collective-permute-done.6.d_ref, ...), custom_call_target="tpu_custom_call" | custom-call | tf_op jit(solution)/shard_map/expert/pallas_call | solution.py:390
  31.3 0.2 collective-permute-start.7
  31.5 1.3 %collective-permute-done.7.far_ref = bf16[32,3072]{1,0:T(8,128)(2,1)S(1)} collective-permute-done((bf16[32,3072]{1,0:T(8,128)(2,1)S(1)}, bf16[32,3072]{1,0:T(8,128)(2,1)S(1)}, u32[]{:S(2)}, u32[]{:S(2)}) %collective-permute-start.7) | collective-permute-done | bytes 196640 | tf_op jit(solution)/shard_map/ppermute | solution.py:404
  32.8 0.2 merge.1
  33.0 2.1 %collective-permute-start.10 = (bf16[8,3072]{1,0:T(8,128)(2,1)S(1)}, bf16[8,3072]{1,0:T(8,128)(2,1)S(1)}, u32[]{:S(2)}, u32[]{:S(2)}) collective-permute-start(bf16[8,3072]{1,0:T(8,128)(2,1)S(1)} %get-tuple-element.26), channel_id=1, source_target_pairs={{0,8},{1,9},{2,10},{3,11},{4,12},{5,13},{6,14},{7,15},{8,0},{9,1},... | collective-permute-start | bytes 147464 | tf_op jit(solution)/shard_map/ppermute | solution.py:404
  35.1 1.1 %collective-permute-start.8 = (bf16[8,3072]{1,0:T(8,128)(2,1)S(1)}, bf16[8,3072]{1,0:T(8,128)(2,1)S(1)}, u32[]{:S(2)}, u32[]{:S(2)}) collective-permute-start(bf16[8,3072]{1,0:T(8,128)(2,1)S(1)} %get-tuple-element.24), channel_id=1, source_target_pairs={{0,12},{1,13},{2,14},{3,15},{4,8},{5,9},{6,10},{7,11},{8,4},{9,5},... | collective-permute-start | bytes 147464 | tf_op jit(solution)/shard_map/ppermute | solution.py:404
  36.2 0.3 collective-permute-start.9
  36.6 1.5 %collective-permute-start = (f32[32,8]{1,0:T(8,128)S(1)}, f32[32,8]{1,0:T(8,128)S(1)}, u32[]{:S(2)}, u32[]{:S(2)}) collective-permute-start(f32[32,8]{1,0:T(8,128)S(1)} %weigh.1.refs_4_.table_ref), channel_id=1, source_target_pairs={{0,2},{1,3},{2,0},{3,1},{4,6},{5,7},{6,4},{7,5},{8,10},{9,11},{10,... | collective-permute-start | bytes 3080 | tf_op jit(solution)/shard_map/ppermute | solution.py:404
  38.1 2.2 %collective-permute-done.other_ref = f32[32,8]{1,0:T(8,128)S(1)} collective-permute-done((f32[32,8]{1,0:T(8,128)S(1)}, f32[32,8]{1,0:T(8,128)S(1)}, u32[]{:S(2)}, u32[]{:S(2)}) %collective-permute-start) | collective-permute-done | bytes 1056 | tf_op jit(solution)/shard_map/ppermute | solution.py:404
  40.3 0.0 collective-permute-done.10.refs_2_
  40.3 0.7 %collective-permute-done.8.refs_0_ = bf16[8,3072]{1,0:T(8,128)(2,1)S(1)} collective-permute-done((bf16[8,3072]{1,0:T(8,128)(2,1)S(1)}, bf16[8,3072]{1,0:T(8,128)(2,1)S(1)}, u32[]{:S(2)}, u32[]{:S(2)}) %collective-permute-start.8) | collective-permute-done | bytes 49184 | tf_op jit(solution)/shard_map/ppermute | solution.py:404
  41.0 0.0 collective-permute-done.9.refs_1_
  41.0 0.3 mix.1
  41.3 1.6 %collective-permute-start.11 = (bf16[8,3072]{1,0:T(8,128)(2,1)S(1)}, bf16[8,3072]{1,0:T(8,128)(2,1)S(1)}, u32[]{:S(2)}, u32[]{:S(2)}) collective-permute-start(bf16[8,3072]{1,0:T(8,128)(2,1)S(1)} %get-tuple-element.29._), channel_id=1, source_target_pairs={{0,2},{1,3},{2,0},{3,1},{4,6},{5,7},{6,4},{7,5},{8,10},{9,11},{10,... | collective-permute-start | bytes 147464 | tf_op jit(solution)/shard_map/ppermute | solution.py:404
  42.9 0.0 copy-done.2
  42.9 0.0 copy-done.3
  42.9 0.0 copy-done.4
  42.9 0.0 copy-done.8
  42.9 0.0 copy-done.9
  43.0 0.0 copy-done.11
  43.0 2.6 %attend.1._ = bf16[8,3072]{1,0:T(8,128)(2,1)} custom-call(s32[8]{0:T(128)S(1)} %copy-done.11, bf16[8,3072]{1,0:T(8,128)(2,1)S(1)} %copy-done.4, bf16[8,64,512]{2,1,0:T(8,128)(2,1)S(1)} %copy-done.2, bf16[8,64,512]{2,1,0:T(8,128)(2,1)S(1)} %copy-done.3, bf16[8,512]{1,0:T(8,128)(2,1)S(1)} %copy-done.8, bf16[8,512]{1,0:T(8,128)(2,1)S(1)} %copy-done.9, ...), custom_call_target="tpu_custom_call" | custom-call | flops 100000000 | bytes 4194304 | tf_op jit(solution)/shard_map/attend/pallas_call | solution.py:390
  45.6 0.0 collective-permute-done.11.other_ref
  45.6 0.6 %final.1 = bf16[8,3072]{1,0:T(8,128)(2,1)} custom-call(f32[8,3072]{1,0:T(8,128)S(1)} %get-tuple-element.28.own_ref, bf16[8,3072]{1,0:T(8,128)(2,1)S(1)} %collective-permute-done.11.other_ref, bf16[8,3072]{1,0:T(8,128)(2,1)} %attend.1._), custom_call_target="tpu_custom_call" | custom-call | tf_op jit(solution)/shard_map/final/pallas_call | solution.py:390
Async XLA Ops:
  0.6 7.1 %copy-start.5 = (bf16[8,3072]{1,0:T(8,128)(2,1)S(1)}, bf16[8,3072]{1,0:T(8,128)(2,1)}, u32[]{:S(2)}) copy-start(bf16[8,3072]{1,0:T(8,128)(2,1)} %x_hbm.1) | copy-start | bytes 147460
  0.6 7.1 %copy-start.6 = (bf16[3072,8]{0,1:T(8,128)(2,1)S(1)}, bf16[3072,8]{0,1:T(8,128)(2,1)}, u32[]{:S(2)}) copy-start(bf16[3072,8]{0,1:T(8,128)(2,1)} %param.15) | copy-start | bytes 147460
  0.7 7.1 %copy-start.7 = (bf16[3072]{0:T(1024)(128)(2,1)S(1)}, bf16[3072]{0:T(1024)(128)(2,1)}, u32[]{:S(2)}) copy-start(bf16[3072]{0:T(1024)(128)(2,1)} %gain_ref.3) | copy-start | bytes 18436
  0.7 7.1 %copy-start.10 = (s32[8,2]{0,1:T(2,128)S(1)}, s32[8,2]{0,1:T(2,128)}, u32[]{:S(2)}) copy-start(s32[8,2]{0,1:T(2,128)} %param.16) | copy-start | bytes 196
  0.7 17.6 %copy-start = (bf16[1,3072,4096]{2,1,0:T(8,128)(2,1)S(1)}, bf16[1,3072,4096]{2,1,0:T(8,128)(2,1)}, u32[]{:S(2)}) copy-start(bf16[1,3072,4096]{2,1,0:T(8,128)(2,1)} %gate_ref.1) | copy-start | bytes 75497472
  0.7 17.6 %copy-start.1 = (bf16[1,3072,4096]{2,1,0:T(8,128)(2,1)S(1)}, bf16[1,3072,4096]{2,1,0:T(8,128)(2,1)}, u32[]{:S(2)}) copy-start(bf16[1,3072,4096]{2,1,0:T(8,128)(2,1)} %up_ref.1) | copy-start | bytes 75497472
  2.0 7.3 %collective-permute-start.1 = (bf16[8,3072]{1,0:T(8,128)(2,1)S(1)}, bf16[8,3072]{1,0:T(8,128)(2,1)S(1)}, u32[]{:S(2)}, u32[]{:S(2)}) collective-permute-start(bf16[8,3072]{1,0:T(8,128)(2,1)S(1)} %get-tuple-element.16), channel_id=1, source_target_pairs={{0,12},{1,13},{2,14},{3,15},{4,8},{5,9},{6,10},{7,11},{8,4},{9,5},... | collective-permute-start | bytes 147464 | tf_op jit(solution)/shard_map/ppermute | solution.py:404
  7.1 5.0 %collective-permute-start.2 = (bf16[8,3072]{1,0:T(8,128)(2,1)S(1)}, bf16[8,3072]{1,0:T(8,128)(2,1)S(1)}, u32[]{:S(2)}, u32[]{:S(2)}) collective-permute-start(bf16[8,3072]{1,0:T(8,128)(2,1)S(1)} %get-tuple-element.17), channel_id=1, source_target_pairs={{0,8},{1,9},{2,10},{3,11},{4,12},{5,13},{6,14},{7,15},{8,0},{9,1},... | collective-permute-start | bytes 147464 | tf_op jit(solution)/shard_map/ppermute | solution.py:404
  7.1 5.0 %collective-permute-start.3 = (bf16[8,3072]{1,0:T(8,128)(2,1)S(1)}, bf16[8,3072]{1,0:T(8,128)(2,1)S(1)}, u32[]{:S(2)}, u32[]{:S(2)}) collective-permute-start(bf16[8,3072]{1,0:T(8,128)(2,1)S(1)} %get-tuple-element.18), channel_id=1, source_target_pairs={{0,4},{1,5},{2,6},{3,7},{4,0},{5,1},{6,2},{7,3},{8,12},{9,13},{10,... | collective-permute-start | bytes 147464 | tf_op jit(solution)/shard_map/ppermute | solution.py:404
  12.3 4.7 %collective-permute-start.4 = (bf16[16,3072]{1,0:T(8,128)(2,1)S(1)}, bf16[16,3072]{1,0:T(8,128)(2,1)S(1)}, u32[]{:S(2)}, u32[]{:S(2)}) collective-permute-start(bf16[16,3072]{1,0:T(8,128)(2,1)S(1)} %get-tuple-element.21), channel_id=1, source_target_pairs={{0,2},{1,3},{2,0},{3,1},{4,6},{5,7},{6,4},{7,5},{8,10},{9,11},{10,... | collective-permute-start | bytes 294920 | tf_op jit(solution)/shard_map/ppermute | solution.py:404
  13.9 29.0 %copy-start.2 = (bf16[8,64,512]{2,1,0:T(8,128)(2,1)S(1)}, bf16[8,64,512]{2,1,0:T(8,128)(2,1)}, u32[]{:S(2)}) copy-start(bf16[8,64,512]{2,1,0:T(8,128)(2,1)} %k_ref.1) | copy-start | bytes 1572868
  13.9 29.0 %copy-start.3 = (bf16[8,64,512]{2,1,0:T(8,128)(2,1)S(1)}, bf16[8,64,512]{2,1,0:T(8,128)(2,1)}, u32[]{:S(2)}) copy-start(bf16[8,64,512]{2,1,0:T(8,128)(2,1)} %v_ref.1) | copy-start | bytes 1572868
  13.9 29.0 %copy-start.4 = (bf16[8,3072]{1,0:T(8,128)(2,1)S(1)}, bf16[8,3072]{1,0:T(8,128)(2,1)}, u32[]{:S(2)}) copy-start(bf16[8,3072]{1,0:T(8,128)(2,1)} %q_ref.1) | copy-start | bytes 147460
  13.9 29.0 %copy-start.8 = (bf16[8,512]{1,0:T(8,128)(2,1)S(1)}, bf16[8,512]{1,0:T(8,128)(2,1)}, u32[]{:S(2)}) copy-start(bf16[8,512]{1,0:T(8,128)(2,1)} %nk_ref.1) | copy-start | bytes 24580
  13.9 29.0 %copy-start.9 = (bf16[8,512]{1,0:T(8,128)(2,1)S(1)}, bf16[8,512]{1,0:T(8,128)(2,1)}, u32[]{:S(2)}) copy-start(bf16[8,512]{1,0:T(8,128)(2,1)} %nv_ref.1) | copy-start | bytes 24580
  13.9 29.0 %copy-start.11 = (s32[8]{0:T(128)S(1)}, s32[8]{0:T(128)}, u32[]{:S(2)}) copy-start(s32[8]{0:T(128)} %lengths_ref.1) | copy-start | bytes 100
  13.9 3.1 %collective-permute-start.5 = (bf16[16,3072]{1,0:T(8,128)(2,1)S(1)}, bf16[16,3072]{1,0:T(8,128)(2,1)S(1)}, u32[]{:S(2)}, u32[]{:S(2)}) collective-permute-start(bf16[16,3072]{1,0:T(8,128)(2,1)S(1)} %get-tuple-element.20.a_ref), channel_id=1, source_target_pairs={{0,1},{1,0},{2,3},{3,2},{4,5},{5,4},{6,7},{7,6},{8,9},{9,8},{10,11... | collective-permute-start | bytes 294920 | tf_op jit(solution)/shard_map/ppermute | solution.py:404
  17.0 1.3 %collective-permute-start.6 = (bf16[16,3072]{1,0:T(8,128)(2,1)S(1)}, bf16[16,3072]{1,0:T(8,128)(2,1)S(1)}, u32[]{:S(2)}, u32[]{:S(2)}) collective-permute-start(bf16[16,3072]{1,0:T(8,128)(2,1)S(1)} %collective-permute-done.4.b_ref), channel_id=1, source_target_pairs={{0,1},{1,0},{2,3},{3,2},{4,5},{5,4},{6,7},{7,6},{8,9},{9,8},{10,11... | collective-permute-start | bytes 294920 | tf_op jit(solution)/shard_map/ppermute | solution.py:404
  31.3 1.5 %collective-permute-start.7 = (bf16[32,3072]{1,0:T(8,128)(2,1)S(1)}, bf16[32,3072]{1,0:T(8,128)(2,1)S(1)}, u32[]{:S(2)}, u32[]{:S(2)}) collective-permute-start(bf16[32,3072]{1,0:T(8,128)(2,1)S(1)} %get-tuple-element.23), channel_id=1, source_target_pairs={{0,1},{1,0},{2,3},{3,2},{4,5},{5,4},{6,7},{7,6},{8,9},{9,8},{10,11... | collective-permute-start | bytes 589832 | tf_op jit(solution)/shard_map/ppermute | solution.py:404
  33.0 7.3 %collective-permute-start.10 = (bf16[8,3072]{1,0:T(8,128)(2,1)S(1)}, bf16[8,3072]{1,0:T(8,128)(2,1)S(1)}, u32[]{:S(2)}, u32[]{:S(2)}) collective-permute-start(bf16[8,3072]{1,0:T(8,128)(2,1)S(1)} %get-tuple-element.26), channel_id=1, source_target_pairs={{0,8},{1,9},{2,10},{3,11},{4,12},{5,13},{6,14},{7,15},{8,0},{9,1},... | collective-permute-start | bytes 147464 | tf_op jit(solution)/shard_map/ppermute | solution.py:404
  35.1 5.9 %collective-permute-start.8 = (bf16[8,3072]{1,0:T(8,128)(2,1)S(1)}, bf16[8,3072]{1,0:T(8,128)(2,1)S(1)}, u32[]{:S(2)}, u32[]{:S(2)}) collective-permute-start(bf16[8,3072]{1,0:T(8,128)(2,1)S(1)} %get-tuple-element.24), channel_id=1, source_target_pairs={{0,12},{1,13},{2,14},{3,15},{4,8},{5,9},{6,10},{7,11},{8,4},{9,5},... | collective-permute-start | bytes 147464 | tf_op jit(solution)/shard_map/ppermute | solution.py:404
  36.2 4.8 %collective-permute-start.9 = (bf16[8,3072]{1,0:T(8,128)(2,1)S(1)}, bf16[8,3072]{1,0:T(8,128)(2,1)S(1)}, u32[]{:S(2)}, u32[]{:S(2)}) collective-permute-start(bf16[8,3072]{1,0:T(8,128)(2,1)S(1)} %get-tuple-element.25), channel_id=1, source_target_pairs={{0,4},{1,5},{2,6},{3,7},{4,0},{5,1},{6,2},{7,3},{8,12},{9,13},{10,... | collective-permute-start | bytes 147464 | tf_op jit(solution)/shard_map/ppermute | solution.py:404
  36.6 3.7 %collective-permute-start = (f32[32,8]{1,0:T(8,128)S(1)}, f32[32,8]{1,0:T(8,128)S(1)}, u32[]{:S(2)}, u32[]{:S(2)}) collective-permute-start(f32[32,8]{1,0:T(8,128)S(1)} %weigh.1.refs_4_.table_ref), channel_id=1, source_target_pairs={{0,2},{1,3},{2,0},{3,1},{4,6},{5,7},{6,4},{7,5},{8,10},{9,11},{10,... | collective-permute-start | bytes 3080 | tf_op jit(solution)/shard_map/ppermute | solution.py:404
  41.3 4.3 %collective-permute-start.11 = (bf16[8,3072]{1,0:T(8,128)(2,1)S(1)}, bf16[8,3072]{1,0:T(8,128)(2,1)S(1)}, u32[]{:S(2)}, u32[]{:S(2)}) collective-permute-start(bf16[8,3072]{1,0:T(8,128)(2,1)S(1)} %get-tuple-element.29._), channel_id=1, source_target_pairs={{0,2},{1,3},{2,0},{3,1},{4,6},{5,7},{6,4},{7,5},{8,10},{9,11},{10,... | collective-permute-start | bytes 147464 | tf_op jit(solution)/shard_map/ppermute | solution.py:404
